TPU v7x, 128 devices: a whole 4x4x4 slice. The times are simulated.
128 devices in a mesh: tile: 32 (over z, y_lo, x), comp: 4 (over y_hi, core).
Axes of the slice: x: 4, y: 4 (y_hi: 2, y_lo: 2; y = y_hi * 2 + y_lo), z: 4, core: 2. Of those that a mesh axis runs over, the one named last changes fastest.
Arguments:
- atm_state: float32 [4, 16, 1024, 512], P(None, None, 'tile', 'comp'), may hold values from -6 to 6
- level_winds: float32 [2, 16], replicated, may hold values from -1 to 1
- physics_flags: int32 [1024, 512], P('tile', 'comp'), may hold values from 0 to 2
- flux_matrix: float32 [12, 4], replicated, may hold values from -3 to 3
- regrid_source: int32 [1024, 8], P(('tile', 'comp')), may hold values from 0 to 4095, as said below
- regrid_weights: bfloat16 [1024, 8, 128, 128], P(('tile', 'comp')), may hold values from -0.1875 to 0.1875
- return_weights: bfloat16 [1024, 8, 128, 128], P(('tile', 'comp')), may hold values from -0.375 to 0.375
- ocean_state: float32 [4, 16, 131072], P(None, None, ('tile', 'comp')), may hold values from -6 to 6
- ocean_neighbors: int32 [6, 131072], P(None, ('tile', 'comp')), may hold values from 0 to 256, as said below
- edge_weights: float32 [6, 131072], P(None, ('tile', 'comp')), may hold values from 0.02 to 0.14
- ocean_coupling: float32 [4, 12], replicated, may hold values from -1.75 to 1.75
Outputs:
- atm_final: float32 [4, 16, 1024, 512], P(None, None, 'tile', 'comp')
- ocean_final: float32 [4, 16, 131072], P(None, None, ('tile', 'comp'))
- ocean_on_atm: float32 [4, 1024, 512], P(None, 'tile', 'comp')
Inputs may be any that keep to these rules, and one draw needn't show every extreme that they name: `regrid_source`: every entry of row b names a surface block in the comp column of row b's owner: entry % (devices along comp) equals (b // 8) % (devices along comp). The rows of one ocean device name blocks of any one tile index (x // 32) at most 4 times, exactly 4 times for one of them. Entries may repeat. `ocean_neighbors`: an entry minus 128 is the signed distance of the neighbour from its own cell in the cyclic order of the 131072 cells; distances of exactly 128 and -128 both occur.
All inputs are finite; a program needn't handle non-finite values.
Results may differ from a plain program's by a relative error of at most 0.0039.
Values may be sent and summed in bfloat16 or wider, within the bound.
No kernel may reach another device: no remote copies, remote signals or barrier semaphores. Data moves between devices by JAX's collectives and lax.ppermute only.
A program may use at most 128 MiB of HBM per device.

v0:
```python
import jax
import jax.numpy as jnp
import numpy as np
from jax import lax
from jax.sharding import PartitionSpec as P

ATM_STEPS = 4
OCEAN_STEPS = 2
HALO = 128


TIME_STEP = 0.02
RELAX_RATE = 5.0
MIXING_RATE = 5.0
OCEAN_MIXING = 0.2
OCEAN_ROTATION = 0.2
FORCING_SCALE = 0.25
SATURATION = 0.5


def padded_2(x, sides, width):
    for axis, dim in sides:
        count, length = (lax.axis_size(axis), x.shape[dim])
        up = [(i, (i + 1) % count) for i in range(count)]
        down = [(j, i) for i, j in up]
        last = lax.slice_in_dim(x, length - width, length, axis=dim)
        initial = lax.slice_in_dim(x, 0, width, axis=dim)
        before = lax.ppermute(last, axis, up)
        after = lax.ppermute(initial, axis, down)
        x = jnp.concatenate([before, x, after], axis=dim)
    return x


def gll_derivative():
    points = np.array([-1.0, -1.0 / np.sqrt(5.0), 1.0 / np.sqrt(5.0), 1.0])
    products = np.array(
        [np.prod([points[r] - points[s] for s in range(4) if s != r]) for r in range(4)]
    )
    deriv_table = np.zeros((4, 4))
    for r in range(4):
        for s in range(4):
            if r != s:
                deriv_table[r, s] = products[r] / (products[s] * (points[r] - points[s]))
        deriv_table[r, r] = sum((1.0 / (points[r] - points[s]) for s in range(4) if s != r))
    return 2.0 * deriv_table


def derivative_x(atm_field):
    n_fields, n_levels, x_nodes, y_nodes = atm_field.shape
    shaped = atm_field.reshape(n_fields, n_levels, x_nodes // 4, 4, y_nodes)
    deriv_table = jnp.asarray(gll_derivative(), jnp.float32)
    result = jnp.einsum("ij,flejy->fleiy", deriv_table, shaped, precision=lax.Precision.HIGHEST)
    return result.reshape(atm_field.shape)


def derivative_y(atm_field):
    n_fields, n_levels, x_nodes, y_nodes = atm_field.shape
    shaped = atm_field.reshape(n_fields, n_levels, x_nodes, y_nodes // 4, 4)
    deriv_table = jnp.asarray(gll_derivative(), jnp.float32)
    result = jnp.einsum("ij,flxej->flxei", deriv_table, shaped, precision=lax.Precision.HIGHEST)
    return result.reshape(atm_field.shape)


def vertical_mix(column_field):
    above = jnp.concatenate([column_field[:, 1:], column_field[:, -1:]], axis=1)
    below = jnp.concatenate([column_field[:, :1], column_field[:, :-1]], axis=1)
    return above - 2.0 * column_field + below


def advance(atm_field, level_winds, physics_flags, coriolis):
    slope_x = derivative_x(atm_field)
    slope_y = derivative_y(atm_field)
    wind_x = level_winds[0][None, :, None, None]
    wind_y = level_winds[1][None, :, None, None]
    advection = -(wind_x * slope_x + wind_y * slope_y)
    u_tend = advection[0] - slope_x[3] + coriolis * atm_field[1]
    v_tend = advection[1] - slope_y[3] - coriolis * atm_field[0]
    col_mean = jnp.mean(atm_field[2], axis=0, keepdims=True)
    t_tend = advection[2] + jnp.where(
        physics_flags == 1, RELAX_RATE * (col_mean - atm_field[2]), 0.0
    )
    h_tend = advection[3] - (slope_x[0] + slope_y[1])
    tendency = jnp.stack([u_tend, v_tend, t_tend, h_tend])
    tendency = tendency + jnp.where(physics_flags == 2, MIXING_RATE * vertical_mix(atm_field), 0.0)
    return atm_field + TIME_STEP * tendency


def average_x(padded):
    inner_count = padded.shape[2] - 2
    middle = padded[:, :, 1:-1]
    left_side = padded[:, :, :-2]
    right_side = padded[:, :, 2:]
    position = (jnp.arange(inner_count) % 4)[:, None]
    return jnp.where(
        position == 0,
        0.5 * (middle + left_side),
        jnp.where(position == 3, 0.5 * (middle + right_side), middle),
    )


def average_y(padded):
    inner_count = padded.shape[3] - 2
    middle = padded[:, :, :, 1:-1]
    left_side = padded[:, :, :, :-2]
    right_side = padded[:, :, :, 2:]
    position = jnp.arange(inner_count) % 4
    return jnp.where(
        position == 0,
        0.5 * (middle + left_side),
        jnp.where(position == 3, 0.5 * (middle + right_side), middle),
    )


def surface_flux(atm_field, flux_matrix):
    bottom = atm_field[:, 0]
    wind_speed = jnp.sqrt(bottom[0] * bottom[0] + bottom[1] * bottom[1] + 1.0)
    mixed_flux = jnp.einsum("cf,fxy->xcy", flux_matrix, bottom, precision=lax.Precision.HIGHEST)
    return (
        mixed_flux * wind_speed[:, None, :] / jnp.sqrt(1.0 + SATURATION * mixed_flux * mixed_flux)
    )


def ocean_update(ocean, neighbor_values, edge_weights, forcing, ocean_coupling):
    lateral = jnp.sum(edge_weights[None, None] * (neighbor_values - ocean[:, :, None, :]), axis=2)
    zero_part = jnp.zeros_like(ocean[0])
    rotation = jnp.stack(
        [zero_part, zero_part, OCEAN_ROTATION * ocean[3], -OCEAN_ROTATION * ocean[2]]
    )
    top_term = FORCING_SCALE * jnp.einsum(
        "gc,cn->gn", ocean_coupling, forcing, precision=lax.Precision.HIGHEST
    )
    updated = ocean + lateral + OCEAN_MIXING * vertical_mix(ocean) + rotation
    return updated.at[:, 0].add(top_term)


def per_device(
    atm_state,
    level_winds,
    physics_flags,
    flux_matrix,
    regrid_source,
    regrid_weights,
    return_weights,
    ocean_state,
    ocean_neighbors,
    edge_weights,
    ocean_coupling,
):
    n_tiles = lax.axis_size("tile")
    n_comps = lax.axis_size("comp")
    n_fields, n_levels, x_nodes, y_nodes = atm_state.shape
    ocean_blocks, per_block = regrid_source.shape
    n_flux = flux_matrix.shape[0]
    n_requests = ocean_blocks * per_block
    capacity = 2 * n_requests // n_tiles
    source_rows = regrid_source.reshape(n_requests) // n_comps
    source_tile = source_rows // x_nodes
    source_row = source_rows % x_nodes
    tile_hit = (source_tile[:, None] == jnp.arange(n_tiles, dtype=jnp.int32)[None, :]).astype(
        jnp.int32
    )
    slot_rank = jnp.sum((jnp.cumsum(tile_hit, axis=0) - tile_hit) * tile_hit, axis=1)
    slot_index = source_tile * capacity + slot_rank
    wanted = jnp.full((n_tiles * capacity,), -1, jnp.int32).at[slot_index].set(source_row)
    served = lax.all_to_all(
        wanted.reshape(n_tiles, capacity), "tile", split_axis=0, concat_axis=0, tiled=True
    ).reshape(n_tiles * capacity)
    pick_rows = jnp.clip(served, 0, x_nodes - 1)
    y_global = (lax.axis_index("comp") * y_nodes + jnp.arange(y_nodes)).astype(jnp.float32)
    coriolis = 0.5 * jnp.sin(2.0 * jnp.pi * (y_global + 0.5) / (y_nodes * n_comps))
    atm_field = atm_state
    flux_total = jnp.zeros((x_nodes, n_flux, y_nodes), jnp.float32)
    for step_index in range(ATM_STEPS):
        atm_field = advance(atm_field, level_winds, physics_flags, coriolis)
        padded = padded_2(atm_field, (("tile", 2),), 1)
        halfway = average_x(padded)
        padded = padded_2(halfway, (("comp", 3),), 1)
        atm_field = average_y(padded)
        flux_total = flux_total + surface_flux(atm_field, flux_matrix)
    sent_rows = (
        (flux_total[pick_rows] / ATM_STEPS)
        .astype(jnp.bfloat16)
        .reshape(n_tiles, capacity, n_flux, y_nodes)
    )
    mean_rows = lax.all_to_all(sent_rows, "tile", split_axis=0, concat_axis=0, tiled=True).reshape(
        n_tiles * capacity, n_flux, y_nodes
    )
    gathered = mean_rows[slot_index].reshape(ocean_blocks, per_block, n_flux, y_nodes)
    forcing = jnp.einsum(
        "bkfa,bkac->fbc", gathered, regrid_weights, preferred_element_type=jnp.float32
    )
    forcing = forcing.reshape(n_flux, ocean_blocks * y_nodes)
    cells = ocean_state.shape[2]
    local_index = jnp.arange(cells, dtype=jnp.int32)[None, :] + ocean_neighbors
    ocean = ocean_state
    for step_index in range(OCEAN_STEPS):
        padded = padded_2(ocean, ((("tile", "comp"), 2),), HALO)
        neighbor_values = jnp.take(padded, local_index, axis=2)
        ocean = ocean_update(ocean, neighbor_values, edge_weights, forcing, ocean_coupling)
    n_ofields = ocean.shape[0]
    surface = ocean[:, 0].astype(jnp.bfloat16).reshape(n_ofields, ocean_blocks, y_nodes)
    parts = jnp.einsum(
        "fbc,bkca->bkfa", surface, return_weights, preferred_element_type=jnp.float32
    )
    parts = parts.reshape(n_requests, n_ofields, y_nodes)
    outgoing = (
        jnp.zeros((n_tiles * capacity, n_ofields, y_nodes), jnp.float32).at[slot_index].set(parts)
    )
    incoming = lax.all_to_all(
        outgoing.reshape(n_tiles, capacity, n_ofields, y_nodes),
        "tile",
        split_axis=0,
        concat_axis=0,
        tiled=True,
    )
    incoming = incoming.reshape(n_tiles * capacity, n_ofields * y_nodes)
    owner = (served[None, :] == jnp.arange(x_nodes, dtype=jnp.int32)[:, None]).astype(jnp.float32)
    summed = jnp.dot(owner, incoming, precision=lax.Precision.HIGHEST)
    ocean_on_atm = summed.reshape(x_nodes, n_ofields, y_nodes).transpose(1, 0, 2)
    return (atm_field, ocean, ocean_on_atm)


def solution(mesh):
    return jax.shard_map(
        per_device,
        mesh=mesh,
        in_specs=(
            P(None, None, "tile", "comp"),
            P(),
            P("tile", "comp"),
            P(),
            P(("tile", "comp"), None),
            P(("tile", "comp"), None, None, None),
            P(("tile", "comp"), None, None, None),
            P(None, None, ("tile", "comp")),
            P(None, ("tile", "comp")),
            P(None, ("tile", "comp")),
            P(),
        ),
        out_specs=(
            P(None, None, "tile", "comp"),
            P(None, None, ("tile", "comp")),
            P(None, "tile", "comp"),
        ),
        check_vma=False,
    )
```

profile of v0, /device:TPU:17, one launch (start us, length us, event | category | flops | bytes accessed | tf_op | source)
XLA Modules:
  0.0 520.6 jit_solution(8938223284893922427)
XLA Ops:
  0.6 4.0 copy.522
  4.7 5.8 %copy.523 = f32[4,16,32,32,4]{3,4,2,1,0:T(4,128)} copy(f32[4,16,32,32,4]{2,1,4,3,0:T(8,128)} %bitcast.177) | data formatting | bytes 2097152 | tf_op jit(solution)/shard_map/reshape | solution.py:58
  10.5 10.6 %convolution_bitcast_fusion = f32[4,16,32,32,4]{3,4,2,1,0:T(4,128)} fusion(f32[4,4,1,1,1]{1,0,4,3,2:T(4,128)S(1)} %copy-done.45, f32[4,16,32,32,4]{3,4,2,1,0:T(4,128)} %copy.523), kind=kOutput, calls=%fused_computation.6 | convolution fusion | flops 12582912 | bytes 2097216 | tf_op jit(solution)/shard_map/ij,flxej->flxei/dot_general | solution.py:60
  21.1 6.2 %copy.524 = f32[4,16,32,32,4]{2,1,4,3,0:T(8,128)} copy(f32[4,16,32,32,4]{3,4,2,1,0:T(4,128)} %convolution_bitcast_fusion) | data formatting | bytes 2097152 | tf_op jit(solution)/shard_map/ij,flxej->flxei/dot_general | solution.py:60
  27.3 3.2 fusion.142
  32.1 4.0 copy.525
  36.1 2.8 fusion.165
  39.6 3.0 copy.526
  44.8 3.0 copy.528
  57.1 5.5 %collective-permute-start.1 = (f32[4,16,1,128]{3,2,1,0:T(1,128)S(1)}, f32[4,16,1,128]{3,2,1,0:T(1,128)S(1)}, u32[]{:S(2)}, u32[]{:S(2)}) collective-permute-start(f32[4,16,1,128]{3,2,1,0:T(1,128)S(1)} %get-tuple-element.108), channel_id=1, source_target_pairs={{4,0},{8,4},{12,8},{16,12},{20,16},{24,20},{28,24},{32,28},{36,32}... | collective-permute-start | bytes 98312 | tf_op jit(solution)/shard_map/ppermute | solution.py:29
  64.7 3.8 all-to-all-start
  69.2 2.5 collective-permute-start.16
  79.5 2.6 fusion.50
  86.1 6.0 %collective-permute-start.2 = (f32[4,16,32,1]{2,1,3,0:T(8,128)S(1)}, f32[4,16,32,1]{2,1,3,0:T(8,128)S(1)}, u32[]{:S(2)}, u32[]{:S(2)}) collective-permute-start(f32[4,16,32,1]{2,1,3,0:T(8,128)S(1)} %copy.530), channel_id=1, source_target_pairs={{0,1},{1,2},{2,3},{3,0},{4,5},{5,6},{6,7},{7,4},{8,9},{9,10},{10,1... | collective-permute-start | bytes 24584 | tf_op jit(solution)/shard_map/ppermute | solution.py:28
  95.6 46.8 %gather_fusion.2 = f32[6144,4,16]{2,1,0:T(4,128)} fusion(f32[4,16,1280]{1,0,2:T(4,128)} %copy.570, s32[6144]{0:T(1024)S(1)} %broadcast_clamp_fusion), kind=kCustom, calls=%fused_computation.clone | custom fusion | bytes 3170304 | tf_op jit(solution)/shard_map/jit(_take)/gather | solution.py:198
  142.4 10.0 %copy.591 = f32[6,1024,4,16]{1,0,3,2:T(8,128)} copy(f32[6,1024,4,16]{3,2,1,0:T(4,128)} %bitcast.172) | data formatting | bytes 3145728 | tf_op jit(solution)/shard_map/jit(_take)/gather | solution.py:198
  155.2 3.6 fusion.44
  158.8 2.9 copy.534
  161.7 5.8 %copy.535 = f32[4,16,32,32,4]{3,4,2,1,0:T(4,128)} copy(f32[4,16,32,32,4]{2,1,4,3,0:T(8,128)} %bitcast.178) | data formatting | bytes 2097152 | tf_op jit(solution)/shard_map/reshape | solution.py:58
  167.6 10.4 %fusion.167 = f32[4,16,32,32,4]{3,4,2,1,0:T(4,128)} fusion(f32[4,16,32,32,4]{3,4,2,1,0:T(4,128)} %copy.535, f32[4,4,1,1,1]{1,0,4,3,2:T(4,128)S(1)} %copy-done.45), kind=kOutput, calls=%fused_computation.310 | convolution fusion | flops 12582912 | bytes 2097216 | tf_op jit(solution)/shard_map/ij,flxej->flxei/dot_general | solution.py:60
  177.9 6.2 %copy.536 = f32[4,16,32,32,4]{2,1,4,3,0:T(8,128)} copy(f32[4,16,32,32,4]{3,4,2,1,0:T(4,128)} %fusion.167) | data formatting | bytes 2097152 | tf_op jit(solution)/shard_map/ij,flxej->flxei/dot_general | solution.py:60
  184.1 3.1 fusion.141
  189.5 4.2 copy.537
  193.7 2.9 fusion.166
  196.6 3.0 copy.538
  201.9 3.0 copy.540
  213.2 5.7 %collective-permute-start.5 = (f32[4,16,1,128]{3,2,1,0:T(1,128)S(1)}, f32[4,16,1,128]{3,2,1,0:T(1,128)S(1)}, u32[]{:S(2)}, u32[]{:S(2)}) collective-permute-start(f32[4,16,1,128]{3,2,1,0:T(1,128)S(1)} %get-tuple-element.99), channel_id=1, source_target_pairs={{4,0},{8,4},{12,8},{16,12},{20,16},{24,20},{28,24},{32,28},{36,32}... | collective-permute-start | bytes 98312 | tf_op jit(solution)/shard_map/ppermute | solution.py:29
  224.9 4.4 collective-permute-start.6
  233.1 2.9 collective-permute-done.7
  238.2 3.6 fusion.32
  241.8 3.1 copy.546
  244.9 5.8 %copy.547 = f32[4,16,32,32,4]{3,4,2,1,0:T(4,128)} copy(f32[4,16,32,32,4]{2,1,4,3,0:T(8,128)} %bitcast.179) | data formatting | bytes 2097152 | tf_op jit(solution)/shard_map/reshape | solution.py:58
  250.7 10.4 %fusion.169 = f32[4,16,32,32,4]{3,4,2,1,0:T(4,128)} fusion(f32[4,16,32,32,4]{3,4,2,1,0:T(4,128)} %copy.547, f32[4,4,1,1,1]{1,0,4,3,2:T(4,128)S(1)} %copy-done.45), kind=kOutput, calls=%fused_computation.312 | convolution fusion | flops 12582912 | bytes 2097216 | tf_op jit(solution)/shard_map/ij,flxej->flxei/dot_general | solution.py:60
  261.1 6.2 %copy.548 = f32[4,16,32,32,4]{2,1,4,3,0:T(8,128)} copy(f32[4,16,32,32,4]{3,4,2,1,0:T(4,128)} %fusion.169) | data formatting | bytes 2097152 | tf_op jit(solution)/shard_map/ij,flxej->flxei/dot_general | solution.py:60
  267.2 3.1 fusion.140
  272.6 4.0 copy.549
  276.6 2.9 fusion.168
  279.5 3.0 copy.550
  284.8 3.0 copy.552
  296.1 6.6 %collective-permute-start.9 = (f32[4,16,1,128]{3,2,1,0:T(1,128)S(1)}, f32[4,16,1,128]{3,2,1,0:T(1,128)S(1)}, u32[]{:S(2)}, u32[]{:S(2)}) collective-permute-start(f32[4,16,1,128]{3,2,1,0:T(1,128)S(1)} %get-tuple-element.90), channel_id=1, source_target_pairs={{4,0},{8,4},{12,8},{16,12},{20,16},{24,20},{28,24},{32,28},{36,32}... | collective-permute-start | bytes 98312 | tf_op jit(solution)/shard_map/ppermute | solution.py:29
  313.2 2.9 collective-permute-done.11
  318.2 3.6 fusion.20
  321.8 3.2 copy.558
  325.0 5.8 %copy.559 = f32[4,16,32,32,4]{3,4,2,1,0:T(4,128)} copy(f32[4,16,32,32,4]{2,1,4,3,0:T(8,128)} %bitcast.180) | data formatting | bytes 2097152 | tf_op jit(solution)/shard_map/reshape | solution.py:58
  330.8 10.4 %fusion.171 = f32[4,16,32,32,4]{3,4,2,1,0:T(4,128)} fusion(f32[4,16,32,32,4]{3,4,2,1,0:T(4,128)} %copy.559, f32[4,4,1,1,1]{1,0,4,3,2:T(4,128)S(1)} %copy-done.45), kind=kOutput, calls=%fused_computation.314 | convolution fusion | flops 12582912 | bytes 2097216 | tf_op jit(solution)/shard_map/ij,flxej->flxei/dot_general | solution.py:60
  341.2 6.2 %copy.560 = f32[4,16,32,32,4]{2,1,4,3,0:T(8,128)} copy(f32[4,16,32,32,4]{3,4,2,1,0:T(4,128)} %fusion.171) | data formatting | bytes 2097152 | tf_op jit(solution)/shard_map/ij,flxej->flxei/dot_general | solution.py:60
  347.4 3.1 fusion.139
  352.7 4.3 copy.561
  357.0 2.9 fusion.170
  359.8 3.0 copy.562
  365.1 3.0 copy.564
  376.5 6.7 %collective-permute-start.13 = (f32[4,16,1,128]{3,2,1,0:T(1,128)S(1)}, f32[4,16,1,128]{3,2,1,0:T(1,128)S(1)}, u32[]{:S(2)}, u32[]{:S(2)}) collective-permute-start(f32[4,16,1,128]{3,2,1,0:T(1,128)S(1)} %get-tuple-element.81), channel_id=1, source_target_pairs={{4,0},{8,4},{12,8},{16,12},{20,16},{24,20},{28,24},{32,28},{36,32}... | collective-permute-start | bytes 98312 | tf_op jit(solution)/shard_map/ppermute | solution.py:29
  392.6 3.9 collective-permute-done.15
  398.7 3.4 fusion.8
  407.2 8.5 %all-to-all-start.1 = ((bf16[32,4,12,128]{3,1,2,0:T(4,128)(2,1)}), bf16[32,4,12,128]{3,1,2,0:T(4,128)(2,1)S(1)}, u32[]{:S(2)}, u32[]{:S(2)}) async-start(bf16[32,4,12,128]{3,1,2,0:T(4,128)(2,1)} %copy.577), calls=%async_computation.1 | async-start | bytes 786432 | tf_op jit(solution)/shard_map/all_to_all | solution.py:185
  415.7 2.5 fusion.3
  419.4 4.9 all-to-all-done.1
  430.3 4.5 collective-permute-done.19
  436.7 46.8 %gather_fusion.3 = f32[6144,4,16]{2,1,0:T(4,128)} fusion(f32[4,16,1280]{1,0,2:T(4,128)} %copy.581, s32[6144]{0:T(1024)S(1)} %broadcast_clamp_fusion), kind=kCustom, calls=%fused_computation.1.clone | custom fusion | bytes 3170304 | tf_op jit(solution)/shard_map/jit(_take)/gather | solution.py:198
  483.5 10.0 %copy.592 = f32[6,1024,4,16]{1,0,3,2:T(8,128)} copy(f32[6,1024,4,16]{3,2,1,0:T(4,128)} %bitcast.171) | data formatting | bytes 3145728 | tf_op jit(solution)/shard_map/jit(_take)/gather | solution.py:198
  493.5 2.5 fusion.1
  498.1 2.6 scatter_fusion
  501.4 9.8 %all-to-all-start.2 = ((f32[32,4,4,128]{3,1,2,0:T(4,128)}), f32[32,4,4,128]{3,1,2,0:T(4,128)S(1)}, u32[]{:S(2)}, u32[]{:S(2)}) async-start(f32[32,4,4,128]{3,1,2,0:T(4,128)} %copy.585), calls=%async_computation.2 | async-start | bytes 524288 | tf_op jit(solution)/shard_map/all_to_all | solution.py:209
  512.2 7.1 %all-to-all-done.2 = f32[32,4,4,128]{3,1,2,0:T(4,128)S(1)} async-done(((f32[32,4,4,128]{3,1,2,0:T(4,128)}), f32[32,4,4,128]{3,1,2,0:T(4,128)S(1)}, u32[]{:S(2)}, u32[]{:S(2)}) %all-to-all-start.2) | async-done | bytes 262176 | tf_op jit(solution)/shard_map/all_to_all | solution.py:209
  (321 shorter events, 127.8 us)
Async XLA Ops:
  0.6 497.0 %copy-start = (bf16[8,8,128,128]{3,2,1,0:T(8,128)(2,1)S(1)}, bf16[8,8,128,128]{3,2,1,0:T(8,128)(2,1)}, u32[]{:S(2)}) copy-start(bf16[8,8,128,128]{3,2,1,0:T(8,128)(2,1)} %param.31) | copy-start | bytes 6291460
  4.7 5.8 %copy-start.45 = (f32[4,4,1,1,1]{1,0,4,3,2:T(4,128)S(1)}, f32[4,4,1,1,1]{1,0,4,3,2:T(4,128)}, u32[]{:S(2)}) copy-start(f32[4,4,1,1,1]{1,0,4,3,2:T(4,128)} %constant.203) | copy-start | bytes 196
  32.1 6.8 %copy-start.59 = (s32[32,128]{1,0:T(8,128)S(1)}, s32[32,128]{1,0:T(8,128)}, u32[]{:S(2)}) copy-start(s32[32,128]{1,0:T(8,128)} %param.27) | copy-start | bytes 49156
  32.1 19.2 %copy-start.61 = (f32[16]{0:T(128)}, f32[16]{0:T(128)S(1)}, u32[]{:S(2)}) copy-start(f32[16]{0:T(128)S(1)} %get-tuple-element.132) | copy-start | bytes 196
  32.1 19.2 %copy-start.62 = (f32[16]{0:T(128)}, f32[16]{0:T(128)S(1)}, u32[]{:S(2)}) copy-start(f32[16]{0:T(128)S(1)} %get-tuple-element.133) | copy-start | bytes 196
  53.1 9.5 %copy-start.60 = (s32[8,8]{1,0:T(8,128)S(1)}, s32[8,8]{1,0:T(8,128)}, u32[]{:S(2)}) copy-start(s32[8,8]{1,0:T(8,128)} %param.29) | copy-start | bytes 772
  53.1 15.4 %copy-start.15 = (f32[4,16,1024]{2,1,0:T(8,128)S(1)}, f32[4,16,1024]{2,1,0:T(8,128)}, u32[]{:S(2)}) copy-start(f32[4,16,1024]{2,1,0:T(8,128)} %param.32) | copy-start | bytes 786436
  55.8 23.7 %collective-permute-start = (f32[4,16,1,128]{3,2,1,0:T(1,128)S(1)}, f32[4,16,1,128]{3,2,1,0:T(1,128)S(1)}, u32[]{:S(2)}, u32[]{:S(2)}) collective-permute-start(f32[4,16,1,128]{3,2,1,0:T(1,128)S(1)} %get-tuple-element.107), channel_id=1, source_target_pairs={{0,4},{4,8},{8,12},{12,16},{16,20},{20,24},{24,28},{28,32},{32,36}... | collective-permute-start | bytes 98312 | tf_op jit(solution)/shard_map/ppermute | solution.py:28
  57.1 22.4 %collective-permute-start.1 = (f32[4,16,1,128]{3,2,1,0:T(1,128)S(1)}, f32[4,16,1,128]{3,2,1,0:T(1,128)S(1)}, u32[]{:S(2)}, u32[]{:S(2)}) collective-permute-start(f32[4,16,1,128]{3,2,1,0:T(1,128)S(1)} %get-tuple-element.108), channel_id=1, source_target_pairs={{4,0},{8,4},{12,8},{16,12},{20,16},{24,20},{28,24},{32,28},{36,32}... | collective-permute-start | bytes 98312 | tf_op jit(solution)/shard_map/ppermute | solution.py:29
  63.2 22.9 %copy-start.72 = (s32[64]{0:T(128)}, s32[64]{0:T(128)S(1)}, u32[]{:S(2)}) copy-start(s32[64]{0:T(128)S(1)} %fusion.134) | copy-start | bytes 772
  64.7 12.2 %all-to-all-start = ((s32[32,1,4]{2,1,0:T(1,128)}), s32[32,1,4]{2,1,0:T(1,128)S(1)}, u32[]{:S(2)}, u32[]{:S(2)}) async-start(s32[32,1,4]{2,1,0:T(1,128)} %bitcast.59), calls=%async_computation | async-start | bytes 32768 | tf_op jit(solution)/shard_map/all_to_all | solution.py:165
  69.2 23.5 %collective-permute-start.16 = (f32[4,16,128]{2,1,0:T(8,128)}, f32[4,16,128]{2,1,0:T(8,128)}, u32[]{:S(2)}, u32[]{:S(2)}) collective-permute-start(f32[4,16,128]{2,1,0:T(8,128)} %get-tuple-element.122), channel_id=1, source_target_pairs={{0,1},{1,2},{2,3},{3,4},{4,5},{5,6},{6,7},{7,8},{8,9},{9,10},{10,1... | collective-permute-start | bytes 98312 | tf_op jit(solution)/shard_map/ppermute | solution.py:28
  71.6 21.0 %collective-permute-start.17 = (f32[4,16,128]{2,1,0:T(8,128)}, f32[4,16,128]{2,1,0:T(8,128)}, u32[]{:S(2)}, u32[]{:S(2)}) collective-permute-start(f32[4,16,128]{2,1,0:T(8,128)} %get-tuple-element.123), channel_id=1, source_target_pairs={{1,0},{2,1},{3,2},{4,3},{5,4},{6,5},{7,6},{8,7},{9,8},{10,9},{11,1... | collective-permute-start | bytes 98312 | tf_op jit(solution)/shard_map/ppermute | solution.py:29
  71.6 14.5 %copy-start.63 = (pred[32]{0:T(512)(128)(4,1)}, pred[32]{0:T(512)(128)(4,1)S(1)}, u32[]{:S(2)}) copy-start(pred[32]{0:T(512)(128)(4,1)S(1)} %get-tuple-element.134) | copy-start | bytes 100
  71.6 14.5 %copy-start.67 = (pred[32]{0:T(512)(128)(4,1)}, pred[32]{0:T(512)(128)(4,1)S(1)}, u32[]{:S(2)}) copy-start(pred[32]{0:T(512)(128)(4,1)S(1)} %get-tuple-element.135) | copy-start | bytes 100
  73.8 341.9 %copy-start.46 = (pred[6,1024]{1,0:T(8,128)(4,1)}, pred[6,1024]{1,0:T(8,128)(4,1)S(1)}, u32[]{:S(2)}) copy-start(pred[6,1024]{1,0:T(8,128)(4,1)S(1)} %compare_and_fusion) | copy-start | bytes 18436
  86.1 66.2 %collective-permute-start.2 = (f32[4,16,32,1]{2,1,3,0:T(8,128)S(1)}, f32[4,16,32,1]{2,1,3,0:T(8,128)S(1)}, u32[]{:S(2)}, u32[]{:S(2)}) collective-permute-start(f32[4,16,32,1]{2,1,3,0:T(8,128)S(1)} %copy.530), channel_id=1, source_target_pairs={{0,1},{1,2},{2,3},{3,0},{4,5},{5,6},{6,7},{7,4},{8,9},{9,10},{10,1... | collective-permute-start | bytes 24584 | tf_op jit(solution)/shard_map/ppermute | solution.py:28
  92.6 61.2 %collective-permute-start.3 = (f32[4,16,32,1]{2,1,3,0:T(8,128)S(1)}, f32[4,16,32,1]{2,1,3,0:T(8,128)S(1)}, u32[]{:S(2)}, u32[]{:S(2)}) collective-permute-start(f32[4,16,32,1]{2,1,3,0:T(8,128)S(1)} %copy.532), channel_id=1, source_target_pairs={{1,0},{2,1},{3,2},{0,3},{5,4},{6,5},{7,6},{4,7},{9,8},{10,9},{11,1... | collective-permute-start | bytes 24584 | tf_op jit(solution)/shard_map/ppermute | solution.py:29
  212.0 6.9 %copy-start.34 = (f32[4,32,128]{2,1,0:T(8,128)S(1)}, f32[4,32,128]{2,1,0:T(8,128)}, u32[]{:S(2)}) copy-start(f32[4,32,128]{2,1,0:T(8,128)} %get-tuple-element.75) | copy-start | bytes 196612
  212.0 6.9 %copy-start.53 = (f32[12,4]{0,1:T(4,128)S(1)}, f32[12,4]{0,1:T(4,128)}, u32[]{:S(2)}) copy-start(f32[12,4]{0,1:T(4,128)} %param.28) | copy-start | bytes 580
  212.0 8.2 %copy-start.64 = (pred[32]{0:T(512)(128)(4,1)S(1)}, pred[32]{0:T(512)(128)(4,1)}, u32[]{:S(2)}) copy-start(pred[32]{0:T(512)(128)(4,1)} %copy-done.63) | copy-start | bytes 100
  212.1 8.2 %copy-start.68 = (pred[32]{0:T(512)(128)(4,1)S(1)}, pred[32]{0:T(512)(128)(4,1)}, u32[]{:S(2)}) copy-start(pred[32]{0:T(512)(128)(4,1)} %copy-done.67) | copy-start | bytes 100
  213.1 7.1 %collective-permute-start.4 = (f32[4,16,1,128]{3,2,1,0:T(1,128)S(1)}, f32[4,16,1,128]{3,2,1,0:T(1,128)S(1)}, u32[]{:S(2)}, u32[]{:S(2)}) collective-permute-start(f32[4,16,1,128]{3,2,1,0:T(1,128)S(1)} %get-tuple-element.98), channel_id=1, source_target_pairs={{0,4},{4,8},{8,12},{12,16},{16,20},{20,24},{24,28},{28,32},{32,36}... | collective-permute-start | bytes 98312 | tf_op jit(solution)/shard_map/ppermute | solution.py:28
  213.2 7.0 %collective-permute-start.5 = (f32[4,16,1,128]{3,2,1,0:T(1,128)S(1)}, f32[4,16,1,128]{3,2,1,0:T(1,128)S(1)}, u32[]{:S(2)}, u32[]{:S(2)}) collective-permute-start(f32[4,16,1,128]{3,2,1,0:T(1,128)S(1)} %get-tuple-element.99), channel_id=1, source_target_pairs={{4,0},{8,4},{12,8},{16,12},{20,16},{24,20},{28,24},{32,28},{36,32}... | collective-permute-start | bytes 98312 | tf_op jit(solution)/shard_map/ppermute | solution.py:29
  224.9 6.7 %collective-permute-start.6 = (f32[4,16,32,1]{2,1,3,0:T(8,128)S(1)}, f32[4,16,32,1]{2,1,3,0:T(8,128)S(1)}, u32[]{:S(2)}, u32[]{:S(2)}) collective-permute-start(f32[4,16,32,1]{2,1,3,0:T(8,128)S(1)} %copy.542), channel_id=1, source_target_pairs={{0,1},{1,2},{2,3},{3,0},{4,5},{5,6},{6,7},{7,4},{8,9},{9,10},{10,1... | collective-permute-start | bytes 24584 | tf_op jit(solution)/shard_map/ppermute | solution.py:28
  231.0 5.0 collective-permute-start.7
  290.1 4.9 copy-start.22
  290.1 4.9 copy-start.32
  290.1 4.9 copy-start.51
  294.9 7.8 %copy-start.35 = (f32[4,32,128]{2,1,0:T(8,128)S(1)}, f32[4,32,128]{2,1,0:T(8,128)}, u32[]{:S(2)}) copy-start(f32[4,32,128]{2,1,0:T(8,128)} %get-tuple-element.72) | copy-start | bytes 196612
  294.9 7.8 %copy-start.54 = (f32[12,4]{0,1:T(4,128)S(1)}, f32[12,4]{0,1:T(4,128)}, u32[]{:S(2)}) copy-start(f32[12,4]{0,1:T(4,128)} %param.28) | copy-start | bytes 580
  295.0 9.0 %copy-start.65 = (pred[32]{0:T(512)(128)(4,1)S(1)}, pred[32]{0:T(512)(128)(4,1)}, u32[]{:S(2)}) copy-start(pred[32]{0:T(512)(128)(4,1)} %copy-done.63) | copy-start | bytes 100
  295.0 9.0 %copy-start.69 = (pred[32]{0:T(512)(128)(4,1)S(1)}, pred[32]{0:T(512)(128)(4,1)}, u32[]{:S(2)}) copy-start(pred[32]{0:T(512)(128)(4,1)} %copy-done.67) | copy-start | bytes 100
  296.1 7.9 %collective-permute-start.8 = (f32[4,16,1,128]{3,2,1,0:T(1,128)S(1)}, f32[4,16,1,128]{3,2,1,0:T(1,128)S(1)}, u32[]{:S(2)}, u32[]{:S(2)}) collective-permute-start(f32[4,16,1,128]{3,2,1,0:T(1,128)S(1)} %get-tuple-element.89), channel_id=1, source_target_pairs={{0,4},{4,8},{8,12},{12,16},{16,20},{20,24},{24,28},{28,32},{32,36}... | collective-permute-start | bytes 98312 | tf_op jit(solution)/shard_map/ppermute | solution.py:28
  296.1 7.9 %collective-permute-start.9 = (f32[4,16,1,128]{3,2,1,0:T(1,128)S(1)}, f32[4,16,1,128]{3,2,1,0:T(1,128)S(1)}, u32[]{:S(2)}, u32[]{:S(2)}) collective-permute-start(f32[4,16,1,128]{3,2,1,0:T(1,128)S(1)} %get-tuple-element.90), channel_id=1, source_target_pairs={{4,0},{8,4},{12,8},{16,12},{20,16},{24,20},{28,24},{32,28},{36,32}... | collective-permute-start | bytes 98312 | tf_op jit(solution)/shard_map/ppermute | solution.py:29
  308.7 3.0 collective-permute-start.10
  311.0 5.0 collective-permute-start.11
  370.4 4.9 copy-start.18
  370.4 4.9 copy-start.30
  370.4 4.9 copy-start.52
  375.3 7.9 %copy-start.33 = (f32[4,32,128]{2,1,0:T(8,128)S(1)}, f32[4,32,128]{2,1,0:T(8,128)}, u32[]{:S(2)}) copy-start(f32[4,32,128]{2,1,0:T(8,128)} %get-tuple-element.69) | copy-start | bytes 196612
  375.3 7.9 %copy-start.55 = (f32[12,4]{0,1:T(4,128)S(1)}, f32[12,4]{0,1:T(4,128)}, u32[]{:S(2)}) copy-start(f32[12,4]{0,1:T(4,128)} %param.28) | copy-start | bytes 580
  375.3 9.1 %copy-start.66 = (pred[32]{0:T(512)(128)(4,1)S(1)}, pred[32]{0:T(512)(128)(4,1)}, u32[]{:S(2)}) copy-start(pred[32]{0:T(512)(128)(4,1)} %copy-done.63) | copy-start | bytes 100
  375.3 9.1 %copy-start.70 = (pred[32]{0:T(512)(128)(4,1)S(1)}, pred[32]{0:T(512)(128)(4,1)}, u32[]{:S(2)}) copy-start(pred[32]{0:T(512)(128)(4,1)} %copy-done.67) | copy-start | bytes 100
  376.4 8.0 %collective-permute-start.12 = (f32[4,16,1,128]{3,2,1,0:T(1,128)S(1)}, f32[4,16,1,128]{3,2,1,0:T(1,128)S(1)}, u32[]{:S(2)}, u32[]{:S(2)}) collective-permute-start(f32[4,16,1,128]{3,2,1,0:T(1,128)S(1)} %get-tuple-element.80), channel_id=1, source_target_pairs={{0,4},{4,8},{8,12},{12,16},{16,20},{20,24},{24,28},{28,32},{32,36}... | collective-permute-start | bytes 98312 | tf_op jit(solution)/shard_map/ppermute | solution.py:28
  376.5 7.9 %collective-permute-start.13 = (f32[4,16,1,128]{3,2,1,0:T(1,128)S(1)}, f32[4,16,1,128]{3,2,1,0:T(1,128)S(1)}, u32[]{:S(2)}, u32[]{:S(2)}) collective-permute-start(f32[4,16,1,128]{3,2,1,0:T(1,128)S(1)} %get-tuple-element.81), channel_id=1, source_target_pairs={{4,0},{8,4},{12,8},{16,12},{20,16},{24,20},{28,24},{32,28},{36,32}... | collective-permute-start | bytes 98312 | tf_op jit(solution)/shard_map/ppermute | solution.py:29
  389.1 3.0 collective-permute-start.14
  391.5 5.0 collective-permute-start.15
  402.1 13.6 %copy-start.43 = (f32[6,1024]{1,0:T(8,128)S(1)}, f32[6,1024]{1,0:T(8,128)}, u32[]{:S(2)}) copy-start(f32[6,1024]{1,0:T(8,128)} %param.34) | copy-start | bytes 73732
  404.4 13.8 %copy-start.39 = (f32[1,16,1024]{2,1,0:T(8,128)S(1)}, f32[1,16,1024]{2,1,0:T(8,128)}, u32[]{:S(2)}) copy-start(f32[1,16,1024]{2,1,0:T(8,128)} %get-tuple-element.124) | copy-start | bytes 196612
  404.4 13.8 %copy-start.48 = (f32[4,1,1024]{2,1,0:T(1,128)S(1)}, f32[4,1,1024]{2,1,0:T(1,128)}, u32[]{:S(2)}) copy-start(f32[4,1,1024]{2,1,0:T(1,128)} %get-tuple-element.126) | copy-start | bytes 49156
  406.2 12.0 %copy-start.28 = (f32[4,15,1024]{2,1,0:T(8,128)S(1)}, f32[4,15,1024]{2,1,0:T(8,128)}, u32[]{:S(2)}) copy-start(f32[4,15,1024]{2,1,0:T(8,128)} %get-tuple-element.128) | copy-start | bytes 737284
  406.3 12.0 %copy-start.40 = (f32[1,16,1024]{2,1,0:T(8,128)S(1)}, f32[1,16,1024]{2,1,0:T(8,128)}, u32[]{:S(2)}) copy-start(f32[1,16,1024]{2,1,0:T(8,128)} %get-tuple-element.125) | copy-start | bytes 196612
  406.3 12.0 %copy-start.49 = (f32[4,1,1024]{2,1,0:T(1,128)S(1)}, f32[4,1,1024]{2,1,0:T(1,128)}, u32[]{:S(2)}) copy-start(f32[4,1,1024]{2,1,0:T(1,128)} %get-tuple-element.127) | copy-start | bytes 49156
  406.3 12.0 %copy-start.71 = (f32[4]{0:T(128)S(1)}, f32[4]{0:T(128)}, u32[]{:S(2)}) copy-start(f32[4]{0:T(128)} %pad.14.clone) | copy-start | bytes 52
  407.2 17.0 %all-to-all-start.1 = ((bf16[32,4,12,128]{3,1,2,0:T(4,128)(2,1)}), bf16[32,4,12,128]{3,1,2,0:T(4,128)(2,1)S(1)}, u32[]{:S(2)}, u32[]{:S(2)}) async-start(bf16[32,4,12,128]{3,1,2,0:T(4,128)(2,1)} %copy.577), calls=%async_computation.1 | async-start | bytes 786432 | tf_op jit(solution)/shard_map/all_to_all | solution.py:185
  418.2 9.3 %copy-start.73 = (f32[4,12]{1,0:T(4,128)S(1)}, f32[4,12]{1,0:T(4,128)}, u32[]{:S(2)}) copy-start(f32[4,12]{1,0:T(4,128)} %param.35) | copy-start | bytes 580
  427.9 2.3 collective-permute-start.18
  429.0 5.7 %collective-permute-start.19 = (f32[4,16,128]{2,1,0:T(8,128)S(1)}, f32[4,16,128]{2,1,0:T(8,128)S(1)}, u32[]{:S(2)}, u32[]{:S(2)}) collective-permute-start(f32[4,16,128]{2,1,0:T(8,128)S(1)} %get-tuple-element.117), channel_id=1, source_target_pairs={{1,0},{2,1},{3,2},{4,3},{5,4},{6,5},{7,6},{8,7},{9,8},{10,9},{11,1... | collective-permute-start | bytes 98312 | tf_op jit(solution)/shard_map/ppermute | solution.py:29
  483.5 10.0 %copy-start.44 = (f32[6,1024]{1,0:T(8,128)S(1)}, f32[6,1024]{1,0:T(8,128)}, u32[]{:S(2)}) copy-start(f32[6,1024]{1,0:T(8,128)} %param.34) | copy-start | bytes 73732
  483.5 10.0 %copy-start.47 = (pred[6,1024]{1,0:T(8,128)(4,1)S(1)}, pred[6,1024]{1,0:T(8,128)(4,1)}, u32[]{:S(2)}) copy-start(pred[6,1024]{1,0:T(8,128)(4,1)} %copy-done.46) | copy-start | bytes 18436
  483.5 12.5 %copy-start.41 = (f32[1,16,1024]{2,1,0:T(8,128)S(1)}, f32[1,16,1024]{2,1,0:T(8,128)}, u32[]{:S(2)}) copy-start(f32[1,16,1024]{2,1,0:T(8,128)} %get-tuple-element.119) | copy-start | bytes 196612
  501.4 17.9 %all-to-all-start.2 = ((f32[32,4,4,128]{3,1,2,0:T(4,128)}), f32[32,4,4,128]{3,1,2,0:T(4,128)S(1)}, u32[]{:S(2)}, u32[]{:S(2)}) async-start(f32[32,4,4,128]{3,1,2,0:T(4,128)} %copy.585), calls=%async_computation.2 | async-start | bytes 524288 | tf_op jit(solution)/shard_map/all_to_all | solution.py:209
  512.2 8.2 %copy-start.29 = (f32[4,16,1024]{2,1,0:T(8,128)}, f32[4,16,1024]{2,1,0:T(8,128)S(1)}, u32[]{:S(2)}) copy-start(f32[4,16,1024]{2,1,0:T(8,128)S(1)} %scatter-add.9) | copy-start | bytes 786436
  (34 other events, 130.9 us)
where the time goes:
time: 529 us; the launch traced here: 521 us
  local copies, waits for them, and re-layouts  315 us (60%)
  starting transfers between devices  63.6 us (12%)
  matrix products  61.2 us (12%)
  other arithmetic  52.4 us (10%)
  waiting for transfers between devices  26.5 us (5%)
    gather x4, local copies, waits for them, and re-layouts, per_device(): neighbor_values = jnp.take(padded, local_index, axis=2)  114 us
    dot_general x4, matrix products, derivative_y(): jnp.einsum('ij,flxej->flxei', deriv_table, shaped, precision=lax.Precisio...  41.7 us
    ppermute x10, starting transfers between devices, padded_2(): after = lax.ppermute(initial, axis, down)  24.8 us
    dot_general x4, local copies, waits for them, and re-layouts, derivative_y(): jnp.einsum('ij,flxej->flxei', deriv_table, shaped, precision=lax.Precisio...  24.7 us
    slice x8, local copies, waits for them, and re-layouts, advance(): v_tend = advection[1] - slope_y[3] - coriolis * atm_field[0]  24.4 us
    reshape x4, local copies, waits for them, and re-layouts, derivative_y(): shaped = atm_field.reshape(n_fields, n_levels, x_nodes, y_nodes // 4, 4)  23.3 us
    ppermute x10, starting transfers between devices, padded_2(): before = lax.ppermute(last, axis, up)  16.7 us
    reshape x4, local copies, waits for them, and re-layouts, derivative_y(): return result.reshape(atm_field.shape)  16.5 us
  transfers between devices with their start and end apart: 23, of which 9 were waited for; matrix products, arithmetic and copies ran while one was open for 18% of the time, Pallas kernels for 0%

commit v1 on v0

v1 whole, which is shorter than its diff:
```python
import functools

import jax
import jax.numpy as jnp
import ml_dtypes
import numpy as np
from jax import lax
from jax.experimental import pallas as pl
from jax.experimental.pallas import tpu as pltpu
from jax.sharding import PartitionSpec as P

F32 = jnp.float32
BF16 = jnp.bfloat16
I32 = jnp.int32
N_TILE, N_COMP = 32, 4
STEPS = 4
LEVELS = 16
NFLUX = 12
DT = 0.02
VMEM = pl.BlockSpec(memory_space=pltpu.VMEM)
SMEM = pl.BlockSpec(memory_space=pltpu.SMEM)
STATE_PLANES = 64
X_PLANES = 74
Y_PLANES = 12


def gll_derivative():
    points = np.array([-1.0, -1.0 / np.sqrt(5.0), 1.0 / np.sqrt(5.0), 1.0])
    products = np.array(
        [np.prod([points[r] - points[s] for s in range(4) if s != r]) for r in range(4)]
    )
    table = np.zeros((4, 4))
    for r in range(4):
        for s in range(4):
            if r != s:
                table[r, s] = products[r] / (products[s] * (points[r] - points[s]))
    table[0, 0], table[3, 3] = -3.0, 3.0
    return 2.0 * table


DERIV = gll_derivative()
ROW_SCALE = np.array([1.375, 1.125, 1.125, 1.375])


def lane_matrices():
    scaled = (DERIV * ROW_SCALE[:, None]).astype(ml_dtypes.bfloat16).astype(np.float64)
    deriv = np.kron(np.eye(32), scaled)
    average = np.eye(128)
    for e in range(31):
        left, right = 4 * e + 3, 4 * e + 4
        average[left, left] = average[left, right] = 0.5
        average[right, left] = average[right, right] = 0.5
    first = np.concatenate([deriv.T, np.eye(128)], axis=1)
    later = np.concatenate([(deriv @ average).T, average.T], axis=1)
    steps = np.stack([np.concatenate([m, m], axis=0) for m in (first, later)])
    out_a, out_b = np.zeros((128, 128)), np.zeros((128, 128))
    out_a[:, :64] = average.T[:, 16:80]
    out_b[:, 64:] = average.T[:, 48:112]
    final = np.concatenate([out_a, out_a, out_b, out_b], axis=0)
    return steps.astype(ml_dtypes.bfloat16), final.astype(ml_dtypes.bfloat16)


def lane_vectors():
    vec = np.zeros((16, 128), np.float32)
    lane = np.arange(128)
    vec[0] = 1.0 / ROW_SCALE[lane % 4]
    for c in range(N_COMP):
        for h in range(2):
            y = c * 128 + lane + (-16 if h == 0 else 16)
            vec[1 + 2 * c + h] = DT * 0.5 * np.sin(2.0 * np.pi * (y + 0.5) / (128 * N_COMP))
    return vec


def split_bf16(x):
    hi = x.astype(BF16)
    return hi, (x - hi.astype(F32)).astype(BF16)


def iota(shape, dim):
    return lax.broadcasted_iota(I32, shape, dim)


def mm(a, b):
    return jnp.dot(a, b, preferred_element_type=F32)


def mm_t(a, b):
    return lax.dot_general(a, b, (((0,), (0,)), ((), ())), preferred_element_type=F32)


def slots_kernel(src_ref, wanted_ref, tcol_ref):
    s = src_ref[...] >> 2
    tile = (s >> 5).astype(F32)
    row = (s & 31).astype(F32)
    r0, a0 = iota((64, 8), 0), iota((64, 8), 1)
    pick_row = ((r0 >> 3) == a0).astype(F32)
    own = (r0 & 7) == a0
    tile_c = jnp.sum(jnp.where(own, mm(pick_row, tile), 0.0), axis=1, keepdims=True)
    b1, r1 = iota((8, 64), 0), iota((8, 64), 1)
    pick_col = (b1 == (r1 & 7)).astype(F32)
    own_t = b1 == (r1 >> 3)
    tile_r = jnp.sum(jnp.where(own_t, mm(tile, pick_col), 0.0), axis=0, keepdims=True)
    row_r = jnp.sum(jnp.where(own_t, mm(row, pick_col), 0.0), axis=0, keepdims=True)
    same = jnp.where(tile_c == tile_r, 1.0, 0.0)
    sub, lane = iota((64, 64), 0), iota((64, 64), 1)
    rank_c = jnp.sum(jnp.where(lane < sub, same, 0.0), axis=1, keepdims=True)
    rank_r = jnp.sum(jnp.where(sub < lane, same, 0.0), axis=0, keepdims=True)
    slot_c = (tile_c * 4.0 + rank_c).astype(I32)
    slot_r = (tile_r * 4.0 + rank_r).astype(I32)
    slot_wide = jnp.broadcast_to(slot_c, (64, 128))
    field = iota((64, 8, 128), 1)
    tcol = jnp.where(field < 4, slot_wide[:, None, :] * 4 + field, -1)
    tcol_ref[...] = tcol.reshape(512, 128)
    q = iota((512, 64), 0)
    val = jnp.sum(jnp.where((q >> 2) == slot_r, row_r + 1.0, 0.0), axis=1, keepdims=True) - 1.0
    f = (iota((512, 1), 0) & 3).astype(F32)
    target = jnp.where(val >= 0.0, f * 32.0 + val, -1.0)
    wanted_ref[...] = jnp.broadcast_to(target, (512, 128)).astype(BF16)


def x_pack_kernel(par_ref, atm_ref, flags_ref, ocean_ref, off_ref, w_ref, out_ref):
    par = par_ref[0]
    flags = flags_ref[...].astype(F32)
    off = off_ref[...].astype(F32)
    pad = jnp.zeros((2, 128), F32)
    for slot, rows, cells in ((par, 16, 768), (1 - par, 0, 0)):
        out_ref[slot, 0:64] = atm_ref[:, rows : rows + 16, :].astype(BF16)
        out_ref[slot, 64] = flags[rows : rows + 16].astype(BF16)
        for part in range(2):
            lanes = slice(cells + 128 * part, cells + 128 * part + 128)
            values = ocean_ref[:, lanes].reshape(4, 16, 128)
            out_ref[slot, 65 + 4 * part : 69 + 4 * part] = values.astype(BF16)
        last = slice(896, 1024) if cells else slice(0, 128)
        pair = jnp.concatenate([off[:, last], pad, w_ref[:, last], pad], axis=0)
        out_ref[slot, 73] = pair.astype(BF16)


def y_pack_kernel(par_ref, atm_ref, flags_ref, xa_ref, xb_ref, xp_ref, out_ref):
    par_t, par_c = par_ref[0], par_ref[1]
    comp = par_ref[2]
    even = par_t == 0
    lane = iota((64, 128), 1)

    def full_plane(main, p):
        a, b = xa_ref[p].astype(F32), xb_ref[p].astype(F32)
        return jnp.concatenate([main, jnp.where(even, a, b), jnp.where(even, b, a)], axis=0)

    def store(q, planes):
        right = jnp.zeros((64, 128), F32)
        left = jnp.zeros((64, 128), F32)
        for s, plane in enumerate(planes):
            here = (lane >> 4) == s
            right = jnp.where(here, pltpu.roll(plane, (s * 16 + 16) % 128, 1), right)
            left = jnp.where(here, pltpu.roll(plane, s * 16, 1) if s else plane, left)
        out_ref[par_c, q] = right.astype(BF16)
        out_ref[1 - par_c, q] = left.astype(BF16)

    def group(q, _):
        store(q, [full_plane(atm_ref[q * 8 + s], q * 8 + s) for s in range(8)])
        return 0

    lax.fori_loop(0, 8, group, 0)
    store(8, [full_plane(flags_ref[...].astype(F32), 64)])
    for j in range(3):
        for part in range(4):
            p = 65 + 4 * j + part
            rows = slice(16 * part, 16 * part + 16)
            if p >= X_PLANES:
                out_ref[0, 9 + j, rows] = jnp.zeros((16, 128), BF16)
                out_ref[1, 9 + j, rows] = jnp.zeros((16, 128), BF16)
                continue
            a, b = xa_ref[p].astype(F32), xb_ref[p].astype(F32)
            from_left, from_right = jnp.where(even, b, a), jnp.where(even, a, b)
            own_right, own_left = xp_ref[par_t, p].astype(F32), xp_ref[1 - par_t, p].astype(F32)
            right = jnp.where(comp == N_COMP - 1, from_left, own_right)
            left = jnp.where(comp == 0, from_right, own_left)
            out_ref[par_c, 9 + j, rows] = right.astype(BF16)
            out_ref[1 - par_c, 9 + j, rows] = left.astype(BF16)


def atm_kernel(
    par_ref,
    winds_ref,
    fm_ref,
    oc_ref,
    atm_ref,
    flags_ref,
    xa_ref,
    xb_ref,
    ya_ref,
    yb_ref,
    served_ref,
    rhs_ref,
    rout_ref,
    vec_ref,
    out_ref,
    rows_ref,
    cb_ref,
    abuf_ref,
    dbuf_ref,
    cs_ref,
    tm_ref,
    r5_ref,
    m5_ref,
    ts_ref,
    facc_ref,
    gs_ref,
):
    par_t, par_c = par_ref[0], par_ref[1]
    comp = par_ref[2]
    even_t, even_c = par_t == 0, par_c == 0
    lane = iota((64, 128), 1)

    def tiles(main, p, y_right, y_left, slot):
        a, b = xa_ref[p].astype(F32), xb_ref[p].astype(F32)
        full = jnp.concatenate([main, jnp.where(even_t, a, b), jnp.where(even_t, b, a)], axis=0)
        left = pltpu.roll(y_left, (128 - slot * 16) % 128, 1) if slot else y_left
        shift = (112 - slot * 16) % 128
        right = pltpu.roll(y_right, shift, 1) if shift else y_right
        ts_ref[slot, 0] = jnp.where(lane < 16, left, pltpu.roll(full, 16, 1))
        ts_ref[slot, 1] = jnp.where(lane >= 112, right, pltpu.roll(full, 112, 1))

    def y_sides(q):
        a, b = ya_ref[q].astype(F32), yb_ref[q].astype(F32)
        return jnp.where(even_c, a, b), jnp.where(even_c, b, a)

    def put(h, l, k, i, value):
        hi, lo = split_bf16(value)
        cb_ref[h, l, k, i, :, 0:128] = hi
        cb_ref[h, l, k, i, :, 128:256] = lo

    def load_group(q, _):
        y_right, y_left = y_sides(q)
        k, half = q // 2, q % 2
        for s in range(8):
            p = q * 8 + s
            tiles(atm_ref[p], p, y_right, y_left, s)
        for s in range(8):
            for h in range(2):
                for i in range(4):
                    put(h, half * 8 + s, k, i, ts_ref[s, h, pl.ds(i, 16, stride=4), :])
        return 0

    lax.fori_loop(0, 8, load_group, 0)
    y_right, y_left = y_sides(8)
    tiles(flags_ref[...].astype(F32), 64, y_right, y_left, 0)
    for h in range(2):
        for i in range(4):
            flag = ts_ref[0, h, pl.ds(i, 16, stride=4), :]
            r5_ref[h, i] = jnp.where(flag == 1.0, 5.0 * DT, 0.0)
            m5_ref[h, i] = jnp.where(flag == 2.0, 5.0 * DT, 0.0)
            total = jnp.zeros((16, 128), F32)
            for l in range(LEVELS):
                pair = cb_ref[h, l, 2, i].astype(F32)
                total = total + (pair[:, 0:128] + pair[:, 128:256])
            cs_ref[h, i] = total
    facc_ref[...] = jnp.zeros_like(facc_ref)

    def main_view(l):
        left = cb_ref[0, l].reshape(256, 256)
        right = cb_ref[1, l].reshape(256, 256)
        both = jnp.concatenate([left, right], axis=1)
        return mm(both, rout_ref[...]).reshape(4, 4, 16, 128)

    inv = vec_ref[0:1, :]
    dt_y = -DT * inv

    def step(si, _):
        which = jnp.minimum(si, 1)

        def one_tile(h, _):
            ff = vec_ref[pl.ds(1 + 2 * comp + h, 1), :]
            hi, lo = split_bf16(cs_ref[h].reshape(64, 128) * (1.0 / LEVELS))
            tm = mm(jnp.concatenate([hi, lo], axis=1), rhs_ref[which])
            tm_ref[...] = tm[:, 128:256].reshape(4, 16, 128)
            cs_ref[h] = jnp.zeros((4, 16, 128), F32)

            def expand(l):
                both = mm(cb_ref[h, l].reshape(256, 256), rhs_ref[which])
                dbuf_ref[l] = both[:, 0:128].reshape(4, 4, 16, 128)
                abuf_ref[l] = both[:, 128:256].reshape(4, 4, 16, 128)

            expand(0)
            expand(1)

            def level(l, _):
                expand(jnp.minimum(l + 2, LEVELS - 1))
                above, below = jnp.minimum(l + 1, LEVELS - 1), jnp.maximum(l - 1, 0)
                cx = -DT * winds_ref[0, l]
                cy = dt_y * winds_ref[1, l]
                a = [[abuf_ref[l, k, i] for i in range(4)] for k in range(4)]

                def dx(k, i):
                    total = None
                    for j in range(4):
                        if abs(DERIV[i, j]) > 1e-9:
                            term = float(DERIV[i, j]) * a[k][j]
                            total = term if total is None else total + term
                    return total

                new = [[None] * 4 for _ in range(4)]
                for i in range(4):
                    m5 = m5_ref[h, i]
                    d = [dx(k, i) for k in range(4)]
                    dy = [dbuf_ref[l, k, i] for k in range(4)]
                    extra = [
                        ff * a[1][i] - DT * d[3],
                        dt_y * dy[3] - ff * a[0][i],
                        r5_ref[h, i] * (tm_ref[i] - a[2][i]),
                        dt_y * dy[1] - DT * d[0],
                    ]
                    for k in range(4):
                        mix = abuf_ref[above, k, i] + abuf_ref[below, k, i] - 2.0 * a[k][i]
                        new[k][i] = a[k][i] + (
                            (cx * d[k] + cy * dy[k]) + (extra[k] + m5 * mix)
                        )
                for k in range(4):
                    first = 0.5 * (new[k][0] + pltpu.roll(new[k][3], 1, 0))
                    values = [first, new[k][1], new[k][2], pltpu.roll(first, 15, 0)]
                    for i in range(4):
                        put(h, l, k, i, values[i])
                        if k == 2:
                            cs_ref[h, i] += values[i]
                return 0

            lax.fori_loop(0, LEVELS, level, 0)
            return 0

        lax.fori_loop(0, 2, one_tile, 0)
        surface = main_view(0)
        for i in range(4):
            u, v, t, z = [surface[k, i, 0:8] for k in range(4)]
            speed = jnp.sqrt(u * u + v * v + 1.0)
            for c in range(NFLUX):
                m = (fm_ref[c, 0] * u + fm_ref[c, 1] * v) + (fm_ref[c, 2] * t + fm_ref[c, 3] * z)
                facc_ref[c, i] += speed * m * lax.rsqrt(1.0 + 0.5 * (m * m))
        return 0

    lax.fori_loop(0, STEPS, step, 0)

    def finish(l, _):
        value = main_view(l)
        for k in range(4):
            for i in range(4):
                out_ref[k * LEVELS + l, pl.ds(i, 8, stride=4), :] = value[k, i, 0:8]
        return 0

    lax.fori_loop(0, LEVELS, finish, 0)
    for i in range(4):
        mean = [(facc_ref[c, i] * (1.0 / STEPS)).astype(BF16).astype(F32) for c in range(NFLUX)]
        for g in range(4):
            total = oc_ref[g, 0] * mean[0]
            for c in range(1, NFLUX):
                total = total + oc_ref[g, c] * mean[c]
            gs_ref[g, pl.ds(i, 8, stride=4), :] = 0.25 * total
    table = gs_ref[...].reshape(128, 128).astype(BF16)
    pick = served_ref[...].astype(F32) == iota((512, 128), 1).astype(F32)
    rows_ref[...] = mm(jnp.where(pick, 1.0, 0.0).astype(BF16), table).astype(BF16)


def ocean_kernel(par_ref, ocean_ref, off_ref, w_ref, ya_ref, yb_ref, n2_ref, wm_ref, sw_ref, o1_ref):
    even_c = par_ref[1] == 0
    comp = par_ref[2]

    def halo_rows(j, part):
        rows = slice(16 * part, 16 * part + 16)
        a, b = ya_ref[9 + j, rows].astype(F32), yb_ref[9 + j, rows].astype(F32)
        return jnp.where(even_c, b, a), jnp.where(even_c, a, b)

    pieces = [halo_rows(n // 4, n % 4) for n in range(9)]
    left = [jnp.concatenate([p[0] for p in pieces[4 * n : 4 * n + 4]], axis=0) for n in range(2)]
    right = [jnp.concatenate([p[1] for p in pieces[4 * n : 4 * n + 4]], axis=0) for n in range(2)]
    values = {-2: left[0], -1: left[1], 8: right[0], 9: right[1]}
    for b in range(8):
        values[b] = ocean_ref[:, 128 * b : 128 * b + 128]
    offw = {-1: pieces[8][0], 8: pieces[8][1]}
    source = iota((384, 128), 0)
    lane = iota((1, 128), 1)
    level = iota((64, 128), 0) & 15

    def matrix(b):
        if b in offw:
            off, w = offw[b][0:6].astype(I32), offw[b][8:14]
        else:
            cells = slice(128 * b, 128 * b + 128)
            off, w = off_ref[:, cells], w_ref[:, cells].astype(BF16).astype(F32)
        total = jnp.zeros((384, 128), F32)
        for j in range(6):
            total = total + jnp.where(source == lane + off[j : j + 1], w[j : j + 1], 0.0)
        return total.astype(BF16), jnp.sum(w, axis=0, keepdims=True)

    def update(own, window, wm, sw):
        hi, lo = split_bf16(window)
        both = mm(jnp.concatenate([hi, lo], axis=0), wm)
        lateral = both[0:64] + both[64:128] - sw * own
        above = jnp.where(level == 15, own, pltpu.roll(own, 63, 0))
        below = jnp.where(level == 0, own, pltpu.roll(own, 1, 0))
        rot = jnp.concatenate([jnp.zeros((32, 128), F32), 0.2 * own[48:64], -0.2 * own[32:48]], axis=0)
        return own + lateral + 0.2 * (above - 2.0 * own + below) + rot

    for b in range(-1, 9):
        wm, sw = matrix(b)
        if 0 <= b < 8:
            wm_ref[b] = wm
            sw_ref[:, 128 * b : 128 * b + 128] = jnp.broadcast_to(sw, (8, 128))
        window = jnp.concatenate([values[b - 1], values[b], values[b + 1]], axis=1)
        o1_ref[b + 1] = update(values[b], window, wm, sw)
    for b in range(8):
        window = jnp.concatenate([o1_ref[b], o1_ref[b + 1], o1_ref[b + 2]], axis=1)
        cells = slice(128 * b, 128 * b + 128)
        n2_ref[:, cells] = update(o1_ref[b + 1], window, wm_ref[b], sw_ref[0:1, cells])


def request_matrix(tcol_ref):
    parts = []
    for chunk in range(4):
        hit = tcol_ref[...] == iota((512, 128), 1) + 128 * chunk
        parts.append(jnp.where(hit, 1.0, 0.0).astype(BF16))
    return jnp.concatenate(parts, axis=1)


def forcing_kernel(par_ref, rows_ref, tcol_ref, weights_ref, f_ref, edge_ref):
    par_c = par_ref[1]
    gathered = mm(request_matrix(tcol_ref), rows_ref[...])
    for b in range(8):
        lhs = jnp.concatenate(
            [gathered[(b * 8 + k) * 8 : (b * 8 + k) * 8 + 8] for k in range(8)], axis=1
        ).astype(BF16)
        f_ref[:, 128 * b : 128 * b + 128] = mm(lhs, weights_ref[b])
    edge_ref[par_c] = f_ref[:, 896:1024]
    edge_ref[1 - par_c] = f_ref[:, 0:128]


def return_kernel(
    par_ref,
    n2_ref,
    wm_ref,
    sw_ref,
    f_ref,
    ea_ref,
    eb_ref,
    tcol_ref,
    weights_ref,
    ocean_ref,
    sent_ref,
    parts_ref,
):
    even_c = par_ref[1] == 0
    ea, eb = ea_ref[...], eb_ref[...]
    blocks = [jnp.where(even_c, eb, ea)]
    blocks += [f_ref[:, 128 * b : 128 * b + 128] for b in range(8)]
    blocks += [jnp.where(even_c, ea, eb)]
    ocean_ref[...] = n2_ref[...]
    for b in range(8):
        cells = slice(128 * b, 128 * b + 128)
        window = jnp.concatenate(blocks[b : b + 3], axis=1)
        hi, lo = split_bf16(window)
        own = blocks[b + 1]
        both = mm(jnp.concatenate([hi.astype(F32), lo.astype(F32)], axis=0).astype(BF16), wm_ref[b])
        top = both[0:8] + both[8:16] + (1.8 - sw_ref[:, cells]) * own
        surface = []
        for k in range(4):
            value = n2_ref[16 * k : 16 * k + 1, cells] + top[k : k + 1]
            if k == 2:
                value = value + 0.2 * own[3:4]
            if k == 3:
                value = value - 0.2 * own[2:3]
            ocean_ref[16 * k : 16 * k + 1, cells] = value
            below = n2_ref[16 * k + 1 : 16 * k + 2, cells] + 0.2 * own[k : k + 1]
            ocean_ref[16 * k + 1 : 16 * k + 2, cells] = below
            surface.append(value)
        lhs = jnp.concatenate(surface + [jnp.zeros((4, 128), F32)], axis=0).astype(BF16)
        for k in range(8):
            part = mm(lhs, weights_ref[b, k])
            parts_ref[(b * 8 + k) * 8 : (b * 8 + k) * 8 + 8, :] = part
    sent_ref[...] = mm_t(request_matrix(tcol_ref), parts_ref[...].astype(BF16)).astype(BF16)


def collect_kernel(served_ref, incoming_ref, out_ref):
    pick = served_ref[...].astype(F32) == iota((512, 128), 1).astype(F32)
    owner = jnp.where(pick, 1.0, 0.0).astype(BF16)
    out_ref[...] = mm_t(owner, incoming_ref[...]).reshape(4, 32, 128)


def swap_pairs(n):
    near = [(i, i ^ 1) for i in range(n)]
    far = [(i, (i + 1) % n if i % 2 else (i - 1) % n) for i in range(n)]
    return near, far


def exchange(payload, axis, n):
    near, far = swap_pairs(n)
    return lax.ppermute(payload[0], axis, near), lax.ppermute(payload[1], axis, far)


def to_tiles(rows):
    moved = lax.all_to_all(
        rows.reshape(N_TILE, 16, 128), "tile", split_axis=0, concat_axis=0, tiled=True
    )
    return moved.reshape(512, 128)


def call(kernel, out, specs, scratch=(), mib=48, cost=None):
    return pl.pallas_call(
        kernel,
        out_shape=out,
        in_specs=specs,
        out_specs=jax.tree.map(lambda _: VMEM, out),
        scratch_shapes=list(scratch),
        compiler_params=pltpu.CompilerParams(vmem_limit_bytes=mib * 2**20),
        cost_estimate=cost,
    )


def per_device(
    atm_state,
    level_winds,
    physics_flags,
    flux_matrix,
    regrid_source,
    regrid_weights,
    return_weights,
    ocean_state,
    ocean_neighbors,
    edge_weights,
    ocean_coupling,
):
    S = jax.ShapeDtypeStruct
    t, c = lax.axis_index("tile"), lax.axis_index("comp")
    par = jnp.stack([t % 2, c % 2, c, t]).astype(I32)
    atm = atm_state.reshape(64, 32, 128)
    ocean = ocean_state.reshape(64, 1024)
    steps_np, final_np = lane_matrices()
    rhs, rout, vec = jnp.asarray(steps_np), jnp.asarray(final_np), jnp.asarray(lane_vectors())

    wanted, tcol = call(slots_kernel, (S((512, 128), BF16), S((512, 128), I32)), [VMEM])(
        regrid_source
    )
    served = to_tiles(wanted)
    x_payload = call(x_pack_kernel, S((2, X_PLANES, 16, 128), BF16), [SMEM] + [VMEM] * 5)(
        par, atm, physics_flags, ocean, ocean_neighbors, edge_weights
    )
    xa, xb = exchange(x_payload, "tile", N_TILE)
    y_payload = call(y_pack_kernel, S((2, Y_PLANES, 64, 128), BF16), [SMEM] + [VMEM] * 5)(
        par, atm, physics_flags, xa, xb, x_payload
    )
    ya, yb = exchange(y_payload, "comp", N_COMP)
    atm_final, rows = call(
        atm_kernel,
        (S((64, 32, 128), F32), S((512, 128), BF16)),
        [SMEM] * 4 + [VMEM] * 10,
        [
            pltpu.VMEM((2, LEVELS, 4, 4, 16, 256), BF16),
            pltpu.VMEM((LEVELS, 4, 4, 16, 128), F32),
            pltpu.VMEM((LEVELS, 4, 4, 16, 128), F32),
            pltpu.VMEM((2, 4, 16, 128), F32),
            pltpu.VMEM((4, 16, 128), F32),
            pltpu.VMEM((2, 4, 16, 128), F32),
            pltpu.VMEM((2, 4, 16, 128), F32),
            pltpu.VMEM((8, 2, 64, 128), F32),
            pltpu.VMEM((NFLUX, 4, 8, 128), F32),
            pltpu.VMEM((4, 32, 128), F32),
        ],
    )(
        par,
        level_winds,
        flux_matrix,
        ocean_coupling,
        atm,
        physics_flags,
        xa,
        xb,
        ya,
        yb,
        served,
        rhs,
        rout,
        vec,
    )
    mean_rows = to_tiles(rows)
    n2, wm, sw = call(
        ocean_kernel,
        (S((64, 1024), F32), S((8, 384, 128), BF16), S((8, 1024), F32)),
        [SMEM] + [VMEM] * 5,
        [pltpu.VMEM((10, 64, 128), F32)],
        cost=pl.CostEstimate(flops=2**27, bytes_accessed=2**24, transcendentals=0),
    )(par, ocean, ocean_neighbors, edge_weights, ya, yb)
    forcing, edges = call(forcing_kernel, (S((8, 1024), F32), S((2, 8, 128), F32)), [SMEM] + [VMEM] * 3)(
        par, mean_rows, tcol, regrid_weights.reshape(8, 1024, 128)
    )
    ea, eb = exchange(edges, ("tile", "comp"), N_TILE * N_COMP)
    ocean_final, sent = call(
        return_kernel,
        (S((64, 1024), F32), S((512, 128), BF16)),
        [SMEM] + [VMEM] * 8,
        [pltpu.VMEM((512, 128), F32)],
    )(par, n2, wm, sw, forcing, ea, eb, tcol, return_weights)
    incoming = to_tiles(sent)
    ocean_on_atm = call(collect_kernel, S((4, 32, 128), F32), [VMEM] * 2)(served, incoming)
    return (
        atm_final.reshape(atm_state.shape),
        ocean_final.reshape(ocean_state.shape),
        ocean_on_atm,
    )


def solution(mesh):
    return jax.shard_map(
        per_device,
        mesh=mesh,
        in_specs=(
            P(None, None, "tile", "comp"),
            P(),
            P("tile", "comp"),
            P(),
            P(("tile", "comp"), None),
            P(("tile", "comp"), None, None, None),
            P(("tile", "comp"), None, None, None),
            P(None, None, ("tile", "comp")),
            P(None, ("tile", "comp")),
            P(None, ("tile", "comp")),
            P(),
        ),
        out_specs=(
            P(None, None, "tile", "comp"),
            P(None, None, ("tile", "comp")),
            P(None, "tile", "comp"),
        ),
        check_vma=False,
    )
```

time: 529 us -> 136 us (0.26)
  the two profiles are of different devices: /device:TPU:17 before, /device:TPU:0 now
where the time goes in v1:
time: 136 us; the launch traced here: 135 us
  Pallas kernels  61.7 us (45%)
  blocking collectives  24 us (18%)
  waiting for transfers between devices  20.7 us (15%)
  starting transfers between devices  18.2 us (13%)
  local copies, waits for them, and re-layouts  9.62 us (7%)
    pallas_call x1, Pallas kernels, per_device(): call(atm_kernel, (S((64, 32, 128), F32), S((512, 128), BF16)), [SMEM] * 4...  49.8 us
    all_to_all x2, blocking collectives, to_tiles(): lax.all_to_all(rows.reshape(N_TILE, 16, 128), 'tile', split_axis=0, conca...  24 us
    ppermute x3, waiting for transfers between devices, exchange(): lax.ppermute(payload[1], axis, far)  10.6 us
    unnamed x49, local copies, waits for them, and re-layouts  8.73 us
    ppermute x3, starting transfers between devices, exchange(): lax.ppermute(payload[1], axis, far)  8.64 us
    all_to_all x1, waiting for transfers between devices, to_tiles(): lax.all_to_all(rows.reshape(N_TILE, 16, 128), 'tile', split_axis=0, conca...  8.61 us
    all_to_all x1, starting transfers between devices, to_tiles(): lax.all_to_all(rows.reshape(N_TILE, 16, 128), 'tile', split_axis=0, conca...  5.69 us
    ppermute x3, starting transfers between devices, exchange(): lax.ppermute(payload[0], axis, near)  3.84 us
  transfers between devices with their start and end apart: 7, of which 4 were waited for; matrix products, arithmetic and copies ran while one was open for 0% of the time, Pallas kernels for 3%

profile of v1, /device:TPU:0, one launch (start us, length us, event | category | flops | bytes accessed | tf_op | source)
XLA Modules:
  0.0 135.1 jit_solution(3132753106661914025)
XLA Ops:
  0.6 0.1 pad_add_fusion.par_ref
  0.7 0.0 copy-start
  0.7 1.2 copy-done
  2.0 0.9 copy-done.6
  2.9 0.0 copy-start.11
  2.9 0.7 copy-done.11
  3.6 0.8 copy-done.13
  4.4 0.8 copy-done.15
  5.1 0.6 shard_map.157.xp_ref
  5.8 0.0 copy-start.20
  5.8 0.1 slice_bitcast_fusion
  5.9 0.0 copy-start.23
  5.9 0.0 copy-start.1
  5.9 0.0 copy-start.12
  5.9 0.0 copy-start.19
  5.9 0.0 copy-start.21
  5.9 0.0 copy-start.22
  6.0 7.4 %collective-permute-start.1 = (bf16[74,16,128]{2,1,0:T(8,128)(2,1)S(1)}, bf16[74,16,128]{2,1,0:T(8,128)(2,1)S(1)}, u32[]{:S(2)}, u32[]{:S(2)}) collective-permute-start(bf16[74,16,128]{2,1,0:T(8,128)(2,1)S(1)} %get-tuple-element.25), channel_id=1, source_target_pairs={{0,124},{4,8},{8,4},{12,16},{16,12},{20,24},{24,20},{28,32},{32,28... | collective-permute-start | bytes 909320 | tf_op jit(solution)/shard_map/ppermute | solution.py:493
  13.4 0.0 collective-permute-start
  13.4 7.2 %collective-permute-done.1.xb_ref = bf16[74,16,128]{2,1,0:T(8,128)(2,1)S(1)} collective-permute-done((bf16[74,16,128]{2,1,0:T(8,128)(2,1)S(1)}, bf16[74,16,128]{2,1,0:T(8,128)(2,1)S(1)}, u32[]{:S(2)}, u32[]{:S(2)}) %collective-permute-start.1) | collective-permute-done | bytes 303136 | tf_op jit(solution)/shard_map/ppermute | solution.py:493
  20.5 1.5 %collective-permute-done.xa_ref = bf16[74,16,128]{2,1,0:T(8,128)(2,1)S(1)} collective-permute-done((bf16[74,16,128]{2,1,0:T(8,128)(2,1)S(1)}, bf16[74,16,128]{2,1,0:T(8,128)(2,1)S(1)}, u32[]{:S(2)}, u32[]{:S(2)}) %collective-permute-start) | collective-permute-done | bytes 303136 | tf_op jit(solution)/shard_map/ppermute | solution.py:493
  22.0 1.7 %shard_map.158 = bf16[2,12,64,128]{3,2,1,0:T(8,128)(2,1)S(1)} custom-call(s32[4]{0:T(128)S(1)} %pad_add_fusion.par_ref, f32[64,32,128]{2,1,0:T(8,128)S(1)} %bitcast.28, s32[32,128]{1,0:T(8,128)S(1)} %copy-done.11, bf16[74,16,128]{2,1,0:T(8,128)(2,1)S(1)} %collective-permute-done.xa_ref, bf16[74,16,128]{2,1,0:T(8,128)(2,1)S(1)} %collective-permute-done.1.xb_ref, ...), custom_call_target="tpu_custom_call" | custom-call | tf_op jit(solution)/shard_map/pallas_call | solution.py:544
  23.7 0.0 copy-start.2
  23.7 0.8 slice_bitcast_fusion.2
  24.5 0.0 copy-done.4
  24.5 1.1 collective-permute-start.3
  25.6 1.9 %collective-permute-start.2 = (bf16[12,64,128]{2,1,0:T(8,128)(2,1)}, bf16[12,64,128]{2,1,0:T(8,128)(2,1)}, u32[]{:S(2)}, u32[]{:S(2)}) collective-permute-start(bf16[12,64,128]{2,1,0:T(8,128)(2,1)} %get-tuple-element.28), channel_id=1, source_target_pairs={{0,1},{1,0},{2,3},{3,2},{4,5},{5,4},{6,7},{7,6},{8,9},{9,8},{10,11... | collective-permute-start | bytes 589832 | tf_op jit(solution)/shard_map/ppermute | solution.py:493
  27.5 0.0 copy-done.20
  27.5 0.4 shard_map.159
  27.9 0.0 copy-start.8
  27.9 0.7 copy-done.8
  28.6 0.6 copy-done.18
  29.2 5.7 %all-to-all-start = ((bf16[32,16,128]{2,1,0:T(8,128)(2,1)}), bf16[32,16,128]{2,1,0:T(8,128)(2,1)}, u32[]{:S(2)}, u32[]{:S(2)}) async-start(bf16[32,16,128]{2,1,0:T(8,128)(2,1)} %bitcast.37), calls=%async_computation | async-start | bytes 262144 | tf_op jit(solution)/shard_map/all_to_all | solution.py:497
  34.9 0.0 copy-done.23
  34.9 0.1 copy.17.fm_ref
  35.0 8.6 %all-to-all-done = bf16[32,16,128]{2,1,0:T(8,128)(2,1)} async-done(((bf16[32,16,128]{2,1,0:T(8,128)(2,1)}), bf16[32,16,128]{2,1,0:T(8,128)(2,1)}, u32[]{:S(2)}, u32[]{:S(2)}) %all-to-all-start) | async-done | bytes 131104 | tf_op jit(solution)/shard_map/all_to_all | solution.py:497
  43.7 0.0 collective-permute-done.3.yb_ref
  43.7 0.0 collective-permute-done.2.ya_ref
  43.7 0.0 copy-done.1
  43.7 0.0 copy-done.12
  43.7 0.0 copy-done.19
  43.7 0.0 copy-done.21
  43.7 0.0 copy-done.22
  43.7 0.0 copy-start.5
  43.7 1.0 copy-done.5
  44.7 0.9 copy-done.10
  45.6 0.9 copy-done.17
  46.5 49.8 %shard_map.160 = (f32[64,32,128]{2,1,0:T(8,128)}, bf16[512,128]{1,0:T(8,128)(2,1)S(1)}) custom-call(s32[4]{0:T(128)S(1)} %pad_add_fusion.par_ref, f32[2,16]{1,0:T(2,128)S(1)} %copy-done.22, f32[12,4]{1,0:T(8,128)S(1)} %copy.17.fm_ref, f32[4,12]{1,0:T(4,128)S(1)} %copy-done.21, f32[64,32,128]{2,1,0:T(8,128)S(1)} %bitcast.29, s32[32,128]{1,0:T(8,128)S(1)} %copy-done.12, ...), custom_call_target="tpu_custom_call" | custom-call | tf_op jit(solution)/shard_map/pallas_call | solution.py:548
  96.3 12.3 %all_to_all.15 = bf16[32,16,128]{2,1,0:T(8,128)(2,1)S(1)} all-to-all(bf16[32,16,128]{2,1,0:T(8,128)(2,1)S(1)} %bitcast.36), channel_id=1, replica_groups=mesh['tile'=32,'comp'=4] {'tile'}, dimensions={0} | all-to-all | bytes 262144 | tf_op jit(solution)/shard_map/all_to_all | solution.py:497
  108.6 0.0 copy-done.2
  108.6 0.0 copy-done.9
  108.6 1.3 shard_map.162
  110.0 0.1 collective-permute-start.5
  110.1 2.0 %collective-permute-start.4 = (f32[8,128]{1,0:T(8,128)S(1)}, f32[8,128]{1,0:T(8,128)S(1)}, u32[]{:S(2)}, u32[]{:S(2)}) collective-permute-start(f32[8,128]{1,0:T(8,128)S(1)} %get-tuple-element.30), channel_id=1, source_target_pairs={{0,1},{1,0},{2,3},{3,2},{4,5},{5,4},{6,7},{7,6},{8,9},{9,8},{10,11... | collective-permute-start | bytes 12296 | tf_op jit(solution)/shard_map/ppermute | solution.py:493
  112.0 0.0 copy-done.7
  112.0 0.0 copy-done.14
  112.0 0.0 copy-done.16
  112.0 3.1 %shard_map.161 = (f32[64,1024]{1,0:T(8,128)S(1)}, bf16[8,384,128]{2,1,0:T(8,128)(2,1)S(1)}, f32[8,1024]{1,0:T(8,128)S(1)}) custom-call(s32[4]{0:T(128)S(1)} %pad_add_fusion.par_ref, f32[64,1024]{1,0:T(8,128)S(1)} %bitcast.32, s32[6,1024]{1,0:T(8,128)S(1)} %copy-done.14, f32[6,1024]{1,0:T(8,128)S(1)} %copy-done.16, ...), custom_call_target="tpu_custom_call" | custom-call | flops 134217728 | bytes 16777216 | tf_op jit(solution)/shard_map/pallas_call | solution.py:581
  115.1 3.4 %collective-permute-done.5.eb_ref = f32[8,128]{1,0:T(8,128)S(1)} collective-permute-done((f32[8,128]{1,0:T(8,128)S(1)}, f32[8,128]{1,0:T(8,128)S(1)}, u32[]{:S(2)}, u32[]{:S(2)}) %collective-permute-start.5) | collective-permute-done | bytes 4128 | tf_op jit(solution)/shard_map/ppermute | solution.py:493
  118.5 0.0 collective-permute-done.4.ea_ref
  118.5 0.0 copy-done.3
  118.5 3.1 %shard_map.163 = (f32[64,1024]{1,0:T(8,128)}, bf16[512,128]{1,0:T(8,128)(2,1)S(1)}) custom-call(s32[4]{0:T(128)S(1)} %pad_add_fusion.par_ref, f32[64,1024]{1,0:T(8,128)S(1)} %get-tuple-element.16.n2_ref, bf16[8,384,128]{2,1,0:T(8,128)(2,1)S(1)} %get-tuple-element.17.wm_ref, f32[8,1024]{1,0:T(8,128)S(1)} %get-tuple-element.18.sw_ref, ...), custom_call_target="tpu_custom_call" | custom-call | tf_op jit(solution)/shard_map/pallas_call | solution.py:592
  121.6 11.7 %all_to_all.16 = bf16[32,16,128]{2,1,0:T(8,128)(2,1)S(1)} all-to-all(bf16[32,16,128]{2,1,0:T(8,128)(2,1)S(1)} %bitcast.35), channel_id=1, replica_groups=mesh['tile'=32,'comp'=4] {'tile'}, dimensions={0} | all-to-all | bytes 262144 | tf_op jit(solution)/shard_map/all_to_all | solution.py:497
  133.3 1.8 %shard_map.164 = f32[4,32,128]{2,1,0:T(8,128)} custom-call(bf16[512,128]{1,0:T(8,128)(2,1)} %bitcast.11.served_ref, bf16[512,128]{1,0:T(8,128)(2,1)S(1)} %bitcast.33), custom_call_target="tpu_custom_call" | custom-call | tf_op jit(solution)/shard_map/pallas_call | solution.py:599
  (13 shorter events, 0.0 us)
Async XLA Ops:
  0.7 1.2 copy-start
  2.0 0.9 copy-start.6
  2.9 0.7 copy-start.11
  3.6 0.8 copy-start.13
  4.4 0.8 copy-start.15
  5.8 21.7 %copy-start.20 = (s32[8,8]{1,0:T(8,128)S(1)}, s32[8,8]{1,0:T(8,128)}, u32[]{:S(2)}) copy-start(s32[8,8]{1,0:T(8,128)} %src_ref.1) | copy-start | bytes 772
  5.9 29.1 %copy-start.23 = (f32[12,4]{0,1:T(4,128)S(1)}, f32[12,4]{0,1:T(4,128)}, u32[]{:S(2)}) copy-start(f32[12,4]{0,1:T(4,128)} %param.17) | copy-start | bytes 580
  5.9 37.8 %copy-start.1 = (f32[4,16,32,128]{3,2,1,0:T(8,128)S(1)}, f32[4,16,32,128]{3,2,1,0:T(8,128)}, u32[]{:S(2)}) copy-start(f32[4,16,32,128]{3,2,1,0:T(8,128)} %param.14) | copy-start | bytes 3145732
  5.9 37.8 %copy-start.12 = (s32[32,128]{1,0:T(8,128)S(1)}, s32[32,128]{1,0:T(8,128)}, u32[]{:S(2)}) copy-start(s32[32,128]{1,0:T(8,128)} %flags_ref.5) | copy-start | bytes 49156
  5.9 37.8 %copy-start.19 = (f32[16,128]{1,0:T(8,128)S(1)}, f32[16,128]{1,0:T(8,128)}, u32[]{:S(2)}) copy-start(f32[16,128]{1,0:T(8,128)} %constant.34.clone.vec_ref) | copy-start | bytes 24580
  5.9 37.8 %copy-start.21 = (f32[4,12]{1,0:T(4,128)S(1)}, f32[4,12]{1,0:T(4,128)}, u32[]{:S(2)}) copy-start(f32[4,12]{1,0:T(4,128)} %oc_ref.1) | copy-start | bytes 580
  5.9 37.8 %copy-start.22 = (f32[2,16]{1,0:T(2,128)S(1)}, f32[2,16]{1,0:T(2,128)}, u32[]{:S(2)}) copy-start(f32[2,16]{1,0:T(2,128)} %winds_ref.1) | copy-start | bytes 388
  6.0 14.6 %collective-permute-start.1 = (bf16[74,16,128]{2,1,0:T(8,128)(2,1)S(1)}, bf16[74,16,128]{2,1,0:T(8,128)(2,1)S(1)}, u32[]{:S(2)}, u32[]{:S(2)}) collective-permute-start(bf16[74,16,128]{2,1,0:T(8,128)(2,1)S(1)} %get-tuple-element.25), channel_id=1, source_target_pairs={{0,124},{4,8},{8,4},{12,16},{16,12},{20,24},{24,20},{28,32},{32,28... | collective-permute-start | bytes 909320 | tf_op jit(solution)/shard_map/ppermute | solution.py:493
  13.4 8.6 %collective-permute-start = (bf16[74,16,128]{2,1,0:T(8,128)(2,1)S(1)}, bf16[74,16,128]{2,1,0:T(8,128)(2,1)S(1)}, u32[]{:S(2)}, u32[]{:S(2)}) collective-permute-start(bf16[74,16,128]{2,1,0:T(8,128)(2,1)S(1)} %get-tuple-element.26), channel_id=1, source_target_pairs={{0,4},{4,0},{8,12},{12,8},{16,20},{20,16},{24,28},{28,24},{32,36},... | collective-permute-start | bytes 909320 | tf_op jit(solution)/shard_map/ppermute | solution.py:493
  22.0 2.5 %copy-start.4 = (bf16[74,16,128]{2,1,0:T(8,128)(2,1)}, bf16[74,16,128]{2,1,0:T(8,128)(2,1)S(1)}, u32[]{:S(2)}) copy-start(bf16[74,16,128]{2,1,0:T(8,128)(2,1)S(1)} %collective-permute-done.xa_ref) | copy-start | bytes 909316
  23.7 85.0 %copy-start.2 = (bf16[8,8,128,128]{3,2,1,0:T(8,128)(2,1)S(1)}, bf16[8,8,128,128]{3,2,1,0:T(8,128)(2,1)}, u32[]{:S(2)}) copy-start(bf16[8,8,128,128]{3,2,1,0:T(8,128)(2,1)} %param.19) | copy-start | bytes 6291460
  24.5 19.2 %collective-permute-start.3 = (bf16[12,64,128]{2,1,0:T(8,128)(2,1)}, bf16[12,64,128]{2,1,0:T(8,128)(2,1)}, u32[]{:S(2)}, u32[]{:S(2)}) collective-permute-start(bf16[12,64,128]{2,1,0:T(8,128)(2,1)} %get-tuple-element.27), channel_id=1, source_target_pairs={{0,3},{1,2},{2,1},{3,0},{4,7},{5,6},{6,5},{7,4},{8,11},{9,10},{10,... | collective-permute-start | bytes 589832 | tf_op jit(solution)/shard_map/ppermute | solution.py:493
  25.6 18.0 %collective-permute-start.2 = (bf16[12,64,128]{2,1,0:T(8,128)(2,1)}, bf16[12,64,128]{2,1,0:T(8,128)(2,1)}, u32[]{:S(2)}, u32[]{:S(2)}) collective-permute-start(bf16[12,64,128]{2,1,0:T(8,128)(2,1)} %get-tuple-element.28), channel_id=1, source_target_pairs={{0,1},{1,0},{2,3},{3,2},{4,5},{5,4},{6,7},{7,6},{8,9},{9,8},{10,11... | collective-permute-start | bytes 589832 | tf_op jit(solution)/shard_map/ppermute | solution.py:493
  27.9 0.7 copy-start.8
  28.6 0.6 copy-start.18
  29.2 14.4 %all-to-all-start = ((bf16[32,16,128]{2,1,0:T(8,128)(2,1)}), bf16[32,16,128]{2,1,0:T(8,128)(2,1)}, u32[]{:S(2)}, u32[]{:S(2)}) async-start(bf16[32,16,128]{2,1,0:T(8,128)(2,1)} %bitcast.37), calls=%async_computation | async-start | bytes 262144 | tf_op jit(solution)/shard_map/all_to_all | solution.py:497
  43.7 1.0 copy-start.5
  44.7 0.9 copy-start.10
  45.6 0.9 copy-start.17
  46.5 62.1 %copy-start.9 = (s32[512,128]{1,0:T(8,128)S(1)}, s32[512,128]{1,0:T(8,128)}, u32[]{:S(2)}) copy-start(s32[512,128]{1,0:T(8,128)} %copy-done.8) | copy-start | bytes 786436
  46.5 65.5 %copy-start.7 = (f32[4,16,1024]{2,1,0:T(8,128)S(1)}, f32[4,16,1024]{2,1,0:T(8,128)}, u32[]{:S(2)}) copy-start(f32[4,16,1024]{2,1,0:T(8,128)} %param.21) | copy-start | bytes 786436
  46.5 65.5 %copy-start.14 = (s32[6,1024]{1,0:T(8,128)S(1)}, s32[6,1024]{1,0:T(8,128)}, u32[]{:S(2)}) copy-start(s32[6,1024]{1,0:T(8,128)} %off_ref.3) | copy-start | bytes 73732
  46.5 65.5 %copy-start.16 = (f32[6,1024]{1,0:T(8,128)S(1)}, f32[6,1024]{1,0:T(8,128)}, u32[]{:S(2)}) copy-start(f32[6,1024]{1,0:T(8,128)} %w_ref.3) | copy-start | bytes 73732
  96.3 22.2 %copy-start.3 = (bf16[8,8,128,128]{3,2,1,0:T(8,128)(2,1)S(1)}, bf16[8,8,128,128]{3,2,1,0:T(8,128)(2,1)}, u32[]{:S(2)}) copy-start(bf16[8,8,128,128]{3,2,1,0:T(8,128)(2,1)} %weights_ref.1) | copy-start | bytes 6291460
  110.0 8.5 %collective-permute-start.5 = (f32[8,128]{1,0:T(8,128)S(1)}, f32[8,128]{1,0:T(8,128)S(1)}, u32[]{:S(2)}, u32[]{:S(2)}) collective-permute-start(f32[8,128]{1,0:T(8,128)S(1)} %get-tuple-element.29), channel_id=1, source_target_pairs={{0,127},{1,2},{2,1},{3,4},{4,3},{5,6},{6,5},{7,8},{8,7},{9,10},{10... | collective-permute-start | bytes 12296 | tf_op jit(solution)/shard_map/ppermute | solution.py:493
  110.1 8.5 %collective-permute-start.4 = (f32[8,128]{1,0:T(8,128)S(1)}, f32[8,128]{1,0:T(8,128)S(1)}, u32[]{:S(2)}, u32[]{:S(2)}) collective-permute-start(f32[8,128]{1,0:T(8,128)S(1)} %get-tuple-element.30), channel_id=1, source_target_pairs={{0,1},{1,0},{2,3},{3,2},{4,5},{5,4},{6,7},{7,6},{8,9},{9,8},{10,11... | collective-permute-start | bytes 12296 | tf_op jit(solution)/shard_map/ppermute | solution.py:493

commit v2 on v1

v2 whole, which is shorter than its diff:
```python
import functools

import jax
import jax.numpy as jnp
import ml_dtypes
import numpy as np
from jax import lax
from jax.experimental import pallas as pl
from jax.experimental.pallas import tpu as pltpu
from jax.sharding import PartitionSpec as P

F32 = jnp.float32
BF16 = jnp.bfloat16
I32 = jnp.int32
N_TILE, N_COMP = 32, 4
STEPS = 4
LEVELS = 16
NFLUX = 12
DT = 0.02
VMEM = pl.BlockSpec(memory_space=pltpu.VMEM)
HBM = pl.BlockSpec(memory_space=pltpu.HBM)
SMEM = pl.BlockSpec(memory_space=pltpu.SMEM)
X_PLANES = 74
Y_ROWS = 672


def gll_derivative():
    points = np.array([-1.0, -1.0 / np.sqrt(5.0), 1.0 / np.sqrt(5.0), 1.0])
    products = np.array(
        [np.prod([points[r] - points[s] for s in range(4) if s != r]) for r in range(4)]
    )
    table = np.zeros((4, 4))
    for r in range(4):
        for s in range(4):
            if r != s:
                table[r, s] = products[r] / (products[s] * (points[r] - points[s]))
    table[0, 0], table[3, 3] = -3.0, 3.0
    return 2.0 * table


DERIV = gll_derivative()
ROW_SCALE = np.array([1.375, 1.125, 1.125, 1.375])


SCALED = (DERIV * ROW_SCALE[:, None]).astype(ml_dtypes.bfloat16).astype(np.float64)


def y_nodes():
    lane = np.arange(32)
    return np.where(lane < 16, 143 - lane, 15 - lane)


def lane_operators(nodes):
    count = len(nodes)
    deriv, average = np.zeros((count, count)), np.eye(count)
    where = {int(y): p for p, y in enumerate(nodes)}
    for y, p in where.items():
        for j in range(4):
            deriv[p, where[y - y % 4 + j]] = SCALED[y % 4, j]
        other = y - 1 if y % 4 == 0 else y + 1
        if y % 4 in (0, 3) and other in where:
            average[p, p] = average[p, where[other]] = 0.5
    return deriv, average


def twice(*matrices):
    both = np.concatenate([m.T for m in matrices], axis=1)
    return np.concatenate([both, both], axis=0)


def lane_matrices():
    eye = np.eye(128)
    deriv, average = lane_operators(np.arange(128))
    main = np.stack([twice(deriv, eye), twice(deriv @ average, average)])
    halo_deriv, halo_average = lane_operators(y_nodes())
    dy, av = np.kron(np.eye(4), halo_deriv), np.kron(np.eye(4), halo_average)
    dx = np.kron(SCALED, np.eye(32))
    halo = np.stack([twice(dx, dy, eye), twice(dx @ av, dy @ av, av)])
    return np.concatenate([main, halo], axis=2).astype(ml_dtypes.bfloat16)


def lane_vectors():
    vec = np.zeros((16, 128), np.float32)
    lane = np.arange(128)
    halo = np.tile(y_nodes(), 4)
    vec[0] = 1.0 / ROW_SCALE[lane % 4]
    vec[1] = 1.0 / ROW_SCALE[halo % 4]
    vec[2] = 1.0 / ROW_SCALE[lane // 32]
    for c in range(N_COMP):
        for row, y in ((4 + c, lane), (8 + c, halo)):
            vec[row] = DT * 0.5 * np.sin(2.0 * np.pi * (c * 128 + y + 0.5) / (128 * N_COMP))
    return vec


def split_bf16(x):
    hi = x.astype(BF16)
    return hi, (x - hi.astype(F32)).astype(BF16)


def iota(shape, dim):
    return lax.broadcasted_iota(I32, shape, dim)


def mm(a, b):
    return jnp.dot(a, b, preferred_element_type=F32)


def mm_t(a, b):
    return lax.dot_general(a, b, (((0,), (0,)), ((), ())), preferred_element_type=F32)


def slots_kernel(src_ref, wanted_ref, tcol_ref):
    s = src_ref[...] >> 2
    tile = (s >> 5).astype(F32)
    row = (s & 31).astype(F32)
    r0, a0 = iota((64, 8), 0), iota((64, 8), 1)
    pick_row = ((r0 >> 3) == a0).astype(F32)
    own = (r0 & 7) == a0
    tile_c = jnp.sum(jnp.where(own, mm(pick_row, tile), 0.0), axis=1, keepdims=True)
    b1, r1 = iota((8, 64), 0), iota((8, 64), 1)
    pick_col = (b1 == (r1 & 7)).astype(F32)
    own_t = b1 == (r1 >> 3)
    tile_r = jnp.sum(jnp.where(own_t, mm(tile, pick_col), 0.0), axis=0, keepdims=True)
    row_r = jnp.sum(jnp.where(own_t, mm(row, pick_col), 0.0), axis=0, keepdims=True)
    same = jnp.where(tile_c == tile_r, 1.0, 0.0)
    sub, lane = iota((64, 64), 0), iota((64, 64), 1)
    rank_c = jnp.sum(jnp.where(lane < sub, same, 0.0), axis=1, keepdims=True)
    rank_r = jnp.sum(jnp.where(sub < lane, same, 0.0), axis=0, keepdims=True)
    slot_c = (tile_c * 4.0 + rank_c).astype(I32)
    slot_r = (tile_r * 4.0 + rank_r).astype(I32)
    slot_wide = jnp.broadcast_to(slot_c, (64, 128))
    field = iota((64, 8, 128), 1)
    tcol = jnp.where(field < 4, slot_wide[:, None, :] * 4 + field, -1)
    tcol_ref[...] = tcol.reshape(512, 128)
    q = iota((512, 64), 0)
    val = jnp.sum(jnp.where((q >> 2) == slot_r, row_r + 1.0, 0.0), axis=1, keepdims=True) - 1.0
    f = (iota((512, 1), 0) & 3).astype(F32)
    target = jnp.where(val >= 0.0, f * 32.0 + val, -1.0)
    wanted_ref[...] = jnp.broadcast_to(target, (512, 128)).astype(BF16)


def one_hot(rows, target):
    return jnp.where(iota((rows, 256), 0) == target, 1.0, 0.0).astype(BF16)


def pack_matrix():
    col = iota((1, 256), 1)
    lane = col & 127
    plane = ((lane >> 4) & 1) * 4 + (lane >> 5)
    return one_hot(1024, plane * 128 + (lane & 15) + jnp.where(col < 128, 0, 112))


def unpack_matrix():
    col = iota((1, 256), 1)
    quarter, n = (col & 127) >> 5, col & 31
    base = 32 * quarter + 16 * (col >> 7)
    return one_hot(256, base + jnp.where(n < 16, 15 - n, 159 - n))


def x_pack_kernel(
    par_ref, atm_ref, flags_ref, ocean_ref, off_ref, w_ref, a_ref, b_ref, flags_out_ref
):
    even = par_ref[0] == 0

    def put(index, right, left):
        a_ref[index] = jnp.where(even, right, left).astype(BF16)
        b_ref[index] = jnp.where(even, left, right).astype(BF16)

    put(slice(0, 64), atm_ref[:, 16:32, :], atm_ref[:, 0:16, :])
    flags = flags_ref[...].astype(F32)
    flags_out_ref[...] = flags
    put(64, flags[16:32], flags[0:16])
    for part in range(2):
        right, left = [
            ocean_ref[:, c + 128 * part : c + 128 * part + 128].reshape(4, 16, 128) for c in (768, 0)
        ]
        put(slice(65 + 4 * part, 69 + 4 * part), right, left)
    off = off_ref[...].astype(F32)
    pad = jnp.zeros((2, 128), F32)
    right, left = [
        jnp.concatenate([off[:, c : c + 128], pad, w_ref[:, c : c + 128], pad], axis=0)
        for c in (896, 0)
    ]
    put(73, right, left)


def x_extended(ts_ref, slot, main, xa_ref, xb_ref, p, even):
    a, b = xa_ref[p].astype(F32), xb_ref[p].astype(F32)
    ts_ref[slot, 0:32] = main
    ts_ref[slot, 32:48] = jnp.where(even, a, b)
    ts_ref[slot, 48:64] = jnp.where(even, b, a)
    return [ts_ref[slot, pl.ds(i, 16, stride=4), :] for i in range(4)]


def y_pack_kernel(
    par_ref, atm_ref, flags_ref, xa_ref, xb_ref, pa_ref, pb_ref, a_ref, b_ref, lhs_ref, ts_ref
):
    even_t, even_c = par_ref[0] == 0, par_ref[1] == 0
    comp = par_ref[2]

    def group(q, _):
        for s in range(8):
            p = q * 8 + s
            rows = x_extended(ts_ref, s, atm_ref[p], xa_ref, xb_ref, p, even_t)
            for i in range(4):
                lanes = slice(((s % 2) * 4 + i) * 128, ((s % 2) * 4 + i) * 128 + 128)
                lhs_ref[q * 4 + s // 2, :, lanes] = rows[i].astype(BF16)
        return 0

    lax.fori_loop(0, 8, group, 0)
    rows = x_extended(ts_ref, 0, flags_ref[...], xa_ref, xb_ref, 64, even_t)
    for i in range(4):
        lhs_ref[32, :, 128 * i : 128 * i + 128] = rows[i].astype(BF16)
    lhs_ref[32, :, 512:1024] = jnp.zeros((16, 512), BF16)
    moved = mm(lhs_ref[...].reshape(528, 1024), pack_matrix())
    left, right = moved[:, 0:128], moved[:, 128:256]
    a_ref[0:528] = jnp.where(even_c, right, left).astype(BF16)
    b_ref[0:528] = jnp.where(even_c, left, right).astype(BF16)
    for n in range(9):
        p = 65 + n
        dest = slice(528 + 16 * n, 544 + 16 * n)
        a, b = xa_ref[p].astype(F32), xb_ref[p].astype(F32)
        own_a, own_b = pa_ref[p].astype(F32), pb_ref[p].astype(F32)
        from_left, from_right = jnp.where(even_t, b, a), jnp.where(even_t, a, b)
        own_right, own_left = jnp.where(even_t, own_a, own_b), jnp.where(even_t, own_b, own_a)
        right = jnp.where(comp == N_COMP - 1, from_left, own_right)
        left = jnp.where(comp == 0, from_right, own_left)
        a_ref[dest] = jnp.where(even_c, right, left).astype(BF16)
        b_ref[dest] = jnp.where(even_c, left, right).astype(BF16)


def prepare_kernel(par_ref, atm_ref, flags_ref, xa_ref, xb_ref, cb_ref, flag_ref, ts_ref):
    even_t = par_ref[0] == 0

    def group(q, _):
        for s in range(8):
            p = q * 8 + s
            rows = x_extended(ts_ref, s, atm_ref[p], xa_ref, xb_ref, p, even_t)
            for i in range(4):
                hi, lo = split_bf16(rows[i])
                cb_ref[(q % 2) * 8 + s, q // 2, i, :, 0:128] = hi
                cb_ref[(q % 2) * 8 + s, q // 2, i, :, 128:256] = lo
        return 0

    lax.fori_loop(0, 8, group, 0)
    rows = x_extended(ts_ref, 0, flags_ref[...], xa_ref, xb_ref, 64, even_t)
    for i in range(4):
        flag_ref[i] = rows[i]


def x_slopes(a):
    sums, diffs = (a[0] + a[3], a[1] + a[2]), (a[0] - a[3], a[1] - a[2])
    across = sums[0] - sums[1]
    out = [None] * 4
    for i in range(2):
        d = DERIV[i]
        odd = float((d[0] - d[3]) / 2) * diffs[0] + float((d[1] - d[2]) / 2) * diffs[1]
        even = float((d[0] + d[3]) / 2) * across
        out[i], out[3 - i] = odd + even, odd - even
    return out


def atm_kernel(
    par_ref,
    scal_ref,
    first_ref,
    flag_ref,
    ya_ref,
    yb_ref,
    vec_ref,
    rhs_ref,
    out_ref,
    table_ref,
    cb_ref,
    abuf_ref,
    dbuf_ref,
    hcb_ref,
    hbuf_ref,
    tm_ref,
    mask_ref,
    r5_ref,
    facc_ref,
    gs_ref,
    first_sem,
    copies,
):
    first_copy = pltpu.make_async_copy(first_ref, cb_ref, first_sem)
    first_copy.start()
    even_c = par_ref[1] == 0
    comp = par_ref[2]
    lane = iota((16, 128), 1)
    edge = (lane == 0) | (lane == 127)
    quarter = lane >> 5
    halo_edge = ((lane & 31) == 15) | ((lane & 31) == 16)

    def put(ref, index, value):
        hi, lo = split_bf16(value)
        ref[(*index, slice(None), slice(0, 128))] = hi
        ref[(*index, slice(None), slice(128, 256))] = lo

    ya, yb = ya_ref[0:528].astype(F32), yb_ref[0:528].astype(F32)
    from_right, from_left = jnp.where(even_c, ya, yb), jnp.where(even_c, yb, ya)
    arrived = jnp.concatenate([from_right, from_left], axis=1).astype(BF16)
    halo = mm(arrived, unpack_matrix()).astype(BF16)
    for k in range(4):
        for l in range(LEVELS):
            rows = slice((k * 8 + l // 2) * 16, (k * 8 + l // 2) * 16 + 16)
            lanes = slice((l % 2) * 128, (l % 2) * 128 + 128)
            hcb_ref[l, k, :, 0:128] = halo[rows, lanes]
            hcb_ref[l, k, :, 128:256] = jnp.zeros((16, 128), BF16)
    halo_flag = halo[512:528, 0:128].astype(F32)
    halo_r5 = jnp.where(halo_flag == 1.0, 5.0 * DT, 0.0)
    halo_m5 = jnp.where(halo_flag == 2.0, 5.0 * DT, 0.0)
    halo_keep = 1.0 - 2.0 * halo_m5
    halo_keep_t = halo_keep - halo_r5
    for i in range(4):
        flag = flag_ref[i]
        m5 = jnp.where(flag == 2.0, 5.0 * DT, 0.0)
        r5_ref[i] = jnp.where(flag == 1.0, 5.0 * DT, 0.0)
        mask_ref[0, i] = m5
        mask_ref[1, i] = 1.0 - 2.0 * m5
        mask_ref[2, i] = 1.0 - 2.0 * m5 - r5_ref[i]
    facc_ref[...] = jnp.zeros_like(facc_ref)
    dt_y = -DT * vec_ref[0:1, :]
    halo_dt_y = -DT * vec_ref[1:2, :]
    halo_dt_x = -DT * vec_ref[2:3, :]
    ff = vec_ref[pl.ds(4 + comp, 1), :]
    halo_ff = vec_ref[pl.ds(8 + comp, 1), :]
    for copy in (first_copy, *copies):
        copy.wait()

    def step(si, _):
        which = jnp.minimum(si, 1)
        both = mm(cb_ref[...].reshape(4096, 256), rhs_ref[which, :, 0:256])
        dbuf_ref[...] = both[:, 0:128].reshape(LEVELS, 4, 4, 16, 128)
        abuf_ref[...] = both[:, 128:256].reshape(LEVELS, 4, 4, 16, 128)
        hbuf_ref[...] = mm(hcb_ref[...].reshape(1024, 256), rhs_ref[which, :, 256:640]).reshape(
            LEVELS, 4, 16, 384
        )
        for i in range(4):
            total = abuf_ref[0, 2, i]
            for l in range(1, LEVELS):
                total = total + abuf_ref[l, 2, i]
            mask_ref[3, i] = r5_ref[i] * (total * (1.0 / LEVELS))
        total = hbuf_ref[0, 2, :, 256:384]
        for l in range(1, LEVELS):
            total = total + hbuf_ref[l, 2, :, 256:384]
        tm_ref[...] = halo_r5 * (total * (1.0 / LEVELS))

        def level(l, _):
            above, below = jnp.minimum(l + 1, LEVELS - 1), jnp.maximum(l - 1, 0)
            wind_x, wind_y = scal_ref[l], scal_ref[LEVELS + l]
            cx = -DT * wind_x
            cy = dt_y * wind_y
            a = [[abuf_ref[l, k, i] for i in range(4)] for k in range(4)]

            slopes = [x_slopes(a[k]) for k in range(4)]
            new = [[None] * 4 for _ in range(4)]
            for i in range(4):
                m5, keep, keep_t, relax = [mask_ref[n, i] for n in range(4)]
                d = [slopes[k][i] for k in range(4)]
                dy = [dbuf_ref[l, k, i] for k in range(4)]
                extra = [
                    ff * a[1][i] - DT * d[3],
                    dt_y * dy[3] - ff * a[0][i],
                    relax,
                    dt_y * dy[1] - DT * d[0],
                ]
                for k in range(4):
                    mix = m5 * (abuf_ref[above, k, i] + abuf_ref[below, k, i])
                    own = (keep_t if k == 2 else keep) * a[k][i]
                    new[k][i] = (own + mix) + ((cx * d[k] + cy * dy[k]) + extra[k])

            halo_cx, halo_cy = halo_dt_x * wind_x, halo_dt_y * wind_y
            hx, hy, ha = [
                [hbuf_ref[l, k, :, 128 * n : 128 * n + 128] for k in range(4)] for n in range(3)
            ]
            extra = [
                halo_ff * ha[1] + halo_dt_x * hx[3],
                halo_dt_y * hy[3] - halo_ff * ha[0],
                tm_ref[...],
                halo_dt_y * hy[1] + halo_dt_x * hx[0],
            ]
            for k in range(4):
                first = 0.5 * (new[k][0] + pltpu.roll(new[k][3], 1, 0))
                values = [first, new[k][1], new[k][2], pltpu.roll(first, 15, 0)]
                up, down = hbuf_ref[above, k, :, 256:384], hbuf_ref[below, k, :, 256:384]
                own = (halo_keep_t if k == 2 else halo_keep) * ha[k] + halo_m5 * (up + down)
                own = own + ((halo_cx * hx[k] + halo_cy * hy[k]) + extra[k])
                lower = pltpu.roll(pltpu.roll(own, 32, 1), 1, 0)
                upper = pltpu.roll(pltpu.roll(own, 96, 1), 15, 0)
                partner = jnp.where(quarter == 0, lower, jnp.where(quarter == 3, upper, own))
                own = 0.5 * (own + partner)
                across = None
                for i in range(4):
                    moved = pltpu.roll(values[i], 32 * i + 16, 1)
                    across = moved if i == 0 else jnp.where(quarter == i, moved, across)
                    back = pltpu.roll(own, 112 - 32 * i, 1)
                    put(cb_ref, (l, k, i), jnp.where(edge, 0.5 * (values[i] + back), values[i]))
                put(hcb_ref, (l, k), jnp.where(halo_edge, 0.5 * (own + across), own))
            return 0

        lax.fori_loop(0, LEVELS, level, 0, unroll=2)
        surface = mm(cb_ref[0].reshape(256, 256), rhs_ref[1, :, 128:256]).reshape(4, 4, 16, 128)
        for i in range(4):
            u, v, t, z = [surface[k, i, 0:8] for k in range(4)]
            speed = jnp.sqrt(u * u + v * v + 1.0)
            for c in range(NFLUX):
                m0, m1, m2, m3 = [scal_ref[32 + 4 * c + k] for k in range(4)]
                m = (m0 * u + m1 * v) + (m2 * t + m3 * z)
                facc_ref[c, i] += speed * m * lax.rsqrt(1.0 + 0.5 * (m * m))
        return 0

    lax.fori_loop(0, STEPS, step, 0)
    final = mm(cb_ref[...].reshape(4096, 256), rhs_ref[1, :, 128:256]).reshape(LEVELS, 4, 4, 16, 128)
    for l in range(LEVELS):
        for k in range(4):
            for i in range(4):
                out_ref[k * LEVELS + l, pl.ds(i, 8, stride=4), :] = final[l, k, i, 0:8]
    for i in range(4):
        mean = [(facc_ref[c, i] * (1.0 / STEPS)).astype(BF16).astype(F32) for c in range(NFLUX)]
        for g in range(4):
            total = scal_ref[80 + 12 * g] * mean[0]
            for c in range(1, NFLUX):
                total = total + scal_ref[80 + 12 * g + c] * mean[c]
            gs_ref[g, pl.ds(i, 8, stride=4), :] = 0.25 * total
    table_ref[...] = gs_ref[...].reshape(128, 128).astype(BF16)


def pick_kernel(served_ref, table_ref, rows_ref):
    pick = served_ref[...].astype(F32) == iota((512, 128), 1).astype(F32)
    rows_ref[...] = mm(jnp.where(pick, 1.0, 0.0).astype(BF16), table_ref[...]).astype(BF16)


def ocean_kernel(par_ref, ocean_ref, off_ref, w_ref, ya_ref, yb_ref, n2_ref, wm_ref, sw_ref, o1_ref):
    even_c = par_ref[1] == 0

    def halo_rows(n):
        rows = slice(528 + 16 * n, 544 + 16 * n)
        a, b = ya_ref[rows].astype(F32), yb_ref[rows].astype(F32)
        return jnp.where(even_c, b, a), jnp.where(even_c, a, b)

    pieces = [halo_rows(n) for n in range(9)]
    left = [jnp.concatenate([p[0] for p in pieces[4 * n : 4 * n + 4]], axis=0) for n in range(2)]
    right = [jnp.concatenate([p[1] for p in pieces[4 * n : 4 * n + 4]], axis=0) for n in range(2)]
    values = {-2: left[0], -1: left[1], 8: right[0], 9: right[1]}
    for b in range(8):
        values[b] = ocean_ref[:, 128 * b : 128 * b + 128]
    offw = {-1: pieces[8][0], 8: pieces[8][1]}
    source = iota((384, 128), 0)
    lane = iota((1, 128), 1)
    level = iota((64, 128), 0) & 15

    def matrix(b):
        if b in offw:
            off, w = offw[b][0:6].astype(I32), offw[b][8:14]
        else:
            cells = slice(128 * b, 128 * b + 128)
            off, w = off_ref[:, cells], w_ref[:, cells].astype(BF16).astype(F32)
        total = jnp.zeros((384, 128), F32)
        for j in range(6):
            total = total + jnp.where(source == lane + off[j : j + 1], w[j : j + 1], 0.0)
        return total.astype(BF16), jnp.sum(w, axis=0, keepdims=True)

    def update(own, window, wm, sw):
        hi, lo = split_bf16(window)
        both = mm(jnp.concatenate([hi, lo], axis=0), wm)
        lateral = both[0:64] + both[64:128] - sw * own
        above = jnp.where(level == 15, own, pltpu.roll(own, 63, 0))
        below = jnp.where(level == 0, own, pltpu.roll(own, 1, 0))
        rot = jnp.concatenate([jnp.zeros((32, 128), F32), 0.2 * own[48:64], -0.2 * own[32:48]], axis=0)
        return own + lateral + 0.2 * (above - 2.0 * own + below) + rot

    for b in range(-1, 9):
        wm, sw = matrix(b)
        if 0 <= b < 8:
            wm_ref[b] = wm
            sw_ref[:, 128 * b : 128 * b + 128] = jnp.broadcast_to(sw, (8, 128))
        window = jnp.concatenate([values[b - 1], values[b], values[b + 1]], axis=1)
        o1_ref[b + 1] = update(values[b], window, wm, sw)
    for b in range(8):
        window = jnp.concatenate([o1_ref[b], o1_ref[b + 1], o1_ref[b + 2]], axis=1)
        cells = slice(128 * b, 128 * b + 128)
        n2_ref[:, cells] = update(o1_ref[b + 1], window, wm_ref[b], sw_ref[0:1, cells])


def request_matrix(tcol_ref):
    parts = []
    for chunk in range(4):
        hit = tcol_ref[...] == iota((512, 128), 1) + 128 * chunk
        parts.append(jnp.where(hit, 1.0, 0.0).astype(BF16))
    return jnp.concatenate(parts, axis=1)


def forcing_kernel(par_ref, rows_ref, tcol_ref, weights_ref, f_ref, a_ref, b_ref):
    even_c = par_ref[1] == 0
    gathered = mm(request_matrix(tcol_ref), rows_ref[...])
    for b in range(8):
        lhs = jnp.concatenate(
            [gathered[(b * 8 + k) * 8 : (b * 8 + k) * 8 + 8] for k in range(8)], axis=1
        ).astype(BF16)
        f_ref[:, 128 * b : 128 * b + 128] = mm(lhs, weights_ref[b])
    right, left = f_ref[:, 896:1024], f_ref[:, 0:128]
    a_ref[...] = jnp.where(even_c, right, left)
    b_ref[...] = jnp.where(even_c, left, right)


def return_kernel(
    par_ref,
    n2_ref,
    wm_ref,
    sw_ref,
    f_ref,
    ea_ref,
    eb_ref,
    tcol_ref,
    weights_ref,
    ocean_ref,
    sent_ref,
    parts_ref,
):
    even_c = par_ref[1] == 0
    ea, eb = ea_ref[...], eb_ref[...]
    blocks = [jnp.where(even_c, eb, ea)]
    blocks += [f_ref[:, 128 * b : 128 * b + 128] for b in range(8)]
    blocks += [jnp.where(even_c, ea, eb)]
    ocean_ref[...] = n2_ref[...]
    for b in range(8):
        cells = slice(128 * b, 128 * b + 128)
        window = jnp.concatenate(blocks[b : b + 3], axis=1)
        hi, lo = split_bf16(window)
        own = blocks[b + 1]
        both = mm(jnp.concatenate([hi.astype(F32), lo.astype(F32)], axis=0).astype(BF16), wm_ref[b])
        top = both[0:8] + both[8:16] + (1.8 - sw_ref[:, cells]) * own
        surface = []
        for k in range(4):
            value = n2_ref[16 * k : 16 * k + 1, cells] + top[k : k + 1]
            if k == 2:
                value = value + 0.2 * own[3:4]
            if k == 3:
                value = value - 0.2 * own[2:3]
            ocean_ref[16 * k : 16 * k + 1, cells] = value
            below = n2_ref[16 * k + 1 : 16 * k + 2, cells] + 0.2 * own[k : k + 1]
            ocean_ref[16 * k + 1 : 16 * k + 2, cells] = below
            surface.append(value)
        lhs = jnp.concatenate(surface + [jnp.zeros((4, 128), F32)], axis=0).astype(BF16)
        wide = jnp.concatenate([weights_ref[b, k] for k in range(8)], axis=1)
        parts = mm(lhs, wide)
        for k in range(8):
            rows = slice((b * 8 + k) * 8, (b * 8 + k) * 8 + 8)
            parts_ref[rows, :] = parts[:, 128 * k : 128 * k + 128]
    sent_ref[...] = mm_t(request_matrix(tcol_ref), parts_ref[...].astype(BF16)).astype(BF16)


def collect_kernel(served_ref, incoming_ref, out_ref):
    pick = served_ref[...].astype(F32) == iota((512, 128), 1).astype(F32)
    owner = jnp.where(pick, 1.0, 0.0).astype(BF16)
    out_ref[...] = mm_t(owner, incoming_ref[...]).reshape(4, 32, 128)


def swap_pairs(n):
    near = [(i, i ^ 1) for i in range(n)]
    far = [(i, (i + 1) % n if i % 2 else (i - 1) % n) for i in range(n)]
    return near, far


def exchange(payloads, axis, n):
    near, far = swap_pairs(n)
    return lax.ppermute(payloads[0], axis, near), lax.ppermute(payloads[1], axis, far)


def to_tiles(rows):
    moved = lax.all_to_all(
        rows.reshape(N_TILE, 16, 128), "tile", split_axis=0, concat_axis=0, tiled=True
    )
    return moved.reshape(512, 128)


def call(kernel, out, specs, scratch=(), mib=16, cost=None):
    return pl.pallas_call(
        kernel,
        out_shape=out,
        in_specs=specs,
        out_specs=jax.tree.map(lambda _: VMEM, out),
        scratch_shapes=list(scratch),
        compiler_params=pltpu.CompilerParams(vmem_limit_bytes=mib * 2**20),
        cost_estimate=cost,
    )


def staged(kernel, out, scalars, resident, arrays, scratch=(), late=0, mib=16, cost=None):
    n_lead, n = len(scalars) + len(resident), len(arrays)
    n_out = len(jax.tree.leaves(out))

    def body(*refs):
        lead_refs, hbm_refs = refs[:n_lead], refs[n_lead : n_lead + n]
        out_refs = refs[n_lead + n : n_lead + n + n_out]
        held, (sems, *rest) = refs[-n - 1 - len(scratch) :][:n], refs[-1 - len(scratch) :]
        copies = [pltpu.make_async_copy(hbm_refs[i], held[i], sems.at[i]) for i in range(n)]
        for copy in copies:
            copy.start()
        for copy in copies[: n - late]:
            copy.wait()
        extra = (copies[n - late :],) if late else ()
        kernel(*lead_refs, *held, *out_refs, *rest, *extra)

    buffers = [pltpu.VMEM(a.shape, a.dtype) for a in arrays]
    scratch_shapes = buffers + [pltpu.SemaphoreType.DMA((n,))] + list(scratch)
    specs = [SMEM] * len(scalars) + [VMEM] * len(resident) + [HBM] * n
    return call(body, out, specs, scratch_shapes, mib, cost)(*scalars, *resident, *arrays)


ATM_SCRATCH = (
    pltpu.VMEM((LEVELS, 4, 4, 16, 256), BF16),
    pltpu.VMEM((LEVELS, 4, 4, 16, 128), F32),
    pltpu.VMEM((LEVELS, 4, 4, 16, 128), F32),
    pltpu.VMEM((LEVELS, 4, 16, 256), BF16),
    pltpu.VMEM((LEVELS, 4, 16, 384), F32),
    pltpu.VMEM((16, 128), F32),
    pltpu.VMEM((4, 4, 16, 128), F32),
    pltpu.VMEM((4, 16, 128), F32),
    pltpu.VMEM((NFLUX, 4, 8, 128), F32),
    pltpu.VMEM((4, 32, 128), F32),
    pltpu.SemaphoreType.DMA,
)


def per_device(
    atm_state,
    level_winds,
    physics_flags,
    flux_matrix,
    regrid_source,
    regrid_weights,
    return_weights,
    ocean_state,
    ocean_neighbors,
    edge_weights,
    ocean_coupling,
):
    S = jax.ShapeDtypeStruct
    t, c = lax.axis_index("tile"), lax.axis_index("comp")
    par = jnp.stack([t % 2, c % 2, c, t]).astype(I32)
    atm = atm_state.reshape(64, 32, 128)
    ocean = ocean_state.reshape(64, 1024)
    scal = jnp.concatenate(
        [level_winds.reshape(-1), flux_matrix.reshape(-1), ocean_coupling.reshape(-1)]
    )
    rhs = jnp.asarray(lane_matrices())
    vec = jnp.asarray(lane_vectors())

    xp_a, xp_b, flags = staged(
        x_pack_kernel,
        (S((X_PLANES, 16, 128), BF16),) * 2 + (S((32, 128), F32),),
        (par,),
        (),
        (atm, physics_flags, ocean, ocean_neighbors, edge_weights),
        mib=12,
    )
    xa, xb = exchange((xp_a, xp_b), "tile", N_TILE)
    wanted, tcol = call(slots_kernel, (S((512, 128), BF16), S((512, 128), I32)), [VMEM])(
        regrid_source
    )
    wanted, tcol, xb = lax.optimization_barrier((wanted, tcol, xb))
    served = to_tiles(wanted)
    y_payload = call(
        y_pack_kernel,
        (S((Y_ROWS, 128), BF16),) * 2,
        [SMEM] + [VMEM] * 6,
        [pltpu.VMEM((33, 16, 1024), BF16), pltpu.VMEM((8, 64, 128), F32)],
    )(par, atm, flags, xa, xb, xp_a, xp_b)
    ya, yb = exchange(y_payload, "comp", N_COMP)
    first, flag = call(
        prepare_kernel,
        (S((LEVELS, 4, 4, 16, 256), BF16), S((4, 16, 128), F32)),
        [SMEM] + [VMEM] * 4,
        [pltpu.VMEM((8, 64, 128), F32)],
        cost=pl.CostEstimate(flops=2**23, bytes_accessed=2**23, transcendentals=0),
    )(par, atm, flags, xa, xb)
    atm_final, table = staged(
        atm_kernel,
        (S((64, 32, 128), F32), S((128, 128), BF16)),
        (par, scal),
        (first, flag, ya, yb),
        (vec, rhs),
        ATM_SCRATCH,
        late=1,
        mib=32,
        cost=pl.CostEstimate(flops=2**33, bytes_accessed=2**26, transcendentals=0),
    )
    rows = call(pick_kernel, S((512, 128), BF16), [VMEM] * 2)(served, table)
    mean_rows = to_tiles(rows)
    n2, wm, sw = call(
        ocean_kernel,
        (S((64, 1024), F32), S((8, 384, 128), BF16), S((8, 1024), F32)),
        [SMEM] + [VMEM] * 5,
        [pltpu.VMEM((10, 64, 128), F32)],
        cost=pl.CostEstimate(flops=2**27, bytes_accessed=2**24, transcendentals=0),
    )(par, ocean, ocean_neighbors, edge_weights, ya, yb)
    forcing, *edges = call(
        forcing_kernel,
        (S((8, 1024), F32), S((8, 128), F32), S((8, 128), F32)),
        [SMEM] + [VMEM] * 3,
    )(par, mean_rows, tcol, regrid_weights.reshape(8, 1024, 128))
    ea, eb = exchange(edges, ("tile", "comp"), N_TILE * N_COMP)
    ocean_final, sent = call(
        return_kernel,
        (S((64, 1024), F32), S((512, 128), BF16)),
        [SMEM] + [VMEM] * 8,
        [pltpu.VMEM((512, 128), F32)],
    )(par, n2, wm, sw, forcing, ea, eb, tcol, return_weights)
    incoming = to_tiles(sent)
    ocean_on_atm = call(collect_kernel, S((4, 32, 128), F32), [VMEM] * 2)(served, incoming)
    return (
        atm_final.reshape(atm_state.shape),
        ocean_final.reshape(ocean_state.shape),
        ocean_on_atm,
    )


def solution(mesh):
    return jax.shard_map(
        per_device,
        mesh=mesh,
        in_specs=(
            P(None, None, "tile", "comp"),
            P(),
            P("tile", "comp"),
            P(),
            P(("tile", "comp"), None),
            P(("tile", "comp"), None, None, None),
            P(("tile", "comp"), None, None, None),
            P(None, None, ("tile", "comp")),
            P(None, ("tile", "comp")),
            P(None, ("tile", "comp")),
            P(),
        ),
        out_specs=(
            P(None, None, "tile", "comp"),
            P(None, None, ("tile", "comp")),
            P(None, "tile", "comp"),
        ),
        check_vma=False,
    )
```

time: 136 us -> 98.7 us (0.73)
  Pallas kernels: 61.7 us -> 32.9 us
  waiting for transfers between devices: 20.7 us -> 10.5 us
  blocking collectives: 24 us -> 28.6 us
  local copies, waits for them, and re-layouts: 9.62 us -> 6.57 us
    pallas_call x4 -> x6, Pallas kernels: 53.4 us -> 25.6 us  [the longest x2 21.8 us: staged(): call(body, out, specs, scratch_shapes, mib, cost)]
    all_to_all x1, waiting for transfers between devices: 8.61 us -> 0.01 us  [to_tiles(): lax.all_to_all(rows.reshape(N_TILE, 16, 128), 'tile', split_axis=0, conca...]
    all_to_all x2, blocking collectives: 24 us -> 28.6 us  [to_tiles(): lax.all_to_all(rows.reshape(N_TILE, 16, 128), 'tile', split_axis=0, conca...]
    unnamed x49 -> x35, local copies, waits for them, and re-layouts: 8.73 us -> 6.32 us
    ppermute x6, waiting for transfers between devices: 12 us -> 10.5 us  [the longest x3 9.05 us: exchange(): lax.ppermute(payloads[1], axis, far)]
  transfers between devices with their start and end apart: 7 -> 7, of which waited for: 4 -> 3; matrix products, arithmetic and copies ran while one was open for 0% -> 0% of each run, Pallas kernels for 3% -> 26%
where the time goes in v2:
time: 98.7 us; the launch traced here: 98.1 us
  Pallas kernels  32.9 us (33%)
  blocking collectives  28.6 us (29%)
  starting transfers between devices  18.5 us (19%)
  waiting for transfers between devices  10.5 us (11%)
  local copies, waits for them, and re-layouts  6.57 us (7%)
    all_to_all x2, blocking collectives, to_tiles(): lax.all_to_all(rows.reshape(N_TILE, 16, 128), 'tile', split_axis=0, conca...  28.6 us
    pallas_call x2, Pallas kernels, staged(): call(body, out, specs, scratch_shapes, mib, cost)  21.8 us
    ppermute x3, starting transfers between devices, exchange(): lax.ppermute(payloads[1], axis, far)  12.7 us
    ppermute x3, waiting for transfers between devices, exchange(): lax.ppermute(payloads[1], axis, far)  9.05 us
    unnamed x35, local copies, waits for them, and re-layouts  6.32 us
    all_to_all x1, starting transfers between devices, to_tiles(): lax.all_to_all(rows.reshape(N_TILE, 16, 128), 'tile', split_axis=0, conca...  5.57 us
    pallas_call x1, Pallas kernels, per_device(): call(return_kernel, (S((64, 1024), F32), S((512, 128), BF16)), [SMEM] + [...  2.81 us
    pallas_call x1, Pallas kernels, per_device(): call(ocean_kernel, (S((64, 1024), F32), S((8, 384, 128), BF16), S((8, 102...  2.6 us
  transfers between devices with their start and end apart: 7, of which 3 were waited for; matrix products, arithmetic and copies ran while one was open for 0% of the time, Pallas kernels for 26%

profile of v2, /device:TPU:0, one launch (start us, length us, event | category | flops | bytes accessed | tf_op | source)
XLA Modules:
  0.0 98.1 jit_solution(3945105535427352779)
XLA Ops:
  0.6 0.0 copy-start.14
  0.6 0.0 copy-start.16
  0.7 0.0 copy-start.15
  0.7 0.1 pad_add_fusion.refs_0_.par_ref
  0.8 0.0 copy-start
  0.8 1.2 %copy-done = f32[4,16,32,128]{3,2,1,0:T(8,128)S(1)} copy-done((f32[4,16,32,128]{3,2,1,0:T(8,128)S(1)}, f32[4,16,32,128]{3,2,1,0:T(8,128)}, u32[]{:S(2)}) %copy-start) | copy-done | bytes 1048600
  2.0 0.0 copy-start.4
  2.0 0.9 copy-done.4
  2.9 0.0 copy-start.6
  2.9 0.8 copy-done.6
  3.7 0.0 copy-start.8
  3.7 0.8 copy-done.8
  4.5 0.0 copy-start.10
  4.5 0.7 copy-done.10
  5.2 0.0 copy-start.1
  5.2 0.9 shard_map.148
  6.0 7.4 %collective-permute-start.1 = (bf16[74,16,128]{2,1,0:T(8,128)(2,1)S(1)}, bf16[74,16,128]{2,1,0:T(8,128)(2,1)S(1)}, u32[]{:S(2)}, u32[]{:S(2)}) collective-permute-start(bf16[74,16,128]{2,1,0:T(8,128)(2,1)S(1)} %get-tuple-element.29.pb_ref), channel_id=1, source_target_pairs={{0,124},{4,8},{8,4},{12,16},{16,12},{20,24},{24,20},{28,32},{32,28... | collective-permute-start | bytes 909320 | tf_op jit(solution)/shard_map/ppermute | solution.py:569
  13.5 0.0 collective-permute-start
  13.5 0.0 copy-start.11
  13.5 0.7 copy-done.11
  14.1 1.0 %shard_map.149 = (bf16[512,128]{1,0:T(8,128)(2,1)}, s32[512,128]{1,0:T(8,128)S(1)}) custom-call(s32[8,8]{1,0:T(8,128)S(1)} %copy-done.11), custom_call_target="tpu_custom_call" | custom-call | tf_op jit(solution)/shard_map/pallas_call | solution.py:661
  15.2 5.5 %collective-permute-done.1.xb_ref = bf16[74,16,128]{2,1,0:T(8,128)(2,1)S(1)} collective-permute-done((bf16[74,16,128]{2,1,0:T(8,128)(2,1)S(1)}, bf16[74,16,128]{2,1,0:T(8,128)(2,1)S(1)}, u32[]{:S(2)}, u32[]{:S(2)}) %collective-permute-start.1) | collective-permute-done | bytes 303136 | tf_op jit(solution)/shard_map/ppermute | solution.py:569
  20.6 1.5 %collective-permute-done.xa_ref = bf16[74,16,128]{2,1,0:T(8,128)(2,1)S(1)} collective-permute-done((bf16[74,16,128]{2,1,0:T(8,128)(2,1)S(1)}, bf16[74,16,128]{2,1,0:T(8,128)(2,1)S(1)}, u32[]{:S(2)}, u32[]{:S(2)}) %collective-permute-start) | collective-permute-done | bytes 303136 | tf_op jit(solution)/shard_map/ppermute | solution.py:569
  22.1 0.0 copy-done.1
  22.1 1.3 %shard_map.151 = (bf16[672,128]{1,0:T(8,128)(2,1)S(1)}, bf16[672,128]{1,0:T(8,128)(2,1)S(1)}) custom-call(s32[4]{0:T(128)S(1)} %pad_add_fusion.refs_0_.par_ref, f32[64,32,128]{2,1,0:T(8,128)S(1)} %bitcast.16, f32[32,128]{1,0:T(8,128)S(1)} %get-tuple-element.25.flags_ref, bf16[74,16,128]{2,1,0:T(8,128)(2,1)S(1)} %collective-permute-done.xa_ref, ...), custom_call_target="tpu_custom_call" | custom-call | tf_op jit(solution)/shard_map/pallas_call | solution.py:666
  23.4 0.1 collective-permute-start.2
  23.5 3.0 %collective-permute-start.3 = (bf16[672,128]{1,0:T(8,128)(2,1)S(1)}, bf16[672,128]{1,0:T(8,128)(2,1)S(1)}, u32[]{:S(2)}, u32[]{:S(2)}) collective-permute-start(bf16[672,128]{1,0:T(8,128)(2,1)S(1)} %get-tuple-element.34), channel_id=1, source_target_pairs={{0,3},{1,2},{2,1},{3,0},{4,7},{5,6},{6,5},{7,4},{8,11},{9,10},{10,... | collective-permute-start | bytes 516104 | tf_op jit(solution)/shard_map/ppermute | solution.py:569
  26.5 0.0 copy-done.14
  26.5 0.1 copy.17
  26.6 0.1 reshape.49
  26.7 0.0 copy-done.16
  26.7 0.1 reshape.48
  26.8 0.0 copy-done.15
  26.8 0.1 reshape.50
  26.9 0.1 pad_maximum_fusion.refs_1_
  27.0 5.6 %all-to-all-start = ((bf16[32,16,128]{2,1,0:T(8,128)(2,1)}), bf16[32,16,128]{2,1,0:T(8,128)(2,1)S(1)}, u32[]{:S(2)}, u32[]{:S(2)}) async-start(bf16[32,16,128]{2,1,0:T(8,128)(2,1)} %bitcast.7), calls=%async_computation | async-start | bytes 262144 | tf_op jit(solution)/shard_map/all_to_all | solution.py:573
  32.5 1.0 %shard_map.150 = (bf16[16,4,4,16,256]{4,3,2,1,0:T(8,128)(2,1)S(1)}, f32[4,16,128]{2,1,0:T(8,128)S(1)}) custom-call(s32[4]{0:T(128)S(1)} %pad_add_fusion.refs_0_.par_ref, f32[64,32,128]{2,1,0:T(8,128)S(1)} %bitcast.17, f32[32,128]{1,0:T(8,128)S(1)} %get-tuple-element.25.flags_ref, bf16[74,16,128]{2,1,0:T(8,128)(2,1)S(1)} %collective-permute-done.xa_ref, ...), custom_call_target="tpu_custom_call" | custom-call | flops 8388608 | bytes 8388608 | tf_op jit(solution)/shard_map/pallas_call | solution.py:673
  33.5 0.0 collective-permute-done.2.refs_4_.ya_ref
  33.5 0.0 collective-permute-done.3.refs_5_.yb_ref
  33.6 0.0 copy-done.13
  33.6 0.0 copy-start.12
  33.6 1.1 %copy-done.12 = bf16[2,256,640]{2,1,0:T(8,128)(2,1)S(1)} copy-done((bf16[2,256,640]{2,1,0:T(8,128)(2,1)S(1)}, bf16[2,256,640]{2,1,0:T(8,128)(2,1)}, u32[]{:S(2)}) %copy-start.12) | copy-done | bytes 655384
  34.7 20.9 %shard_map.152 = (f32[64,32,128]{2,1,0:T(8,128)}, bf16[128,128]{1,0:T(8,128)(2,1)S(1)}) custom-call(s32[4]{0:T(128)S(1)} %pad_add_fusion.refs_0_.par_ref, f32[128]{0:T(128)S(1)} %pad_maximum_fusion.refs_1_, bf16[16,4,4,16,256]{4,3,2,1,0:T(8,128)(2,1)S(1)} %get-tuple-element.31.refs_2_, f32[4,16,128]{2,1,0:T(8,128)S(1)} %get-tuple-element.32.refs_3_, ...), custom_call_target="tpu_custom_call" | custom-call | flops 8589934592 | bytes 67108864 | tf_op jit(solution)/shard_map/pallas_call | solution.py:610
  55.6 0.0 copy-start.5
  55.6 0.0 copy-start.7
  55.6 0.0 copy-start.9
  55.6 0.0 all-to-all-done
  55.7 0.0 copy-start.3
  55.7 0.2 shard_map.154
  55.8 16.9 %all_to_all.15 = bf16[32,16,128]{2,1,0:T(8,128)(2,1)S(1)} all-to-all(bf16[32,16,128]{2,1,0:T(8,128)(2,1)S(1)} %bitcast.24), channel_id=1, replica_groups=mesh['tile'=32,'comp'=4] {'tile'}, dimensions={0} | all-to-all | bytes 262144 | tf_op jit(solution)/shard_map/all_to_all | solution.py:573
  72.8 0.0 copy-done.2
  72.8 1.3 %shard_map.155 = (f32[8,1024]{1,0:T(8,128)S(1)}, f32[8,128]{1,0:T(8,128)S(1)}, f32[8,128]{1,0:T(8,128)S(1)}) custom-call(s32[4]{0:T(128)S(1)} %pad_add_fusion.refs_0_.par_ref, bf16[512,128]{1,0:T(8,128)(2,1)S(1)} %bitcast.25, s32[512,128]{1,0:T(8,128)S(1)} %get-tuple-element.41.tcol_ref, bf16[8,1024,128]{2,1,0:T(8,128)(2,1)S(1)} %bitcast.18), custom_call_target="tpu_custom_call" | custom-call | tf_op jit(solution)/shard_map/pallas_call | solution.py:700
  74.1 0.1 collective-permute-start.4
  74.2 2.3 %collective-permute-start.5 = (f32[8,128]{1,0:T(8,128)S(1)}, f32[8,128]{1,0:T(8,128)S(1)}, u32[]{:S(2)}, u32[]{:S(2)}) collective-permute-start(f32[8,128]{1,0:T(8,128)S(1)} %get-tuple-element.44), channel_id=1, source_target_pairs={{0,127},{1,2},{2,1},{3,4},{4,3},{5,6},{6,5},{7,8},{8,7},{9,10},{10... | collective-permute-start | bytes 12296 | tf_op jit(solution)/shard_map/ppermute | solution.py:569
  76.5 0.0 copy-done.5
  76.5 0.0 copy-done.7
  76.5 0.0 copy-done.9
  76.5 2.6 %shard_map.153 = (f32[64,1024]{1,0:T(8,128)S(1)}, bf16[8,384,128]{2,1,0:T(8,128)(2,1)S(1)}, f32[8,1024]{1,0:T(8,128)S(1)}) custom-call(s32[4]{0:T(128)S(1)} %pad_add_fusion.refs_0_.par_ref, f32[64,1024]{1,0:T(8,128)S(1)} %bitcast.22, s32[6,1024]{1,0:T(8,128)S(1)} %copy-done.7, f32[6,1024]{1,0:T(8,128)S(1)} %copy-done.9, ...), custom_call_target="tpu_custom_call" | custom-call | flops 134217728 | bytes 16777216 | tf_op jit(solution)/shard_map/pallas_call | solution.py:693
  79.1 0.0 collective-permute-done.4.ea_ref
  79.1 3.6 %collective-permute-done.5.eb_ref = f32[8,128]{1,0:T(8,128)S(1)} collective-permute-done((f32[8,128]{1,0:T(8,128)S(1)}, f32[8,128]{1,0:T(8,128)S(1)}, u32[]{:S(2)}, u32[]{:S(2)}) %collective-permute-start.5) | collective-permute-done | bytes 4128 | tf_op jit(solution)/shard_map/ppermute | solution.py:569
  82.7 0.0 copy-done.3
  82.7 2.8 %shard_map.156 = (f32[64,1024]{1,0:T(8,128)}, bf16[512,128]{1,0:T(8,128)(2,1)S(1)}) custom-call(s32[4]{0:T(128)S(1)} %pad_add_fusion.refs_0_.par_ref, f32[64,1024]{1,0:T(8,128)S(1)} %get-tuple-element.36.n2_ref, bf16[8,384,128]{2,1,0:T(8,128)(2,1)S(1)} %get-tuple-element.37.wm_ref, f32[8,1024]{1,0:T(8,128)S(1)} %get-tuple-element.38.sw_ref, ...), custom_call_target="tpu_custom_call" | custom-call | tf_op jit(solution)/shard_map/pallas_call | solution.py:706
  85.6 11.7 %all_to_all.16 = bf16[32,16,128]{2,1,0:T(8,128)(2,1)S(1)} all-to-all(bf16[32,16,128]{2,1,0:T(8,128)(2,1)S(1)} %bitcast.26), channel_id=1, replica_groups=mesh['tile'=32,'comp'=4] {'tile'}, dimensions={0} | all-to-all | bytes 262144 | tf_op jit(solution)/shard_map/all_to_all | solution.py:573
  97.3 0.9 shard_map.157
  (2 shorter events, 0.0 us)
Async XLA Ops:
  0.6 25.9 %copy-start.14 = (f32[12,4]{0,1:T(4,128)S(1)}, f32[12,4]{0,1:T(4,128)}, u32[]{:S(2)}) copy-start(f32[12,4]{0,1:T(4,128)} %param.16) | copy-start | bytes 580
  0.6 26.1 %copy-start.16 = (f32[2,16]{1,0:T(2,128)S(1)}, f32[2,16]{1,0:T(2,128)}, u32[]{:S(2)}) copy-start(f32[2,16]{1,0:T(2,128)} %param.14) | copy-start | bytes 388
  0.7 26.2 %copy-start.15 = (f32[4,12]{1,0:T(4,128)S(1)}, f32[4,12]{1,0:T(4,128)}, u32[]{:S(2)}) copy-start(f32[4,12]{1,0:T(4,128)} %param.23) | copy-start | bytes 580
  0.8 1.2 %copy-start = (f32[4,16,32,128]{3,2,1,0:T(8,128)S(1)}, f32[4,16,32,128]{3,2,1,0:T(8,128)}, u32[]{:S(2)}) copy-start(f32[4,16,32,128]{3,2,1,0:T(8,128)} %param.13) | copy-start | bytes 3145732
  2.0 0.9 copy-start.4
  2.9 0.8 copy-start.6
  3.7 0.8 copy-start.8
  4.5 0.7 copy-start.10
  5.2 16.9 %copy-start.1 = (f32[4,16,32,128]{3,2,1,0:T(8,128)S(1)}, f32[4,16,32,128]{3,2,1,0:T(8,128)}, u32[]{:S(2)}) copy-start(f32[4,16,32,128]{3,2,1,0:T(8,128)} %param.13) | copy-start | bytes 3145732
  6.0 14.6 %collective-permute-start.1 = (bf16[74,16,128]{2,1,0:T(8,128)(2,1)S(1)}, bf16[74,16,128]{2,1,0:T(8,128)(2,1)S(1)}, u32[]{:S(2)}, u32[]{:S(2)}) collective-permute-start(bf16[74,16,128]{2,1,0:T(8,128)(2,1)S(1)} %get-tuple-element.29.pb_ref), channel_id=1, source_target_pairs={{0,124},{4,8},{8,4},{12,16},{16,12},{20,24},{24,20},{28,32},{32,28... | collective-permute-start | bytes 909320 | tf_op jit(solution)/shard_map/ppermute | solution.py:569
  13.5 8.6 %collective-permute-start = (bf16[74,16,128]{2,1,0:T(8,128)(2,1)S(1)}, bf16[74,16,128]{2,1,0:T(8,128)(2,1)S(1)}, u32[]{:S(2)}, u32[]{:S(2)}) collective-permute-start(bf16[74,16,128]{2,1,0:T(8,128)(2,1)S(1)} %get-tuple-element.26.pa_ref), channel_id=1, source_target_pairs={{0,4},{4,0},{8,12},{12,8},{16,20},{20,16},{24,28},{28,24},{32,36},... | collective-permute-start | bytes 909320 | tf_op jit(solution)/shard_map/ppermute | solution.py:569
  13.5 0.7 copy-start.11
  22.1 11.5 %copy-start.13 = (f32[16,128]{1,0:T(8,128)S(1)}, f32[16,128]{1,0:T(8,128)}, u32[]{:S(2)}) copy-start(f32[16,128]{1,0:T(8,128)} %constant.31.clone.refs_6_) | copy-start | bytes 24580
  23.4 10.1 %collective-permute-start.2 = (bf16[672,128]{1,0:T(8,128)(2,1)S(1)}, bf16[672,128]{1,0:T(8,128)(2,1)S(1)}, u32[]{:S(2)}, u32[]{:S(2)}) collective-permute-start(bf16[672,128]{1,0:T(8,128)(2,1)S(1)} %get-tuple-element.33), channel_id=1, source_target_pairs={{0,1},{1,0},{2,3},{3,2},{4,5},{5,4},{6,7},{7,6},{8,9},{9,8},{10,11... | collective-permute-start | bytes 516104 | tf_op jit(solution)/shard_map/ppermute | solution.py:569
  23.5 10.0 %collective-permute-start.3 = (bf16[672,128]{1,0:T(8,128)(2,1)S(1)}, bf16[672,128]{1,0:T(8,128)(2,1)S(1)}, u32[]{:S(2)}, u32[]{:S(2)}) collective-permute-start(bf16[672,128]{1,0:T(8,128)(2,1)S(1)} %get-tuple-element.34), channel_id=1, source_target_pairs={{0,3},{1,2},{2,1},{3,0},{4,7},{5,6},{6,5},{7,4},{8,11},{9,10},{10,... | collective-permute-start | bytes 516104 | tf_op jit(solution)/shard_map/ppermute | solution.py:569
  27.0 28.7 %all-to-all-start = ((bf16[32,16,128]{2,1,0:T(8,128)(2,1)}), bf16[32,16,128]{2,1,0:T(8,128)(2,1)S(1)}, u32[]{:S(2)}, u32[]{:S(2)}) async-start(bf16[32,16,128]{2,1,0:T(8,128)(2,1)} %bitcast.7), calls=%async_computation | async-start | bytes 262144 | tf_op jit(solution)/shard_map/all_to_all | solution.py:573
  33.6 1.1 %copy-start.12 = (bf16[2,256,640]{2,1,0:T(8,128)(2,1)S(1)}, bf16[2,256,640]{2,1,0:T(8,128)(2,1)}, u32[]{:S(2)}) copy-start(bf16[2,256,640]{2,1,0:T(8,128)(2,1)} %constant.30.clone.refs_7_) | copy-start | bytes 1966084
  34.7 38.1 %copy-start.2 = (bf16[8,8,128,128]{3,2,1,0:T(8,128)(2,1)S(1)}, bf16[8,8,128,128]{3,2,1,0:T(8,128)(2,1)}, u32[]{:S(2)}) copy-start(bf16[8,8,128,128]{3,2,1,0:T(8,128)(2,1)} %param.18) | copy-start | bytes 6291460
  55.6 20.9 %copy-start.5 = (f32[4,16,1024]{2,1,0:T(8,128)S(1)}, f32[4,16,1024]{2,1,0:T(8,128)}, u32[]{:S(2)}) copy-start(f32[4,16,1024]{2,1,0:T(8,128)} %param.20) | copy-start | bytes 786436
  55.6 20.9 %copy-start.7 = (s32[6,1024]{1,0:T(8,128)S(1)}, s32[6,1024]{1,0:T(8,128)}, u32[]{:S(2)}) copy-start(s32[6,1024]{1,0:T(8,128)} %off_ref.1) | copy-start | bytes 73732
  55.6 20.9 %copy-start.9 = (f32[6,1024]{1,0:T(8,128)S(1)}, f32[6,1024]{1,0:T(8,128)}, u32[]{:S(2)}) copy-start(f32[6,1024]{1,0:T(8,128)} %w_ref.1) | copy-start | bytes 73732
  55.7 27.1 %copy-start.3 = (bf16[8,8,128,128]{3,2,1,0:T(8,128)(2,1)S(1)}, bf16[8,8,128,128]{3,2,1,0:T(8,128)(2,1)}, u32[]{:S(2)}) copy-start(bf16[8,8,128,128]{3,2,1,0:T(8,128)(2,1)} %weights_ref.1) | copy-start | bytes 6291460
  74.1 5.0 %collective-permute-start.4 = (f32[8,128]{1,0:T(8,128)S(1)}, f32[8,128]{1,0:T(8,128)S(1)}, u32[]{:S(2)}, u32[]{:S(2)}) collective-permute-start(f32[8,128]{1,0:T(8,128)S(1)} %get-tuple-element.43), channel_id=1, source_target_pairs={{0,1},{1,0},{2,3},{3,2},{4,5},{5,4},{6,7},{7,6},{8,9},{9,8},{10,11... | collective-permute-start | bytes 12296 | tf_op jit(solution)/shard_map/ppermute | solution.py:569
  74.2 8.5 %collective-permute-start.5 = (f32[8,128]{1,0:T(8,128)S(1)}, f32[8,128]{1,0:T(8,128)S(1)}, u32[]{:S(2)}, u32[]{:S(2)}) collective-permute-start(f32[8,128]{1,0:T(8,128)S(1)} %get-tuple-element.44), channel_id=1, source_target_pairs={{0,127},{1,2},{2,1},{3,4},{4,3},{5,6},{6,5},{7,8},{8,7},{9,10},{10... | collective-permute-start | bytes 12296 | tf_op jit(solution)/shard_map/ppermute | solution.py:569

commit v3 on v2

--- a/solution.py
+++ b/solution.py
@@ -18,7 +18,6 @@
 NFLUX = 12
 DT = 0.02
 VMEM = pl.BlockSpec(memory_space=pltpu.VMEM)
-HBM = pl.BlockSpec(memory_space=pltpu.HBM)
 SMEM = pl.BlockSpec(memory_space=pltpu.SMEM)
 X_PLANES = 74
 Y_ROWS = 672
@@ -109,7 +108,9 @@
     return lax.dot_general(a, b, (((0,), (0,)), ((), ())), preferred_element_type=F32)
 
 
-def slots_kernel(src_ref, wanted_ref, tcol_ref):
+def slots_kernel(src_ref, rhs_ref, vec_ref, wanted_ref, tcol_ref, rhs_out_ref, vec_out_ref):
+    rhs_out_ref[...] = rhs_ref[...]
+    vec_out_ref[...] = vec_ref[...]
     s = src_ref[...] >> 2
     tile = (s >> 5).astype(F32)
     row = (s & 31).astype(F32)
@@ -157,9 +158,15 @@
     return one_hot(256, base + jnp.where(n < 16, 15 - n, 159 - n))
 
 
-def x_pack_kernel(
-    par_ref, atm_ref, flags_ref, ocean_ref, off_ref, w_ref, a_ref, b_ref, flags_out_ref
-):
+def edge_rows(ocean, off, w, flags):
+    ends = (0, 128, 768, 896)
+    rows = [ocean[:, c : c + 128] for c in ends]
+    for array in (off, w):
+        rows += [array[:, 0:128].astype(F32), array[:, 896:1024].astype(F32)]
+    return jnp.concatenate(rows + [flags.astype(F32)], axis=0)
+
+
+def x_pack_kernel(par_ref, atm_ref, small_ref, a_ref, b_ref, flags_out_ref):
     even = par_ref[0] == 0
 
     def put(index, right, left):
@@ -167,20 +174,16 @@
         b_ref[index] = jnp.where(even, left, right).astype(BF16)
 
     put(slice(0, 64), atm_ref[:, 16:32, :], atm_ref[:, 0:16, :])
-    flags = flags_ref[...].astype(F32)
+    flags = small_ref[280:312]
     flags_out_ref[...] = flags
     put(64, flags[16:32], flags[0:16])
     for part in range(2):
-        right, left = [
-            ocean_ref[:, c + 128 * part : c + 128 * part + 128].reshape(4, 16, 128) for c in (768, 0)
-        ]
+        left = small_ref[64 * part : 64 * part + 64].reshape(4, 16, 128)
+        right = small_ref[128 + 64 * part : 192 + 64 * part].reshape(4, 16, 128)
         put(slice(65 + 4 * part, 69 + 4 * part), right, left)
-    off = off_ref[...].astype(F32)
     pad = jnp.zeros((2, 128), F32)
-    right, left = [
-        jnp.concatenate([off[:, c : c + 128], pad, w_ref[:, c : c + 128], pad], axis=0)
-        for c in (896, 0)
-    ]
+    left = jnp.concatenate([small_ref[256:262], pad, small_ref[268:274], pad], axis=0)
+    right = jnp.concatenate([small_ref[262:268], pad, small_ref[274:280], pad], axis=0)
     put(73, right, left)
 
 
@@ -193,7 +196,19 @@
 
 
 def y_pack_kernel(
-    par_ref, atm_ref, flags_ref, xa_ref, xb_ref, pa_ref, pb_ref, a_ref, b_ref, lhs_ref, ts_ref
+    par_ref,
+    atm_ref,
+    flags_ref,
+    xa_ref,
+    xb_ref,
+    pa_ref,
+    pb_ref,
+    a_ref,
+    b_ref,
+    cb_ref,
+    flag_ref,
+    lhs_ref,
+    ts_ref,
 ):
     even_t, even_c = par_ref[0] == 0, par_ref[1] == 0
     comp = par_ref[2]
@@ -204,13 +219,17 @@
             rows = x_extended(ts_ref, s, atm_ref[p], xa_ref, xb_ref, p, even_t)
             for i in range(4):
                 lanes = slice(((s % 2) * 4 + i) * 128, ((s % 2) * 4 + i) * 128 + 128)
-                lhs_ref[q * 4 + s // 2, :, lanes] = rows[i].astype(BF16)
+                hi, lo = split_bf16(rows[i])
+                lhs_ref[q * 4 + s // 2, :, lanes] = hi
+                cb_ref[(q % 2) * 8 + s, q // 2, i, :, 0:128] = hi
+                cb_ref[(q % 2) * 8 + s, q // 2, i, :, 128:256] = lo
         return 0
 
     lax.fori_loop(0, 8, group, 0)
     rows = x_extended(ts_ref, 0, flags_ref[...], xa_ref, xb_ref, 64, even_t)
     for i in range(4):
         lhs_ref[32, :, 128 * i : 128 * i + 128] = rows[i].astype(BF16)
+        flag_ref[i] = rows[i]
     lhs_ref[32, :, 512:1024] = jnp.zeros((16, 512), BF16)
     moved = mm(lhs_ref[...].reshape(528, 1024), pack_matrix())
     left, right = moved[:, 0:128], moved[:, 128:256]
@@ -227,25 +246,6 @@
         left = jnp.where(comp == 0, from_right, own_left)
         a_ref[dest] = jnp.where(even_c, right, left).astype(BF16)
         b_ref[dest] = jnp.where(even_c, left, right).astype(BF16)
-
-
-def prepare_kernel(par_ref, atm_ref, flags_ref, xa_ref, xb_ref, cb_ref, flag_ref, ts_ref):
-    even_t = par_ref[0] == 0
-
-    def group(q, _):
-        for s in range(8):
-            p = q * 8 + s
-            rows = x_extended(ts_ref, s, atm_ref[p], xa_ref, xb_ref, p, even_t)
-            for i in range(4):
-                hi, lo = split_bf16(rows[i])
-                cb_ref[(q % 2) * 8 + s, q // 2, i, :, 0:128] = hi
-                cb_ref[(q % 2) * 8 + s, q // 2, i, :, 128:256] = lo
-        return 0
-
-    lax.fori_loop(0, 8, group, 0)
-    rows = x_extended(ts_ref, 0, flags_ref[...], xa_ref, xb_ref, 64, even_t)
-    for i in range(4):
-        flag_ref[i] = rows[i]
 
 
 def x_slopes(a):
@@ -282,7 +282,6 @@
     facc_ref,
     gs_ref,
     first_sem,
-    copies,
 ):
     first_copy = pltpu.make_async_copy(first_ref, cb_ref, first_sem)
     first_copy.start()
@@ -326,8 +325,7 @@
     halo_dt_x = -DT * vec_ref[2:3, :]
     ff = vec_ref[pl.ds(4 + comp, 1), :]
     halo_ff = vec_ref[pl.ds(8 + comp, 1), :]
-    for copy in (first_copy, *copies):
-        copy.wait()
+    first_copy.wait()
 
     def step(si, _):
         which = jnp.minimum(si, 1)
@@ -588,28 +586,6 @@
     )
 
 
-def staged(kernel, out, scalars, resident, arrays, scratch=(), late=0, mib=16, cost=None):
-    n_lead, n = len(scalars) + len(resident), len(arrays)
-    n_out = len(jax.tree.leaves(out))
-
-    def body(*refs):
-        lead_refs, hbm_refs = refs[:n_lead], refs[n_lead : n_lead + n]
-        out_refs = refs[n_lead + n : n_lead + n + n_out]
-        held, (sems, *rest) = refs[-n - 1 - len(scratch) :][:n], refs[-1 - len(scratch) :]
-        copies = [pltpu.make_async_copy(hbm_refs[i], held[i], sems.at[i]) for i in range(n)]
-        for copy in copies:
-            copy.start()
-        for copy in copies[: n - late]:
-            copy.wait()
-        extra = (copies[n - late :],) if late else ()
-        kernel(*lead_refs, *held, *out_refs, *rest, *extra)
-
-    buffers = [pltpu.VMEM(a.shape, a.dtype) for a in arrays]
-    scratch_shapes = buffers + [pltpu.SemaphoreType.DMA((n,))] + list(scratch)
-    specs = [SMEM] * len(scalars) + [VMEM] * len(resident) + [HBM] * n
-    return call(body, out, specs, scratch_shapes, mib, cost)(*scalars, *resident, *arrays)
-
-
 ATM_SCRATCH = (
     pltpu.VMEM((LEVELS, 4, 4, 16, 256), BF16),
     pltpu.VMEM((LEVELS, 4, 4, 16, 128), F32),
@@ -649,45 +625,36 @@
     rhs = jnp.asarray(lane_matrices())
     vec = jnp.asarray(lane_vectors())
 
-    xp_a, xp_b, flags = staged(
+    small = edge_rows(ocean, ocean_neighbors, edge_weights, physics_flags)
+    xp_a, xp_b, flags = call(
         x_pack_kernel,
         (S((X_PLANES, 16, 128), BF16),) * 2 + (S((32, 128), F32),),
-        (par,),
-        (),
-        (atm, physics_flags, ocean, ocean_neighbors, edge_weights),
-        mib=12,
-    )
+        [SMEM] + [VMEM] * 2,
+    )(par, atm, small)
     xa, xb = exchange((xp_a, xp_b), "tile", N_TILE)
-    wanted, tcol = call(slots_kernel, (S((512, 128), BF16), S((512, 128), I32)), [VMEM])(
-        regrid_source
-    )
-    wanted, tcol, xb = lax.optimization_barrier((wanted, tcol, xb))
+    wanted, tcol, rhs, vec = call(
+        slots_kernel,
+        (S((512, 128), BF16), S((512, 128), I32), S(rhs.shape, BF16), S(vec.shape, F32)),
+        [VMEM] * 3,
+    )(regrid_source, rhs, vec)
+    wanted, tcol, rhs, vec, xb = lax.optimization_barrier((wanted, tcol, rhs, vec, xb))
     served = to_tiles(wanted)
-    y_payload = call(
+    *y_payload, first, flag = call(
         y_pack_kernel,
-        (S((Y_ROWS, 128), BF16),) * 2,
+        (S((Y_ROWS, 128), BF16),) * 2
+        + (S((LEVELS, 4, 4, 16, 256), BF16), S((4, 16, 128), F32)),
         [SMEM] + [VMEM] * 6,
         [pltpu.VMEM((33, 16, 1024), BF16), pltpu.VMEM((8, 64, 128), F32)],
     )(par, atm, flags, xa, xb, xp_a, xp_b)
     ya, yb = exchange(y_payload, "comp", N_COMP)
-    first, flag = call(
-        prepare_kernel,
-        (S((LEVELS, 4, 4, 16, 256), BF16), S((4, 16, 128), F32)),
-        [SMEM] + [VMEM] * 4,
-        [pltpu.VMEM((8, 64, 128), F32)],
-        cost=pl.CostEstimate(flops=2**23, bytes_accessed=2**23, transcendentals=0),
-    )(par, atm, flags, xa, xb)
-    atm_final, table = staged(
+    atm_final, table = call(
         atm_kernel,
         (S((64, 32, 128), F32), S((128, 128), BF16)),
-        (par, scal),
-        (first, flag, ya, yb),
-        (vec, rhs),
+        [SMEM] * 2 + [VMEM] * 6,
         ATM_SCRATCH,
-        late=1,
         mib=32,
         cost=pl.CostEstimate(flops=2**33, bytes_accessed=2**26, transcendentals=0),
-    )
+    )(par, scal, first, flag, ya, yb, vec, rhs)
     rows = call(pick_kernel, S((512, 128), BF16), [VMEM] * 2)(served, table)
     mean_rows = to_tiles(rows)
     n2, wm, sw = call(

time: 98.7 us -> 99.6 us (level)
  local copies, waits for them, and re-layouts: 6.57 us -> 8.81 us
  Pallas kernels: 32.9 us -> 30.9 us
  other arithmetic: 0.15 us -> 1.58 us
    pallas_call x5 -> x4, Pallas kernels: 25.1 us -> 23.2 us  [the longest x1 19.9 us: per_device(): call(atm_kernel, (S((64, 32, 128), F32), S((128, 128), BF16)), [SMEM] * 2...]
    slice x0 -> x2, local copies, waits for them, and re-layouts: none -> 1.59 us  [the longest x1 0.88 us: edge_rows(): rows = [ocean[:, c:c + 128] for c in ends]]
    convert_element_type x0 -> x2, other arithmetic: none -> 1.42 us  [the longest x1 0.72 us: edge_rows(): return jnp.concatenate(rows + [flags.astype(F32)], axis=0)]
  transfers between devices with their start and end apart: 7 -> 7, of which waited for: 3 -> 3; matrix products, arithmetic and copies ran while one was open for 0% -> 0% of each run, Pallas kernels for 26% -> 24%
where the time goes in v3:
time: 99.6 us; the launch traced here: 99 us
  Pallas kernels  30.9 us (31%)
  blocking collectives  28.7 us (29%)
  starting transfers between devices  18.4 us (18%)
  waiting for transfers between devices  9.77 us (10%)
  local copies, waits for them, and re-layouts  8.81 us (9%)
  other arithmetic  1.58 us (2%)
    all_to_all x2, blocking collectives, to_tiles(): lax.all_to_all(rows.reshape(N_TILE, 16, 128), 'tile', split_axis=0, conca...  28.7 us
    pallas_call x1, Pallas kernels, per_device(): call(atm_kernel, (S((64, 32, 128), F32), S((128, 128), BF16)), [SMEM] * 2...  19.9 us
    ppermute x3, starting transfers between devices, exchange(): lax.ppermute(payloads[1], axis, far)  12.7 us
    ppermute x3, waiting for transfers between devices, exchange(): lax.ppermute(payloads[1], axis, far)  8.3 us
    unnamed x35, local copies, waits for them, and re-layouts  6.77 us
    all_to_all x1, starting transfers between devices, to_tiles(): lax.all_to_all(rows.reshape(N_TILE, 16, 128), 'tile', split_axis=0, conca...  5.57 us
    pallas_call x1, Pallas kernels, per_device(): call(return_kernel, (S((64, 1024), F32), S((512, 128), BF16)), [SMEM] + [...  2.81 us
    pallas_call x1, Pallas kernels, per_device(): call(ocean_kernel, (S((64, 1024), F32), S((8, 384, 128), BF16), S((8, 102...  2.6 us
  transfers between devices with their start and end apart: 7, of which 3 were waited for; matrix products, arithmetic and copies ran while one was open for 0% of the time, Pallas kernels for 24%

profile of v3, /device:TPU:0, one launch (start us, length us, event | category | flops | bytes accessed | tf_op | source)
XLA Modules:
  0.0 99.0 jit_solution(11356320230734080879)
XLA Ops:
  0.6 0.0 copy-start.4
  0.7 0.9 fusion
  1.5 0.7 fusion.1
  2.3 0.7 slice_convert_fusion
  3.0 0.7 convert_element_type.11
  3.7 0.1 pad_add_fusion.par_ref
  3.8 0.2 concatenate.7.small_ref
  4.0 0.0 copy-start.16
  4.0 0.0 copy-start
  4.0 1.2 %copy-done = f32[4,16,32,128]{3,2,1,0:T(8,128)S(1)} copy-done((f32[4,16,32,128]{3,2,1,0:T(8,128)S(1)}, f32[4,16,32,128]{3,2,1,0:T(8,128)}, u32[]{:S(2)}) %copy-start) | copy-done | bytes 1048600
  5.2 0.0 copy-start.1
  5.2 0.0 copy-start.14
  5.2 0.6 shard_map.148
  5.9 7.4 %collective-permute-start.1 = (bf16[74,16,128]{2,1,0:T(8,128)(2,1)S(1)}, bf16[74,16,128]{2,1,0:T(8,128)(2,1)S(1)}, u32[]{:S(2)}, u32[]{:S(2)}) collective-permute-start(bf16[74,16,128]{2,1,0:T(8,128)(2,1)S(1)} %get-tuple-element.35.pb_ref), channel_id=1, source_target_pairs={{0,124},{4,8},{8,4},{12,16},{16,12},{20,24},{24,20},{28,32},{32,28... | collective-permute-start | bytes 909320 | tf_op jit(solution)/shard_map/ppermute | solution.py:567
  13.3 0.0 collective-permute-start
  13.3 0.0 copy-done.4
  13.3 0.7 copy-done.8
  14.0 0.7 copy-done.9
  14.7 1.1 %shard_map.149 = (bf16[512,128]{1,0:T(8,128)(2,1)}, s32[512,128]{1,0:T(8,128)S(1)}, bf16[2,256,640]{2,1,0:T(8,128)(2,1)S(1)}, f32[16,128]{1,0:T(8,128)S(1)}) custom-call(s32[8,8]{1,0:T(8,128)S(1)} %copy-done.9, bf16[2,256,640]{2,1,0:T(8,128)(2,1)S(1)} %copy-done.4, f32[16,128]{1,0:T(8,128)S(1)} %copy-done.8), custom_call_target="tpu_custom_call" | custom-call | tf_op jit(solution)/shard_map/pallas_call | solution.py:635
  15.7 4.7 %collective-permute-done.1.xb_ref = bf16[74,16,128]{2,1,0:T(8,128)(2,1)S(1)} collective-permute-done((bf16[74,16,128]{2,1,0:T(8,128)(2,1)S(1)}, bf16[74,16,128]{2,1,0:T(8,128)(2,1)S(1)}, u32[]{:S(2)}, u32[]{:S(2)}) %collective-permute-start.1) | collective-permute-done | bytes 303136 | tf_op jit(solution)/shard_map/ppermute | solution.py:567
  20.4 1.5 %collective-permute-done.xa_ref = bf16[74,16,128]{2,1,0:T(8,128)(2,1)S(1)} collective-permute-done((bf16[74,16,128]{2,1,0:T(8,128)(2,1)S(1)}, bf16[74,16,128]{2,1,0:T(8,128)(2,1)S(1)}, u32[]{:S(2)}, u32[]{:S(2)}) %collective-permute-start) | collective-permute-done | bytes 303136 | tf_op jit(solution)/shard_map/ppermute | solution.py:567
  21.9 0.0 copy-done.1
  21.9 1.6 %shard_map.150 = (bf16[672,128]{1,0:T(8,128)(2,1)S(1)}, bf16[672,128]{1,0:T(8,128)(2,1)S(1)}, bf16[16,4,4,16,256]{4,3,2,1,0:T(8,128)(2,1)S(1)}, f32[4,16,128]{2,1,0:T(8,128)S(1)}) custom-call(s32[4]{0:T(128)S(1)} %pad_add_fusion.par_ref, f32[64,32,128]{2,1,0:T(8,128)S(1)} %bitcast.16, f32[32,128]{1,0:T(8,128)S(1)} %get-tuple-element.29.flags_ref, ...), custom_call_target="tpu_custom_call" | custom-call | tf_op jit(solution)/shard_map/pallas_call | solution.py:642
  23.5 0.0 copy-done.12
  23.5 0.0 copy-start.10
  23.5 1.3 %copy-done.10 = bf16[16,4,4,16,256]{4,3,2,1,0:T(8,128)(2,1)} copy-done((bf16[16,4,4,16,256]{4,3,2,1,0:T(8,128)(2,1)}, bf16[16,4,4,16,256]{4,3,2,1,0:T(8,128)(2,1)S(1)}, u32[]{:S(2)}) %copy-start.10) | copy-done | bytes 2097176
  24.8 0.0 collective-permute-start.2
  24.8 3.0 %collective-permute-start.3 = (bf16[672,128]{1,0:T(8,128)(2,1)S(1)}, bf16[672,128]{1,0:T(8,128)(2,1)S(1)}, u32[]{:S(2)}, u32[]{:S(2)}) collective-permute-start(bf16[672,128]{1,0:T(8,128)(2,1)S(1)} %get-tuple-element.40), channel_id=1, source_target_pairs={{0,3},{1,2},{2,1},{3,0},{4,7},{5,6},{6,5},{7,4},{8,11},{9,10},{10,... | collective-permute-start | bytes 516104 | tf_op jit(solution)/shard_map/ppermute | solution.py:567
  27.9 0.0 copy-done.14
  27.9 0.1 copy.17
  28.0 0.1 reshape.49
  28.0 0.0 copy-done.16
  28.1 0.1 reshape.48
  28.1 0.0 copy-done.15
  28.1 0.1 reshape.50
  28.2 0.1 pad_maximum_fusion.scal_ref
  28.3 5.6 %all-to-all-start = ((bf16[32,16,128]{2,1,0:T(8,128)(2,1)}), bf16[32,16,128]{2,1,0:T(8,128)(2,1)S(1)}, u32[]{:S(2)}, u32[]{:S(2)}) async-start(bf16[32,16,128]{2,1,0:T(8,128)(2,1)} %bitcast.7), calls=%async_computation | async-start | bytes 262144 | tf_op jit(solution)/shard_map/all_to_all | solution.py:571
  33.9 0.0 collective-permute-done.2.ya_ref
  33.9 0.0 collective-permute-done.3.yb_ref
  33.9 0.0 copy-start.11
  33.9 1.6 %copy-done.11 = bf16[16,4,4,16,256]{4,3,2,1,0:T(8,128)(2,1)S(1)} copy-done((bf16[16,4,4,16,256]{4,3,2,1,0:T(8,128)(2,1)S(1)}, bf16[16,4,4,16,256]{4,3,2,1,0:T(8,128)(2,1)}, u32[]{:S(2)}) %copy-start.11) | copy-done | bytes 2097176
  35.5 1.1 %copy-done.13 = bf16[2,256,640]{2,1,0:T(8,128)(2,1)S(1)} copy-done((bf16[2,256,640]{2,1,0:T(8,128)(2,1)S(1)}, bf16[2,256,640]{2,1,0:T(8,128)(2,1)}, u32[]{:S(2)}) %copy-start.13) | copy-done | bytes 655384
  36.6 19.9 %shard_map.151 = (f32[64,32,128]{2,1,0:T(8,128)}, bf16[128,128]{1,0:T(8,128)(2,1)S(1)}) custom-call(s32[4]{0:T(128)S(1)} %pad_add_fusion.par_ref, f32[128]{0:T(128)S(1)} %pad_maximum_fusion.scal_ref, bf16[16,4,4,16,256]{4,3,2,1,0:T(8,128)(2,1)S(1)} %copy-done.11, f32[4,16,128]{2,1,0:T(8,128)S(1)} %get-tuple-element.38.flag_ref, ...), custom_call_target="tpu_custom_call" | custom-call | flops 8589934592 | bytes 67108864 | tf_op jit(solution)/shard_map/pallas_call | solution.py:650
  56.4 0.0 copy-start.5
  56.5 0.0 copy-start.6
  56.5 0.0 copy-start.7
  56.5 0.0 all-to-all-done
  56.5 0.0 copy-start.3
  56.5 0.2 shard_map.153
  56.7 17.0 %all_to_all.15 = bf16[32,16,128]{2,1,0:T(8,128)(2,1)S(1)} all-to-all(bf16[32,16,128]{2,1,0:T(8,128)(2,1)S(1)} %bitcast.23), channel_id=1, replica_groups=mesh['tile'=32,'comp'=4] {'tile'}, dimensions={0} | all-to-all | bytes 262144 | tf_op jit(solution)/shard_map/all_to_all | solution.py:571
  73.7 0.0 copy-done.2
  73.7 1.3 %shard_map.154 = (f32[8,1024]{1,0:T(8,128)S(1)}, f32[8,128]{1,0:T(8,128)S(1)}, f32[8,128]{1,0:T(8,128)S(1)}) custom-call(s32[4]{0:T(128)S(1)} %pad_add_fusion.par_ref, bf16[512,128]{1,0:T(8,128)(2,1)S(1)} %bitcast.24, s32[512,128]{1,0:T(8,128)S(1)} %get-tuple-element.49.tcol_ref, bf16[8,1024,128]{2,1,0:T(8,128)(2,1)S(1)} %bitcast.17), custom_call_target="tpu_custom_call" | custom-call | tf_op jit(solution)/shard_map/pallas_call | solution.py:667
  75.0 0.1 collective-permute-start.4
  75.1 2.3 %collective-permute-start.5 = (f32[8,128]{1,0:T(8,128)S(1)}, f32[8,128]{1,0:T(8,128)S(1)}, u32[]{:S(2)}, u32[]{:S(2)}) collective-permute-start(f32[8,128]{1,0:T(8,128)S(1)} %get-tuple-element.52), channel_id=1, source_target_pairs={{0,127},{1,2},{2,1},{3,4},{4,3},{5,6},{6,5},{7,8},{8,7},{9,10},{10... | collective-permute-start | bytes 12296 | tf_op jit(solution)/shard_map/ppermute | solution.py:567
  77.4 0.0 copy-done.5
  77.4 0.0 copy-done.6
  77.4 0.0 copy-done.7
  77.4 2.6 %shard_map.152 = (f32[64,1024]{1,0:T(8,128)S(1)}, bf16[8,384,128]{2,1,0:T(8,128)(2,1)S(1)}, f32[8,1024]{1,0:T(8,128)S(1)}) custom-call(s32[4]{0:T(128)S(1)} %pad_add_fusion.par_ref, f32[64,1024]{1,0:T(8,128)S(1)} %bitcast.21, s32[6,1024]{1,0:T(8,128)S(1)} %copy-done.6, f32[6,1024]{1,0:T(8,128)S(1)} %copy-done.7, ...), custom_call_target="tpu_custom_call" | custom-call | flops 134217728 | bytes 16777216 | tf_op jit(solution)/shard_map/pallas_call | solution.py:660
  80.0 0.0 collective-permute-done.4.ea_ref
  80.0 3.6 %collective-permute-done.5.eb_ref = f32[8,128]{1,0:T(8,128)S(1)} collective-permute-done((f32[8,128]{1,0:T(8,128)S(1)}, f32[8,128]{1,0:T(8,128)S(1)}, u32[]{:S(2)}, u32[]{:S(2)}) %collective-permute-start.5) | collective-permute-done | bytes 4128 | tf_op jit(solution)/shard_map/ppermute | solution.py:567
  83.6 0.0 copy-done.3
  83.6 2.8 %shard_map.155 = (f32[64,1024]{1,0:T(8,128)}, bf16[512,128]{1,0:T(8,128)(2,1)S(1)}) custom-call(s32[4]{0:T(128)S(1)} %pad_add_fusion.par_ref, f32[64,1024]{1,0:T(8,128)S(1)} %get-tuple-element.44.n2_ref, bf16[8,384,128]{2,1,0:T(8,128)(2,1)S(1)} %get-tuple-element.45.wm_ref, f32[8,1024]{1,0:T(8,128)S(1)} %get-tuple-element.46.sw_ref, ...), custom_call_target="tpu_custom_call" | custom-call | tf_op jit(solution)/shard_map/pallas_call | solution.py:673
  86.4 11.7 %all_to_all.16 = bf16[32,16,128]{2,1,0:T(8,128)(2,1)S(1)} all-to-all(bf16[32,16,128]{2,1,0:T(8,128)(2,1)S(1)} %bitcast.25), channel_id=1, replica_groups=mesh['tile'=32,'comp'=4] {'tile'}, dimensions={0} | all-to-all | bytes 262144 | tf_op jit(solution)/shard_map/all_to_all | solution.py:571
  98.1 0.9 shard_map.156
  (6 shorter events, 0.0 us)
Async XLA Ops:
  0.6 12.6 %copy-start.4 = (bf16[2,256,640]{2,1,0:T(8,128)(2,1)S(1)}, bf16[2,256,640]{2,1,0:T(8,128)(2,1)}, u32[]{:S(2)}) copy-start(bf16[2,256,640]{2,1,0:T(8,128)(2,1)} %constant.30.clone.rhs_ref) | copy-start | bytes 1966084
  4.0 24.1 %copy-start.16 = (f32[2,16]{1,0:T(2,128)S(1)}, f32[2,16]{1,0:T(2,128)}, u32[]{:S(2)}) copy-start(f32[2,16]{1,0:T(2,128)} %param.14) | copy-start | bytes 388
  4.0 1.2 %copy-start = (f32[4,16,32,128]{3,2,1,0:T(8,128)S(1)}, f32[4,16,32,128]{3,2,1,0:T(8,128)}, u32[]{:S(2)}) copy-start(f32[4,16,32,128]{3,2,1,0:T(8,128)} %param.13) | copy-start | bytes 3145732
  5.2 16.7 %copy-start.1 = (f32[4,16,32,128]{3,2,1,0:T(8,128)S(1)}, f32[4,16,32,128]{3,2,1,0:T(8,128)}, u32[]{:S(2)}) copy-start(f32[4,16,32,128]{3,2,1,0:T(8,128)} %param.13) | copy-start | bytes 3145732
  5.2 22.7 %copy-start.14 = (f32[12,4]{0,1:T(4,128)S(1)}, f32[12,4]{0,1:T(4,128)}, u32[]{:S(2)}) copy-start(f32[12,4]{0,1:T(4,128)} %param.16) | copy-start | bytes 580
  5.2 22.9 %copy-start.15 = (f32[4,12]{1,0:T(4,128)S(1)}, f32[4,12]{1,0:T(4,128)}, u32[]{:S(2)}) copy-start(f32[4,12]{1,0:T(4,128)} %param.23) | copy-start | bytes 580
  5.9 14.6 %collective-permute-start.1 = (bf16[74,16,128]{2,1,0:T(8,128)(2,1)S(1)}, bf16[74,16,128]{2,1,0:T(8,128)(2,1)S(1)}, u32[]{:S(2)}, u32[]{:S(2)}) collective-permute-start(bf16[74,16,128]{2,1,0:T(8,128)(2,1)S(1)} %get-tuple-element.35.pb_ref), channel_id=1, source_target_pairs={{0,124},{4,8},{8,4},{12,16},{16,12},{20,24},{24,20},{28,32},{32,28... | collective-permute-start | bytes 909320 | tf_op jit(solution)/shard_map/ppermute | solution.py:567
  13.3 8.6 %collective-permute-start = (bf16[74,16,128]{2,1,0:T(8,128)(2,1)S(1)}, bf16[74,16,128]{2,1,0:T(8,128)(2,1)S(1)}, u32[]{:S(2)}, u32[]{:S(2)}) collective-permute-start(bf16[74,16,128]{2,1,0:T(8,128)(2,1)S(1)} %get-tuple-element.30.pa_ref), channel_id=1, source_target_pairs={{0,4},{4,0},{8,12},{12,8},{16,20},{20,16},{24,28},{28,24},{32,36},... | collective-permute-start | bytes 909320 | tf_op jit(solution)/shard_map/ppermute | solution.py:567
  13.3 0.7 copy-start.8
  14.0 0.7 copy-start.9
  15.7 7.7 %copy-start.12 = (bf16[2,256,640]{2,1,0:T(8,128)(2,1)}, bf16[2,256,640]{2,1,0:T(8,128)(2,1)S(1)}, u32[]{:S(2)}) copy-start(bf16[2,256,640]{2,1,0:T(8,128)(2,1)S(1)} %get-tuple-element.42.rhs_ref) | copy-start | bytes 1966084
  23.5 1.4 %copy-start.10 = (bf16[16,4,4,16,256]{4,3,2,1,0:T(8,128)(2,1)}, bf16[16,4,4,16,256]{4,3,2,1,0:T(8,128)(2,1)S(1)}, u32[]{:S(2)}) copy-start(bf16[16,4,4,16,256]{4,3,2,1,0:T(8,128)(2,1)S(1)} %get-tuple-element.37.first_ref) | copy-start | bytes 6291460
  24.8 9.0 %collective-permute-start.2 = (bf16[672,128]{1,0:T(8,128)(2,1)S(1)}, bf16[672,128]{1,0:T(8,128)(2,1)S(1)}, u32[]{:S(2)}, u32[]{:S(2)}) collective-permute-start(bf16[672,128]{1,0:T(8,128)(2,1)S(1)} %get-tuple-element.39), channel_id=1, source_target_pairs={{0,1},{1,0},{2,3},{3,2},{4,5},{5,4},{6,7},{7,6},{8,9},{9,8},{10,11... | collective-permute-start | bytes 516104 | tf_op jit(solution)/shard_map/ppermute | solution.py:567
  24.8 9.0 %collective-permute-start.3 = (bf16[672,128]{1,0:T(8,128)(2,1)S(1)}, bf16[672,128]{1,0:T(8,128)(2,1)S(1)}, u32[]{:S(2)}, u32[]{:S(2)}) collective-permute-start(bf16[672,128]{1,0:T(8,128)(2,1)S(1)} %get-tuple-element.40), channel_id=1, source_target_pairs={{0,3},{1,2},{2,1},{3,0},{4,7},{5,6},{6,5},{7,4},{8,11},{9,10},{10,... | collective-permute-start | bytes 516104 | tf_op jit(solution)/shard_map/ppermute | solution.py:567
  28.3 28.2 %all-to-all-start = ((bf16[32,16,128]{2,1,0:T(8,128)(2,1)}), bf16[32,16,128]{2,1,0:T(8,128)(2,1)S(1)}, u32[]{:S(2)}, u32[]{:S(2)}) async-start(bf16[32,16,128]{2,1,0:T(8,128)(2,1)} %bitcast.7), calls=%async_computation | async-start | bytes 262144 | tf_op jit(solution)/shard_map/all_to_all | solution.py:571
  33.9 1.6 %copy-start.11 = (bf16[16,4,4,16,256]{4,3,2,1,0:T(8,128)(2,1)S(1)}, bf16[16,4,4,16,256]{4,3,2,1,0:T(8,128)(2,1)}, u32[]{:S(2)}) copy-start(bf16[16,4,4,16,256]{4,3,2,1,0:T(8,128)(2,1)} %copy-done.10) | copy-start | bytes 6291460
  35.5 1.1 %copy-start.13 = (bf16[2,256,640]{2,1,0:T(8,128)(2,1)S(1)}, bf16[2,256,640]{2,1,0:T(8,128)(2,1)}, u32[]{:S(2)}) copy-start(bf16[2,256,640]{2,1,0:T(8,128)(2,1)} %copy-done.12) | copy-start | bytes 1966084
  36.6 37.1 %copy-start.2 = (bf16[8,8,128,128]{3,2,1,0:T(8,128)(2,1)S(1)}, bf16[8,8,128,128]{3,2,1,0:T(8,128)(2,1)}, u32[]{:S(2)}) copy-start(bf16[8,8,128,128]{3,2,1,0:T(8,128)(2,1)} %param.18) | copy-start | bytes 6291460
  56.4 20.9 %copy-start.5 = (f32[4,16,1024]{2,1,0:T(8,128)S(1)}, f32[4,16,1024]{2,1,0:T(8,128)}, u32[]{:S(2)}) copy-start(f32[4,16,1024]{2,1,0:T(8,128)} %param.20) | copy-start | bytes 786436
  56.5 20.9 %copy-start.6 = (s32[6,1024]{1,0:T(8,128)S(1)}, s32[6,1024]{1,0:T(8,128)}, u32[]{:S(2)}) copy-start(s32[6,1024]{1,0:T(8,128)} %off_ref.1) | copy-start | bytes 73732
  56.5 20.9 %copy-start.7 = (f32[6,1024]{1,0:T(8,128)S(1)}, f32[6,1024]{1,0:T(8,128)}, u32[]{:S(2)}) copy-start(f32[6,1024]{1,0:T(8,128)} %w_ref.1) | copy-start | bytes 73732
  56.5 27.1 %copy-start.3 = (bf16[8,8,128,128]{3,2,1,0:T(8,128)(2,1)S(1)}, bf16[8,8,128,128]{3,2,1,0:T(8,128)(2,1)}, u32[]{:S(2)}) copy-start(bf16[8,8,128,128]{3,2,1,0:T(8,128)(2,1)} %weights_ref.1) | copy-start | bytes 6291460
  75.0 5.0 %collective-permute-start.4 = (f32[8,128]{1,0:T(8,128)S(1)}, f32[8,128]{1,0:T(8,128)S(1)}, u32[]{:S(2)}, u32[]{:S(2)}) collective-permute-start(f32[8,128]{1,0:T(8,128)S(1)} %get-tuple-element.51), channel_id=1, source_target_pairs={{0,1},{1,0},{2,3},{3,2},{4,5},{5,4},{6,7},{7,6},{8,9},{9,8},{10,11... | collective-permute-start | bytes 12296 | tf_op jit(solution)/shard_map/ppermute | solution.py:567
  75.1 8.5 %collective-permute-start.5 = (f32[8,128]{1,0:T(8,128)S(1)}, f32[8,128]{1,0:T(8,128)S(1)}, u32[]{:S(2)}, u32[]{:S(2)}) collective-permute-start(f32[8,128]{1,0:T(8,128)S(1)} %get-tuple-element.52), channel_id=1, source_target_pairs={{0,127},{1,2},{2,1},{3,4},{4,3},{5,6},{6,5},{7,8},{8,7},{9,10},{10... | collective-permute-start | bytes 12296 | tf_op jit(solution)/shard_map/ppermute | solution.py:567

commit v4 on v2

--- a/solution.py
+++ b/solution.py
@@ -229,25 +229,6 @@
         b_ref[dest] = jnp.where(even_c, left, right).astype(BF16)
 
 
-def prepare_kernel(par_ref, atm_ref, flags_ref, xa_ref, xb_ref, cb_ref, flag_ref, ts_ref):
-    even_t = par_ref[0] == 0
-
-    def group(q, _):
-        for s in range(8):
-            p = q * 8 + s
-            rows = x_extended(ts_ref, s, atm_ref[p], xa_ref, xb_ref, p, even_t)
-            for i in range(4):
-                hi, lo = split_bf16(rows[i])
-                cb_ref[(q % 2) * 8 + s, q // 2, i, :, 0:128] = hi
-                cb_ref[(q % 2) * 8 + s, q // 2, i, :, 128:256] = lo
-        return 0
-
-    lax.fori_loop(0, 8, group, 0)
-    rows = x_extended(ts_ref, 0, flags_ref[...], xa_ref, xb_ref, 64, even_t)
-    for i in range(4):
-        flag_ref[i] = rows[i]
-
-
 def x_slopes(a):
     sums, diffs = (a[0] + a[3], a[1] + a[2]), (a[0] - a[3], a[1] - a[2])
     across = sums[0] - sums[1]
@@ -263,8 +244,10 @@
 def atm_kernel(
     par_ref,
     scal_ref,
-    first_ref,
-    flag_ref,
+    atm_ref,
+    flags_ref,
+    xa_ref,
+    xb_ref,
     ya_ref,
     yb_ref,
     vec_ref,
@@ -281,11 +264,10 @@
     r5_ref,
     facc_ref,
     gs_ref,
-    first_sem,
+    ts_ref,
     copies,
 ):
-    first_copy = pltpu.make_async_copy(first_ref, cb_ref, first_sem)
-    first_copy.start()
+    even_t = par_ref[0] == 0
     even_c = par_ref[1] == 0
     comp = par_ref[2]
     lane = iota((16, 128), 1)
@@ -313,8 +295,19 @@
     halo_m5 = jnp.where(halo_flag == 2.0, 5.0 * DT, 0.0)
     halo_keep = 1.0 - 2.0 * halo_m5
     halo_keep_t = halo_keep - halo_r5
+
+    def prepare(q, _):
+        for s in range(8):
+            p = q * 8 + s
+            rows = x_extended(ts_ref, s, atm_ref[p], xa_ref, xb_ref, p, even_t)
+            for i in range(4):
+                put(cb_ref, ((q % 2) * 8 + s, q // 2, i), rows[i])
+        return 0
+
+    lax.fori_loop(0, 8, prepare, 0)
+    flag_rows = x_extended(ts_ref, 0, flags_ref[...], xa_ref, xb_ref, 64, even_t)
     for i in range(4):
-        flag = flag_ref[i]
+        flag = flag_rows[i]
         m5 = jnp.where(flag == 2.0, 5.0 * DT, 0.0)
         r5_ref[i] = jnp.where(flag == 1.0, 5.0 * DT, 0.0)
         mask_ref[0, i] = m5
@@ -326,7 +319,7 @@
     halo_dt_x = -DT * vec_ref[2:3, :]
     ff = vec_ref[pl.ds(4 + comp, 1), :]
     halo_ff = vec_ref[pl.ds(8 + comp, 1), :]
-    for copy in (first_copy, *copies):
+    for copy in copies:
         copy.wait()
 
     def step(si, _):
@@ -432,7 +425,59 @@
     rows_ref[...] = mm(jnp.where(pick, 1.0, 0.0).astype(BF16), table_ref[...]).astype(BF16)
 
 
-def ocean_kernel(par_ref, ocean_ref, off_ref, w_ref, ya_ref, yb_ref, n2_ref, wm_ref, sw_ref, o1_ref):
+def request_matrix(tcol_ref):
+    parts = []
+    for chunk in range(4):
+        hit = tcol_ref[...] == iota((512, 128), 1) + 128 * chunk
+        parts.append(jnp.where(hit, 1.0, 0.0).astype(BF16))
+    return jnp.concatenate(parts, axis=1)
+
+
+def force_block(window, wm, sw, n2_ref, ocean_ref, b):
+    cells = slice(128 * b, 128 * b + 128)
+    hi, lo = split_bf16(window)
+    own = window[:, 128:256]
+    both = mm(jnp.concatenate([hi.astype(F32), lo.astype(F32)], axis=0).astype(BF16), wm)
+    top = both[0:8] + both[8:16] + (1.8 - sw) * own
+    surface = []
+    for k in range(4):
+        value = n2_ref[16 * k : 16 * k + 1, cells] + top[k : k + 1]
+        if k == 2:
+            value = value + 0.2 * own[3:4]
+        if k == 3:
+            value = value - 0.2 * own[2:3]
+        below = n2_ref[16 * k + 1 : 16 * k + 2, cells] + 0.2 * own[k : k + 1]
+        ocean_ref[16 * k : 16 * k + 1, cells] = value
+        ocean_ref[16 * k + 1 : 16 * k + 2, cells] = below
+        surface.append(value)
+    return jnp.concatenate(surface + [jnp.zeros((4, 128), F32)], axis=0).astype(BF16)
+
+
+def return_parts(surface, weights, parts_ref, b):
+    parts = mm(surface, jnp.concatenate([weights[k] for k in range(8)], axis=1))
+    for k in range(8):
+        rows = slice((b * 8 + k) * 8, (b * 8 + k) * 8 + 8)
+        parts_ref[rows, :] = parts[:, 128 * k : 128 * k + 128]
+
+
+def ocean_kernel(
+    par_ref,
+    ocean_ref,
+    off_ref,
+    w_ref,
+    ya_ref,
+    yb_ref,
+    f_ref,
+    weights_ref,
+    tcol_ref,
+    n2_ref,
+    ends_ref,
+    sw_ref,
+    parts_ref,
+    table_ref,
+    o1_ref,
+    wm_ref,
+):
     even_c = par_ref[1] == 0
 
     def halo_rows(n):
@@ -482,14 +527,16 @@
         window = jnp.concatenate([o1_ref[b], o1_ref[b + 1], o1_ref[b + 2]], axis=1)
         cells = slice(128 * b, 128 * b + 128)
         n2_ref[:, cells] = update(o1_ref[b + 1], window, wm_ref[b], sw_ref[0:1, cells])
-
-
-def request_matrix(tcol_ref):
-    parts = []
-    for chunk in range(4):
-        hit = tcol_ref[...] == iota((512, 128), 1) + 128 * chunk
-        parts.append(jnp.where(hit, 1.0, 0.0).astype(BF16))
-    return jnp.concatenate(parts, axis=1)
+    for b in range(1, 7):
+        cells = slice(128 * b, 128 * b + 128)
+        window = f_ref[:, 128 * b - 128 : 128 * b + 256]
+        surface = force_block(window, wm_ref[b], sw_ref[:, cells], n2_ref, n2_ref, b)
+        return_parts(surface, weights_ref[b], parts_ref, b)
+    ends_ref[0] = wm_ref[0]
+    ends_ref[1] = wm_ref[7]
+    for b in (0, 7):
+        parts_ref[64 * b : 64 * b + 64, :] = jnp.zeros((64, 128), F32)
+    table_ref[...] = request_matrix(tcol_ref)
 
 
 def forcing_kernel(par_ref, rows_ref, tcol_ref, weights_ref, f_ref, a_ref, b_ref):
@@ -508,48 +555,30 @@
 def return_kernel(
     par_ref,
     n2_ref,
-    wm_ref,
+    ends_ref,
     sw_ref,
     f_ref,
     ea_ref,
     eb_ref,
-    tcol_ref,
-    weights_ref,
+    inner_ref,
+    table_ref,
+    first_ref,
+    last_ref,
     ocean_ref,
     sent_ref,
     parts_ref,
 ):
     even_c = par_ref[1] == 0
     ea, eb = ea_ref[...], eb_ref[...]
-    blocks = [jnp.where(even_c, eb, ea)]
-    blocks += [f_ref[:, 128 * b : 128 * b + 128] for b in range(8)]
-    blocks += [jnp.where(even_c, ea, eb)]
     ocean_ref[...] = n2_ref[...]
-    for b in range(8):
-        cells = slice(128 * b, 128 * b + 128)
-        window = jnp.concatenate(blocks[b : b + 3], axis=1)
-        hi, lo = split_bf16(window)
-        own = blocks[b + 1]
-        both = mm(jnp.concatenate([hi.astype(F32), lo.astype(F32)], axis=0).astype(BF16), wm_ref[b])
-        top = both[0:8] + both[8:16] + (1.8 - sw_ref[:, cells]) * own
-        surface = []
-        for k in range(4):
-            value = n2_ref[16 * k : 16 * k + 1, cells] + top[k : k + 1]
-            if k == 2:
-                value = value + 0.2 * own[3:4]
-            if k == 3:
-                value = value - 0.2 * own[2:3]
-            ocean_ref[16 * k : 16 * k + 1, cells] = value
-            below = n2_ref[16 * k + 1 : 16 * k + 2, cells] + 0.2 * own[k : k + 1]
-            ocean_ref[16 * k + 1 : 16 * k + 2, cells] = below
-            surface.append(value)
-        lhs = jnp.concatenate(surface + [jnp.zeros((4, 128), F32)], axis=0).astype(BF16)
-        wide = jnp.concatenate([weights_ref[b, k] for k in range(8)], axis=1)
-        parts = mm(lhs, wide)
-        for k in range(8):
-            rows = slice((b * 8 + k) * 8, (b * 8 + k) * 8 + 8)
-            parts_ref[rows, :] = parts[:, 128 * k : 128 * k + 128]
-    sent_ref[...] = mm_t(request_matrix(tcol_ref), parts_ref[...].astype(BF16)).astype(BF16)
+    parts_ref[...] = inner_ref[...]
+    window = jnp.concatenate([jnp.where(even_c, eb, ea), f_ref[:, 0:256]], axis=1)
+    surface = force_block(window, ends_ref[0], sw_ref[:, 0:128], n2_ref, ocean_ref, 0)
+    return_parts(surface, first_ref, parts_ref, 0)
+    window = jnp.concatenate([f_ref[:, 768:1024], jnp.where(even_c, ea, eb)], axis=1)
+    surface = force_block(window, ends_ref[1], sw_ref[:, 896:1024], n2_ref, ocean_ref, 7)
+    return_parts(surface, last_ref, parts_ref, 7)
+    sent_ref[...] = mm_t(table_ref[...], parts_ref[...].astype(BF16)).astype(BF16)
 
 
 def collect_kernel(served_ref, incoming_ref, out_ref):
@@ -621,7 +650,7 @@
     pltpu.VMEM((4, 16, 128), F32),
     pltpu.VMEM((NFLUX, 4, 8, 128), F32),
     pltpu.VMEM((4, 32, 128), F32),
-    pltpu.SemaphoreType.DMA,
+    pltpu.VMEM((8, 64, 128), F32),
 )
 
 
@@ -670,18 +699,11 @@
         [pltpu.VMEM((33, 16, 1024), BF16), pltpu.VMEM((8, 64, 128), F32)],
     )(par, atm, flags, xa, xb, xp_a, xp_b)
     ya, yb = exchange(y_payload, "comp", N_COMP)
-    first, flag = call(
-        prepare_kernel,
-        (S((LEVELS, 4, 4, 16, 256), BF16), S((4, 16, 128), F32)),
-        [SMEM] + [VMEM] * 4,
-        [pltpu.VMEM((8, 64, 128), F32)],
-        cost=pl.CostEstimate(flops=2**23, bytes_accessed=2**23, transcendentals=0),
-    )(par, atm, flags, xa, xb)
     atm_final, table = staged(
         atm_kernel,
         (S((64, 32, 128), F32), S((128, 128), BF16)),
         (par, scal),
-        (first, flag, ya, yb),
+        (atm, flags, xa, xb, ya, yb),
         (vec, rhs),
         ATM_SCRATCH,
         late=1,
@@ -690,25 +712,31 @@
     )
     rows = call(pick_kernel, S((512, 128), BF16), [VMEM] * 2)(served, table)
     mean_rows = to_tiles(rows)
-    n2, wm, sw = call(
-        ocean_kernel,
-        (S((64, 1024), F32), S((8, 384, 128), BF16), S((8, 1024), F32)),
-        [SMEM] + [VMEM] * 5,
-        [pltpu.VMEM((10, 64, 128), F32)],
-        cost=pl.CostEstimate(flops=2**27, bytes_accessed=2**24, transcendentals=0),
-    )(par, ocean, ocean_neighbors, edge_weights, ya, yb)
     forcing, *edges = call(
         forcing_kernel,
         (S((8, 1024), F32), S((8, 128), F32), S((8, 128), F32)),
         [SMEM] + [VMEM] * 3,
     )(par, mean_rows, tcol, regrid_weights.reshape(8, 1024, 128))
     ea, eb = exchange(edges, ("tile", "comp"), N_TILE * N_COMP)
+    n2, ends, sw, parts, table = call(
+        ocean_kernel,
+        (
+            S((64, 1024), F32),
+            S((2, 384, 128), BF16),
+            S((8, 1024), F32),
+            S((512, 128), F32),
+            S((512, 512), BF16),
+        ),
+        [SMEM] + [VMEM] * 8,
+        [pltpu.VMEM((10, 64, 128), F32), pltpu.VMEM((8, 384, 128), BF16)],
+        cost=pl.CostEstimate(flops=2**27, bytes_accessed=2**24, transcendentals=0),
+    )(par, ocean, ocean_neighbors, edge_weights, ya, yb, forcing, return_weights, tcol)
     ocean_final, sent = call(
         return_kernel,
         (S((64, 1024), F32), S((512, 128), BF16)),
-        [SMEM] + [VMEM] * 8,
+        [SMEM] + [VMEM] * 10,
         [pltpu.VMEM((512, 128), F32)],
-    )(par, n2, wm, sw, forcing, ea, eb, tcol, return_weights)
+    )(par, n2, ends, sw, forcing, ea, eb, parts, table, return_weights[0], return_weights[7])
     incoming = to_tiles(sent)
     ocean_on_atm = call(collect_kernel, S((4, 32, 128), F32), [VMEM] * 2)(served, incoming)
     return (

time: 98.7 us -> 106 us (1.074)
  blocking collectives: 28.6 us -> 12.2 us
  starting transfers between devices: 18.5 us -> 26.7 us
  local copies, waits for them, and re-layouts: 6.57 us -> 14.6 us
  waiting for transfers between devices: 10.5 us -> 16.1 us
  Pallas kernels: 32.9 us -> 34.8 us
    all_to_all x2 -> x1, blocking collectives: 28.6 us -> 12.2 us  [to_tiles(): lax.all_to_all(rows.reshape(N_TILE, 16, 128), 'tile', split_axis=0, conca...]
    all_to_all x1 -> x2, waiting for transfers between devices: 0.01 us -> 8.69 us  [to_tiles(): lax.all_to_all(rows.reshape(N_TILE, 16, 128), 'tile', split_axis=0, conca...]
    all_to_all x1 -> x2, starting transfers between devices: 5.57 us -> 13.9 us  [to_tiles(): lax.all_to_all(rows.reshape(N_TILE, 16, 128), 'tile', split_axis=0, conca...]
    unnamed x35 -> x51, local copies, waits for them, and re-layouts: 6.32 us -> 14.3 us
    ppermute x3, waiting for transfers between devices: 9.05 us -> 5.96 us  [exchange(): lax.ppermute(payloads[1], axis, far)]
    pallas_call x2 -> x1, Pallas kernels: 3.6 us -> 4.21 us  [per_device(): call(ocean_kernel, (S((64, 1024), F32), S((2, 384, 128), BF16), S((8, 102...]
  transfers between devices with their start and end apart: 7 -> 8, of which waited for: 3 -> 4; matrix products, arithmetic and copies ran while one was open for 0% -> 0% of each run, Pallas kernels for 26% -> 26%
where the time goes in v4:
time: 106 us; the launch traced here: 105 us
  Pallas kernels  34.8 us (33%)
  starting transfers between devices  26.7 us (25%)
  waiting for transfers between devices  16.1 us (15%)
  local copies, waits for them, and re-layouts  14.6 us (14%)
  blocking collectives  12.2 us (12%)
    pallas_call x2, Pallas kernels, staged(): call(body, out, specs, scratch_shapes, mib, cost)  22.6 us
    unnamed x51, local copies, waits for them, and re-layouts  14.3 us
    all_to_all x2, starting transfers between devices, to_tiles(): lax.all_to_all(rows.reshape(N_TILE, 16, 128), 'tile', split_axis=0, conca...  13.9 us
    ppermute x3, starting transfers between devices, exchange(): lax.ppermute(payloads[1], axis, far)  12.7 us
    all_to_all x1, blocking collectives, to_tiles(): lax.all_to_all(rows.reshape(N_TILE, 16, 128), 'tile', split_axis=0, conca...  12.2 us
    all_to_all x2, waiting for transfers between devices, to_tiles(): lax.all_to_all(rows.reshape(N_TILE, 16, 128), 'tile', split_axis=0, conca...  8.69 us
    ppermute x3, waiting for transfers between devices, exchange(): lax.ppermute(payloads[1], axis, far)  5.96 us
    pallas_call x1, Pallas kernels, per_device(): call(ocean_kernel, (S((64, 1024), F32), S((2, 384, 128), BF16), S((8, 102...  4.21 us
  transfers between devices with their start and end apart: 8, of which 4 were waited for; matrix products, arithmetic and copies ran while one was open for 0% of the time, Pallas kernels for 26%

profile of v4, /device:TPU:0, one launch (start us, length us, event | category | flops | bytes accessed | tf_op | source)
XLA Modules:
  0.0 105.4 jit_solution(8489714241520941068)
XLA Ops:
  0.6 0.0 copy-start.21
  0.6 0.0 copy-start.23
  0.7 0.0 copy-start.22
  0.7 0.0 copy-start.24
  0.7 0.1 pad_add_fusion.refs_0_.par_ref
  0.8 1.2 %copy-done = f32[4,16,32,128]{3,2,1,0:T(8,128)S(1)} copy-done((f32[4,16,32,128]{3,2,1,0:T(8,128)S(1)}, f32[4,16,32,128]{3,2,1,0:T(8,128)}, u32[]{:S(2)}) %copy-start) | copy-done | bytes 1048600
  2.0 0.9 copy-done.4
  2.9 0.8 copy-done.10
  3.7 0.8 copy-done.12
  4.5 0.7 copy-done.16
  5.2 0.9 shard_map.148
  6.1 0.0 copy-start.17
  6.1 7.4 %collective-permute-start.1 = (bf16[74,16,128]{2,1,0:T(8,128)(2,1)S(1)}, bf16[74,16,128]{2,1,0:T(8,128)(2,1)S(1)}, u32[]{:S(2)}, u32[]{:S(2)}) collective-permute-start(bf16[74,16,128]{2,1,0:T(8,128)(2,1)S(1)} %get-tuple-element.29.pb_ref), channel_id=1, source_target_pairs={{0,124},{4,8},{8,4},{12,16},{16,12},{20,24},{24,20},{28,32},{32,28... | collective-permute-start | bytes 909320 | tf_op jit(solution)/shard_map/ppermute | solution.py:598
  13.5 0.0 collective-permute-start
  13.5 0.7 copy-done.19
  14.2 1.0 shard_map.149
  15.2 5.5 %collective-permute-done.1.xb_ref.refs_5_ = bf16[74,16,128]{2,1,0:T(8,128)(2,1)S(1)} collective-permute-done((bf16[74,16,128]{2,1,0:T(8,128)(2,1)S(1)}, bf16[74,16,128]{2,1,0:T(8,128)(2,1)S(1)}, u32[]{:S(2)}, u32[]{:S(2)}) %collective-permute-start.1) | collective-permute-done | bytes 303136 | tf_op jit(solution)/shard_map/ppermute | solution.py:598
  20.7 1.5 %collective-permute-done.xa_ref.refs_4_ = bf16[74,16,128]{2,1,0:T(8,128)(2,1)S(1)} collective-permute-done((bf16[74,16,128]{2,1,0:T(8,128)(2,1)S(1)}, bf16[74,16,128]{2,1,0:T(8,128)(2,1)S(1)}, u32[]{:S(2)}, u32[]{:S(2)}) %collective-permute-start) | collective-permute-done | bytes 303136 | tf_op jit(solution)/shard_map/ppermute | solution.py:598
  22.1 0.0 copy-done.1
  22.1 2.0 %shard_map.150 = (bf16[672,128]{1,0:T(8,128)(2,1)}, bf16[672,128]{1,0:T(8,128)(2,1)}) custom-call(s32[4]{0:T(128)S(1)} %pad_add_fusion.refs_0_.par_ref, f32[64,32,128]{2,1,0:T(8,128)S(1)} %bitcast.20, f32[32,128]{1,0:T(8,128)S(1)} %get-tuple-element.25.flags_ref.refs_3_, bf16[74,16,128]{2,1,0:T(8,128)(2,1)S(1)} %collective-permute-done.xa_ref.refs_4_, ...), custom_call_target="tpu_custom_call" | custom-call | tf_op jit(solution)/shard_map/pallas_call | solution.py:695
  24.2 0.0 copy-done.8
  24.2 0.7 copy-done.6
  24.9 0.0 copy-done.17
  24.9 0.0 collective-permute-start.2
  24.9 3.0 %collective-permute-start.3 = (bf16[672,128]{1,0:T(8,128)(2,1)}, bf16[672,128]{1,0:T(8,128)(2,1)}, u32[]{:S(2)}, u32[]{:S(2)}) collective-permute-start(bf16[672,128]{1,0:T(8,128)(2,1)} %get-tuple-element.32), channel_id=1, source_target_pairs={{0,3},{1,2},{2,1},{3,0},{4,7},{5,6},{6,5},{7,4},{8,11},{9,10},{10,... | collective-permute-start | bytes 516104 | tf_op jit(solution)/shard_map/ppermute | solution.py:598
  27.9 0.0 copy-done.23
  27.9 0.1 reshape.50
  28.0 0.0 copy-done.22
  28.0 0.1 copy.17
  28.1 0.1 reshape.49
  28.2 0.0 copy-done.24
  28.2 0.1 reshape.48
  28.3 0.1 pad_maximum_fusion.refs_1_
  28.4 5.6 %all-to-all-start = ((bf16[32,16,128]{2,1,0:T(8,128)(2,1)}), bf16[32,16,128]{2,1,0:T(8,128)(2,1)S(1)}, u32[]{:S(2)}, u32[]{:S(2)}) async-start(bf16[32,16,128]{2,1,0:T(8,128)(2,1)} %bitcast.7), calls=%async_computation | async-start | bytes 262144 | tf_op jit(solution)/shard_map/all_to_all | solution.py:602
  33.9 0.0 copy-start.2
  33.9 0.0 collective-permute-done.2.refs_6_.ya_ref
  34.0 0.0 collective-permute-done.3.refs_7_.yb_ref
  34.0 0.0 copy-done.21
  34.0 0.0 copy-start.7
  34.0 1.1 %copy-done.7 = bf16[74,16,128]{2,1,0:T(8,128)(2,1)S(1)} copy-done((bf16[74,16,128]{2,1,0:T(8,128)(2,1)S(1)}, bf16[74,16,128]{2,1,0:T(8,128)(2,1)}, u32[]{:S(2)}) %copy-start.7) | copy-done | bytes 303128
  35.1 1.0 copy-done.9
  36.1 0.7 copy-done.18
  36.8 1.1 %copy-done.20 = bf16[2,256,640]{2,1,0:T(8,128)(2,1)S(1)} copy-done((bf16[2,256,640]{2,1,0:T(8,128)(2,1)S(1)}, bf16[2,256,640]{2,1,0:T(8,128)(2,1)}, u32[]{:S(2)}) %copy-start.20) | copy-done | bytes 655384
  37.9 21.8 %shard_map.151 = (f32[64,32,128]{2,1,0:T(8,128)}, bf16[128,128]{1,0:T(8,128)(2,1)S(1)}) custom-call(s32[4]{0:T(128)S(1)} %pad_add_fusion.refs_0_.par_ref, f32[128]{0:T(128)S(1)} %pad_maximum_fusion.refs_1_, f32[64,32,128]{2,1,0:T(8,128)S(1)} %bitcast.21, f32[32,128]{1,0:T(8,128)S(1)} %copy-done.18, bf16[74,16,128]{2,1,0:T(8,128)(2,1)S(1)} %copy-done.9, ...), custom_call_target="tpu_custom_call" | custom-call | flops 8589934592 | bytes 67108864 | tf_op jit(solution)/shard_map/pallas_call | solution.py:639
  59.6 0.0 copy-start.14
  59.6 0.6 copy-done.14
  60.2 0.0 all-to-all-done
  60.2 0.8 copy-done.15
  61.0 0.8 shard_map.152
  61.9 8.3 %all-to-all-start.1 = ((bf16[32,16,128]{2,1,0:T(8,128)(2,1)}), bf16[32,16,128]{2,1,0:T(8,128)(2,1)S(1)}, u32[]{:S(2)}, u32[]{:S(2)}) async-start(bf16[32,16,128]{2,1,0:T(8,128)(2,1)} %bitcast.9), calls=%async_computation.1 | async-start | bytes 262144 | tf_op jit(solution)/shard_map/all_to_all | solution.py:602
  70.2 0.0 copy-done.2
  70.2 8.7 %all-to-all-done.1 = bf16[32,16,128]{2,1,0:T(8,128)(2,1)S(1)} async-done(((bf16[32,16,128]{2,1,0:T(8,128)(2,1)}), bf16[32,16,128]{2,1,0:T(8,128)(2,1)S(1)}, u32[]{:S(2)}, u32[]{:S(2)}) %all-to-all-start.1) | async-done | bytes 131104 | tf_op jit(solution)/shard_map/all_to_all | solution.py:602
  78.9 1.6 %copy-done.3 = bf16[8,8,128,128]{3,2,1,0:T(8,128)(2,1)S(1)} copy-done((bf16[8,8,128,128]{3,2,1,0:T(8,128)(2,1)S(1)}, bf16[8,8,128,128]{3,2,1,0:T(8,128)(2,1)}, u32[]{:S(2)}) %copy-start.3) | copy-done | bytes 2097176
  80.5 1.3 %shard_map.153 = (f32[8,1024]{1,0:T(8,128)S(1)}, f32[8,128]{1,0:T(8,128)S(1)}, f32[8,128]{1,0:T(8,128)S(1)}) custom-call(s32[4]{0:T(128)S(1)} %pad_add_fusion.refs_0_.par_ref, bf16[512,128]{1,0:T(8,128)(2,1)S(1)} %bitcast.28, s32[512,128]{1,0:T(8,128)S(1)} %get-tuple-element.36.tcol_ref, bf16[8,1024,128]{2,1,0:T(8,128)(2,1)S(1)} %bitcast.22), custom_call_target="tpu_custom_call" | custom-call | tf_op jit(solution)/shard_map/pallas_call | solution.py:715
  81.8 0.1 collective-permute-start.4
  81.9 2.3 %collective-permute-start.5 = (f32[8,128]{1,0:T(8,128)S(1)}, f32[8,128]{1,0:T(8,128)S(1)}, u32[]{:S(2)}, u32[]{:S(2)}) collective-permute-start(f32[8,128]{1,0:T(8,128)S(1)} %get-tuple-element.42), channel_id=1, source_target_pairs={{0,127},{1,2},{2,1},{3,4},{4,3},{5,6},{6,5},{7,8},{8,7},{9,10},{10... | collective-permute-start | bytes 12296 | tf_op jit(solution)/shard_map/ppermute | solution.py:598
  84.2 0.8 copy-done.11
  85.0 0.8 copy-done.13
  85.8 4.2 %shard_map.154 = (f32[64,1024]{1,0:T(8,128)S(1)}, bf16[2,384,128]{2,1,0:T(8,128)(2,1)S(1)}, f32[8,1024]{1,0:T(8,128)S(1)}, f32[512,128]{1,0:T(8,128)S(1)}, bf16[512,512]{1,0:T(8,128)(2,1)S(1)}) custom-call(s32[4]{0:T(128)S(1)} %pad_add_fusion.refs_0_.par_ref, f32[64,1024]{1,0:T(8,128)S(1)} %bitcast.26, s32[6,1024]{1,0:T(8,128)S(1)} %copy-done.11, ...), custom_call_target="tpu_custom_call" | custom-call | flops 134217728 | bytes 16777216 | tf_op jit(solution)/shard_map/pallas_call | solution.py:721
  90.0 0.0 collective-permute-done.4.ea_ref
  90.0 0.5 collective-permute-done.5.eb_ref
  90.5 1.9 %shard_map.155 = (f32[64,1024]{1,0:T(8,128)}, bf16[512,128]{1,0:T(8,128)(2,1)S(1)}) custom-call(s32[4]{0:T(128)S(1)} %pad_add_fusion.refs_0_.par_ref, f32[64,1024]{1,0:T(8,128)S(1)} %get-tuple-element.38.n2_ref, bf16[2,384,128]{2,1,0:T(8,128)(2,1)S(1)} %get-tuple-element.39.ends_ref, f32[8,1024]{1,0:T(8,128)S(1)} %get-tuple-element.40.sw_ref, ...), custom_call_target="tpu_custom_call" | custom-call | tf_op jit(solution)/shard_map/pallas_call | solution.py:734
  92.3 12.2 %all_to_all.15 = bf16[32,16,128]{2,1,0:T(8,128)(2,1)S(1)} all-to-all(bf16[32,16,128]{2,1,0:T(8,128)(2,1)S(1)} %bitcast.29), channel_id=1, replica_groups=mesh['tile'=32,'comp'=4] {'tile'}, dimensions={0} | all-to-all | bytes 262144 | tf_op jit(solution)/shard_map/all_to_all | solution.py:602
  104.5 0.9 shard_map.156
  (19 shorter events, 0.1 us)
Async XLA Ops:
  0.6 33.3 %copy-start.21 = (f32[16,128]{1,0:T(8,128)S(1)}, f32[16,128]{1,0:T(8,128)}, u32[]{:S(2)}) copy-start(f32[16,128]{1,0:T(8,128)} %constant.31.clone.refs_8_) | copy-start | bytes 24580
  0.6 27.3 %copy-start.23 = (f32[4,12]{1,0:T(4,128)S(1)}, f32[4,12]{1,0:T(4,128)}, u32[]{:S(2)}) copy-start(f32[4,12]{1,0:T(4,128)} %param.23) | copy-start | bytes 580
  0.7 27.4 %copy-start.22 = (f32[12,4]{0,1:T(4,128)S(1)}, f32[12,4]{0,1:T(4,128)}, u32[]{:S(2)}) copy-start(f32[12,4]{0,1:T(4,128)} %param.16) | copy-start | bytes 580
  0.7 27.5 %copy-start.24 = (f32[2,16]{1,0:T(2,128)S(1)}, f32[2,16]{1,0:T(2,128)}, u32[]{:S(2)}) copy-start(f32[2,16]{1,0:T(2,128)} %param.14) | copy-start | bytes 388
  0.8 1.2 %copy-start = (f32[4,16,32,128]{3,2,1,0:T(8,128)S(1)}, f32[4,16,32,128]{3,2,1,0:T(8,128)}, u32[]{:S(2)}) copy-start(f32[4,16,32,128]{3,2,1,0:T(8,128)} %param.13) | copy-start | bytes 3145732
  2.0 0.9 copy-start.4
  2.9 0.8 copy-start.10
  3.7 0.8 copy-start.12
  4.5 0.7 copy-start.16
  5.2 16.9 %copy-start.1 = (f32[4,16,32,128]{3,2,1,0:T(8,128)S(1)}, f32[4,16,32,128]{3,2,1,0:T(8,128)}, u32[]{:S(2)}) copy-start(f32[4,16,32,128]{3,2,1,0:T(8,128)} %param.13) | copy-start | bytes 3145732
  6.1 18.8 %copy-start.17 = (f32[32,128]{1,0:T(8,128)}, f32[32,128]{1,0:T(8,128)S(1)}, u32[]{:S(2)}) copy-start(f32[32,128]{1,0:T(8,128)S(1)} %get-tuple-element.25.flags_ref.refs_3_) | copy-start | bytes 49156
  6.1 14.6 %collective-permute-start.1 = (bf16[74,16,128]{2,1,0:T(8,128)(2,1)S(1)}, bf16[74,16,128]{2,1,0:T(8,128)(2,1)S(1)}, u32[]{:S(2)}, u32[]{:S(2)}) collective-permute-start(bf16[74,16,128]{2,1,0:T(8,128)(2,1)S(1)} %get-tuple-element.29.pb_ref), channel_id=1, source_target_pairs={{0,124},{4,8},{8,4},{12,16},{16,12},{20,24},{24,20},{28,32},{32,28... | collective-permute-start | bytes 909320 | tf_op jit(solution)/shard_map/ppermute | solution.py:598
  13.5 8.6 %collective-permute-start = (bf16[74,16,128]{2,1,0:T(8,128)(2,1)S(1)}, bf16[74,16,128]{2,1,0:T(8,128)(2,1)S(1)}, u32[]{:S(2)}, u32[]{:S(2)}) collective-permute-start(bf16[74,16,128]{2,1,0:T(8,128)(2,1)S(1)} %get-tuple-element.26.pa_ref), channel_id=1, source_target_pairs={{0,4},{4,0},{8,12},{12,8},{16,20},{20,16},{24,28},{28,24},{32,36},... | collective-permute-start | bytes 909320 | tf_op jit(solution)/shard_map/ppermute | solution.py:598
  13.5 0.7 copy-start.19
  22.1 2.1 %copy-start.8 = (bf16[74,16,128]{2,1,0:T(8,128)(2,1)}, bf16[74,16,128]{2,1,0:T(8,128)(2,1)S(1)}, u32[]{:S(2)}) copy-start(bf16[74,16,128]{2,1,0:T(8,128)(2,1)S(1)} %collective-permute-done.xa_ref.refs_4_) | copy-start | bytes 909316
  24.2 0.7 copy-start.6
  24.9 9.1 %collective-permute-start.2 = (bf16[672,128]{1,0:T(8,128)(2,1)}, bf16[672,128]{1,0:T(8,128)(2,1)}, u32[]{:S(2)}, u32[]{:S(2)}) collective-permute-start(bf16[672,128]{1,0:T(8,128)(2,1)} %get-tuple-element.31), channel_id=1, source_target_pairs={{0,1},{1,0},{2,3},{3,2},{4,5},{5,4},{6,7},{7,6},{8,9},{9,8},{10,11... | collective-permute-start | bytes 516104 | tf_op jit(solution)/shard_map/ppermute | solution.py:598
  24.9 9.1 %collective-permute-start.3 = (bf16[672,128]{1,0:T(8,128)(2,1)}, bf16[672,128]{1,0:T(8,128)(2,1)}, u32[]{:S(2)}, u32[]{:S(2)}) collective-permute-start(bf16[672,128]{1,0:T(8,128)(2,1)} %get-tuple-element.32), channel_id=1, source_target_pairs={{0,3},{1,2},{2,1},{3,0},{4,7},{5,6},{6,5},{7,4},{8,11},{9,10},{10,... | collective-permute-start | bytes 516104 | tf_op jit(solution)/shard_map/ppermute | solution.py:598
  28.4 31.9 %all-to-all-start = ((bf16[32,16,128]{2,1,0:T(8,128)(2,1)}), bf16[32,16,128]{2,1,0:T(8,128)(2,1)S(1)}, u32[]{:S(2)}, u32[]{:S(2)}) async-start(bf16[32,16,128]{2,1,0:T(8,128)(2,1)} %bitcast.7), calls=%async_computation | async-start | bytes 262144 | tf_op jit(solution)/shard_map/all_to_all | solution.py:602
  33.9 36.2 %copy-start.2 = (bf16[8,8,128,128]{3,2,1,0:T(8,128)(2,1)S(1)}, bf16[8,8,128,128]{3,2,1,0:T(8,128)(2,1)}, u32[]{:S(2)}) copy-start(bf16[8,8,128,128]{3,2,1,0:T(8,128)(2,1)} %weights_ref.1) | copy-start | bytes 6291460
  34.0 1.1 %copy-start.7 = (bf16[74,16,128]{2,1,0:T(8,128)(2,1)S(1)}, bf16[74,16,128]{2,1,0:T(8,128)(2,1)}, u32[]{:S(2)}) copy-start(bf16[74,16,128]{2,1,0:T(8,128)(2,1)} %copy-done.6) | copy-start | bytes 909316
  35.1 1.0 copy-start.9
  36.1 0.7 copy-start.18
  36.8 1.1 %copy-start.20 = (bf16[2,256,640]{2,1,0:T(8,128)(2,1)S(1)}, bf16[2,256,640]{2,1,0:T(8,128)(2,1)}, u32[]{:S(2)}) copy-start(bf16[2,256,640]{2,1,0:T(8,128)(2,1)} %constant.30.clone.refs_9_) | copy-start | bytes 1966084
  59.6 0.6 copy-start.14
  60.2 24.0 %copy-start.5 = (f32[4,16,1024]{2,1,0:T(8,128)S(1)}, f32[4,16,1024]{2,1,0:T(8,128)}, u32[]{:S(2)}) copy-start(f32[4,16,1024]{2,1,0:T(8,128)} %param.20) | copy-start | bytes 786436
  60.2 0.8 copy-start.15
  61.9 17.0 %all-to-all-start.1 = ((bf16[32,16,128]{2,1,0:T(8,128)(2,1)}), bf16[32,16,128]{2,1,0:T(8,128)(2,1)S(1)}, u32[]{:S(2)}, u32[]{:S(2)}) async-start(bf16[32,16,128]{2,1,0:T(8,128)(2,1)} %bitcast.9), calls=%async_computation.1 | async-start | bytes 262144 | tf_op jit(solution)/shard_map/all_to_all | solution.py:602
  78.9 1.6 %copy-start.3 = (bf16[8,8,128,128]{3,2,1,0:T(8,128)(2,1)S(1)}, bf16[8,8,128,128]{3,2,1,0:T(8,128)(2,1)}, u32[]{:S(2)}) copy-start(bf16[8,8,128,128]{3,2,1,0:T(8,128)(2,1)} %param.18) | copy-start | bytes 6291460
  81.8 8.1 %collective-permute-start.4 = (f32[8,128]{1,0:T(8,128)S(1)}, f32[8,128]{1,0:T(8,128)S(1)}, u32[]{:S(2)}, u32[]{:S(2)}) collective-permute-start(f32[8,128]{1,0:T(8,128)S(1)} %get-tuple-element.41), channel_id=1, source_target_pairs={{0,1},{1,0},{2,3},{3,2},{4,5},{5,4},{6,7},{7,6},{8,9},{9,8},{10,11... | collective-permute-start | bytes 12296 | tf_op jit(solution)/shard_map/ppermute | solution.py:598
  81.9 8.5 %collective-permute-start.5 = (f32[8,128]{1,0:T(8,128)S(1)}, f32[8,128]{1,0:T(8,128)S(1)}, u32[]{:S(2)}, u32[]{:S(2)}) collective-permute-start(f32[8,128]{1,0:T(8,128)S(1)} %get-tuple-element.42), channel_id=1, source_target_pairs={{0,127},{1,2},{2,1},{3,4},{4,3},{5,6},{6,5},{7,8},{8,7},{9,10},{10... | collective-permute-start | bytes 12296 | tf_op jit(solution)/shard_map/ppermute | solution.py:598
  84.2 0.8 copy-start.11
  85.0 0.8 copy-start.13

commit v5 on v4

--- a/solution.py
+++ b/solution.py
@@ -229,6 +229,25 @@
         b_ref[dest] = jnp.where(even_c, left, right).astype(BF16)
 
 
+def prepare_kernel(par_ref, atm_ref, flags_ref, xa_ref, xb_ref, cb_ref, flag_ref, ts_ref):
+    even_t = par_ref[0] == 0
+
+    def group(q, _):
+        for s in range(8):
+            p = q * 8 + s
+            rows = x_extended(ts_ref, s, atm_ref[p], xa_ref, xb_ref, p, even_t)
+            for i in range(4):
+                hi, lo = split_bf16(rows[i])
+                cb_ref[(q % 2) * 8 + s, q // 2, i, :, 0:128] = hi
+                cb_ref[(q % 2) * 8 + s, q // 2, i, :, 128:256] = lo
+        return 0
+
+    lax.fori_loop(0, 8, group, 0)
+    rows = x_extended(ts_ref, 0, flags_ref[...], xa_ref, xb_ref, 64, even_t)
+    for i in range(4):
+        flag_ref[i] = rows[i]
+
+
 def x_slopes(a):
     sums, diffs = (a[0] + a[3], a[1] + a[2]), (a[0] - a[3], a[1] - a[2])
     across = sums[0] - sums[1]
@@ -244,10 +263,8 @@
 def atm_kernel(
     par_ref,
     scal_ref,
-    atm_ref,
-    flags_ref,
-    xa_ref,
-    xb_ref,
+    first_ref,
+    flag_ref,
     ya_ref,
     yb_ref,
     vec_ref,
@@ -264,10 +281,11 @@
     r5_ref,
     facc_ref,
     gs_ref,
-    ts_ref,
+    first_sem,
     copies,
 ):
-    even_t = par_ref[0] == 0
+    first_copy = pltpu.make_async_copy(first_ref, cb_ref, first_sem)
+    first_copy.start()
     even_c = par_ref[1] == 0
     comp = par_ref[2]
     lane = iota((16, 128), 1)
@@ -295,19 +313,8 @@
     halo_m5 = jnp.where(halo_flag == 2.0, 5.0 * DT, 0.0)
     halo_keep = 1.0 - 2.0 * halo_m5
     halo_keep_t = halo_keep - halo_r5
-
-    def prepare(q, _):
-        for s in range(8):
-            p = q * 8 + s
-            rows = x_extended(ts_ref, s, atm_ref[p], xa_ref, xb_ref, p, even_t)
-            for i in range(4):
-                put(cb_ref, ((q % 2) * 8 + s, q // 2, i), rows[i])
-        return 0
-
-    lax.fori_loop(0, 8, prepare, 0)
-    flag_rows = x_extended(ts_ref, 0, flags_ref[...], xa_ref, xb_ref, 64, even_t)
     for i in range(4):
-        flag = flag_rows[i]
+        flag = flag_ref[i]
         m5 = jnp.where(flag == 2.0, 5.0 * DT, 0.0)
         r5_ref[i] = jnp.where(flag == 1.0, 5.0 * DT, 0.0)
         mask_ref[0, i] = m5
@@ -319,7 +326,7 @@
     halo_dt_x = -DT * vec_ref[2:3, :]
     ff = vec_ref[pl.ds(4 + comp, 1), :]
     halo_ff = vec_ref[pl.ds(8 + comp, 1), :]
-    for copy in copies:
+    for copy in (first_copy, *copies):
         copy.wait()
 
     def step(si, _):
@@ -650,7 +657,7 @@
     pltpu.VMEM((4, 16, 128), F32),
     pltpu.VMEM((NFLUX, 4, 8, 128), F32),
     pltpu.VMEM((4, 32, 128), F32),
-    pltpu.VMEM((8, 64, 128), F32),
+    pltpu.SemaphoreType.DMA,
 )
 
 
@@ -699,11 +706,18 @@
         [pltpu.VMEM((33, 16, 1024), BF16), pltpu.VMEM((8, 64, 128), F32)],
     )(par, atm, flags, xa, xb, xp_a, xp_b)
     ya, yb = exchange(y_payload, "comp", N_COMP)
+    first, flag = call(
+        prepare_kernel,
+        (S((LEVELS, 4, 4, 16, 256), BF16), S((4, 16, 128), F32)),
+        [SMEM] + [VMEM] * 4,
+        [pltpu.VMEM((8, 64, 128), F32)],
+        cost=pl.CostEstimate(flops=2**23, bytes_accessed=2**23, transcendentals=0),
+    )(par, atm, flags, xa, xb)
     atm_final, table = staged(
         atm_kernel,
         (S((64, 32, 128), F32), S((128, 128), BF16)),
         (par, scal),
-        (atm, flags, xa, xb, ya, yb),
+        (first, flag, ya, yb),
         (vec, rhs),
         ATM_SCRATCH,
         late=1,

time: 106 us -> 101 us (0.953)
  local copies, waits for them, and re-layouts: 14.6 us -> 8.92 us
  waiting for transfers between devices: 16.1 us -> 18.1 us
  Pallas kernels: 34.8 us -> 33.7 us
    unnamed x51 -> x43, local copies, waits for them, and re-layouts: 14.3 us -> 8.63 us
    ppermute x3, waiting for transfers between devices: 5.96 us -> 7.92 us  [exchange(): lax.ppermute(payloads[1], axis, far)]
  transfers between devices with their start and end apart: 8 -> 8, of which waited for: 4 -> 4; matrix products, arithmetic and copies ran while one was open for 0% -> 0% of each run, Pallas kernels for 26% -> 27%
where the time goes in v5:
time: 101 us; the launch traced here: 100 us
  Pallas kernels  33.7 us (33%)
  starting transfers between devices  26.8 us (27%)
  waiting for transfers between devices  18.1 us (18%)
  blocking collectives  11.7 us (12%)
  local copies, waits for them, and re-layouts  8.92 us (9%)
    pallas_call x2, Pallas kernels, staged(): call(body, out, specs, scratch_shapes, mib, cost)  21.8 us
    all_to_all x2, starting transfers between devices, to_tiles(): lax.all_to_all(rows.reshape(N_TILE, 16, 128), 'tile', split_axis=0, conca...  13.9 us
    ppermute x3, starting transfers between devices, exchange(): lax.ppermute(payloads[1], axis, far)  12.7 us
    all_to_all x1, blocking collectives, to_tiles(): lax.all_to_all(rows.reshape(N_TILE, 16, 128), 'tile', split_axis=0, conca...  11.7 us
    all_to_all x2, waiting for transfers between devices, to_tiles(): lax.all_to_all(rows.reshape(N_TILE, 16, 128), 'tile', split_axis=0, conca...  8.69 us
    unnamed x43, local copies, waits for them, and re-layouts  8.63 us
    ppermute x3, waiting for transfers between devices, exchange(): lax.ppermute(payloads[1], axis, far)  7.92 us
    pallas_call x1, Pallas kernels, per_device(): call(ocean_kernel, (S((64, 1024), F32), S((2, 384, 128), BF16), S((8, 102...  3.74 us
  transfers between devices with their start and end apart: 8, of which 4 were waited for; matrix products, arithmetic and copies ran while one was open for 0% of the time, Pallas kernels for 27%

profile of v5, /device:TPU:0, one launch (start us, length us, event | category | flops | bytes accessed | tf_op | source)
XLA Modules:
  0.0 100.2 jit_solution(6816786379637995988)
XLA Ops:
  0.6 0.0 copy-start.18
  0.6 0.0 copy-start.20
  0.7 0.0 copy-start.19
  0.7 0.1 pad_add_fusion.refs_0_.par_ref
  0.8 0.0 copy-start
  0.8 1.2 %copy-done = f32[4,16,32,128]{3,2,1,0:T(8,128)S(1)} copy-done((f32[4,16,32,128]{3,2,1,0:T(8,128)S(1)}, f32[4,16,32,128]{3,2,1,0:T(8,128)}, u32[]{:S(2)}) %copy-start) | copy-done | bytes 1048600
  2.0 0.0 copy-start.4
  2.0 0.9 copy-done.4
  2.9 0.0 copy-start.10
  2.9 0.8 copy-done.10
  3.7 0.0 copy-start.12
  3.7 0.8 copy-done.12
  4.5 0.7 copy-done.14
  5.2 0.9 shard_map.148
  6.0 7.4 %collective-permute-start.1 = (bf16[74,16,128]{2,1,0:T(8,128)(2,1)S(1)}, bf16[74,16,128]{2,1,0:T(8,128)(2,1)S(1)}, u32[]{:S(2)}, u32[]{:S(2)}) collective-permute-start(bf16[74,16,128]{2,1,0:T(8,128)(2,1)S(1)} %get-tuple-element.31.pb_ref), channel_id=1, source_target_pairs={{0,124},{4,8},{8,4},{12,16},{16,12},{20,24},{24,20},{28,32},{32,28... | collective-permute-start | bytes 909320 | tf_op jit(solution)/shard_map/ppermute | solution.py:605
  13.5 0.0 collective-permute-start
  13.5 0.7 copy-done.15
  14.1 1.0 %shard_map.149 = (bf16[512,128]{1,0:T(8,128)(2,1)}, s32[512,128]{1,0:T(8,128)S(1)}) custom-call(s32[8,8]{1,0:T(8,128)S(1)} %copy-done.15), custom_call_target="tpu_custom_call" | custom-call | tf_op jit(solution)/shard_map/pallas_call | solution.py:697
  15.2 5.5 %collective-permute-done.1.xb_ref = bf16[74,16,128]{2,1,0:T(8,128)(2,1)S(1)} collective-permute-done((bf16[74,16,128]{2,1,0:T(8,128)(2,1)S(1)}, bf16[74,16,128]{2,1,0:T(8,128)(2,1)S(1)}, u32[]{:S(2)}, u32[]{:S(2)}) %collective-permute-start.1) | collective-permute-done | bytes 303136 | tf_op jit(solution)/shard_map/ppermute | solution.py:605
  20.6 1.5 %collective-permute-done.xa_ref = bf16[74,16,128]{2,1,0:T(8,128)(2,1)S(1)} collective-permute-done((bf16[74,16,128]{2,1,0:T(8,128)(2,1)S(1)}, bf16[74,16,128]{2,1,0:T(8,128)(2,1)S(1)}, u32[]{:S(2)}, u32[]{:S(2)}) %collective-permute-start) | collective-permute-done | bytes 303136 | tf_op jit(solution)/shard_map/ppermute | solution.py:605
  22.1 0.0 copy-done.1
  22.1 1.3 %shard_map.151 = (bf16[672,128]{1,0:T(8,128)(2,1)S(1)}, bf16[672,128]{1,0:T(8,128)(2,1)S(1)}) custom-call(s32[4]{0:T(128)S(1)} %pad_add_fusion.refs_0_.par_ref, f32[64,32,128]{2,1,0:T(8,128)S(1)} %bitcast.20, f32[32,128]{1,0:T(8,128)S(1)} %get-tuple-element.27.flags_ref, bf16[74,16,128]{2,1,0:T(8,128)(2,1)S(1)} %collective-permute-done.xa_ref, ...), custom_call_target="tpu_custom_call" | custom-call | tf_op jit(solution)/shard_map/pallas_call | solution.py:702
  23.4 0.1 collective-permute-start.2
  23.5 3.0 %collective-permute-start.3 = (bf16[672,128]{1,0:T(8,128)(2,1)S(1)}, bf16[672,128]{1,0:T(8,128)(2,1)S(1)}, u32[]{:S(2)}, u32[]{:S(2)}) collective-permute-start(bf16[672,128]{1,0:T(8,128)(2,1)S(1)} %get-tuple-element.36), channel_id=1, source_target_pairs={{0,3},{1,2},{2,1},{3,0},{4,7},{5,6},{6,5},{7,4},{8,11},{9,10},{10,... | collective-permute-start | bytes 516104 | tf_op jit(solution)/shard_map/ppermute | solution.py:605
  26.5 0.0 copy-done.18
  26.5 0.1 copy.17
  26.6 0.1 reshape.49
  26.7 0.0 copy-done.20
  26.7 0.1 reshape.48
  26.8 0.0 copy-done.19
  26.8 0.1 reshape.50
  26.9 0.1 pad_maximum_fusion.refs_1_
  27.0 5.6 %all-to-all-start = ((bf16[32,16,128]{2,1,0:T(8,128)(2,1)}), bf16[32,16,128]{2,1,0:T(8,128)(2,1)S(1)}, u32[]{:S(2)}, u32[]{:S(2)}) async-start(bf16[32,16,128]{2,1,0:T(8,128)(2,1)} %bitcast.7), calls=%async_computation | async-start | bytes 262144 | tf_op jit(solution)/shard_map/all_to_all | solution.py:609
  32.5 1.0 shard_map.150
  33.5 0.0 collective-permute-done.2.refs_4_.ya_ref
  33.5 0.0 collective-permute-done.3.refs_5_.yb_ref
  33.6 0.0 copy-start.8
  33.6 0.0 copy-done.17
  33.6 0.0 copy-start.16
  33.6 1.1 %copy-done.16 = bf16[2,256,640]{2,1,0:T(8,128)(2,1)S(1)} copy-done((bf16[2,256,640]{2,1,0:T(8,128)(2,1)S(1)}, bf16[2,256,640]{2,1,0:T(8,128)(2,1)}, u32[]{:S(2)}) %copy-start.16) | copy-done | bytes 655384
  34.7 20.9 %shard_map.152 = (f32[64,32,128]{2,1,0:T(8,128)}, bf16[128,128]{1,0:T(8,128)(2,1)S(1)}) custom-call(s32[4]{0:T(128)S(1)} %pad_add_fusion.refs_0_.par_ref, f32[128]{0:T(128)S(1)} %pad_maximum_fusion.refs_1_, bf16[16,4,4,16,256]{4,3,2,1,0:T(8,128)(2,1)S(1)} %get-tuple-element.33.refs_2_, f32[4,16,128]{2,1,0:T(8,128)S(1)} %get-tuple-element.34.refs_3_, ...), custom_call_target="tpu_custom_call" | custom-call | flops 8589934592 | bytes 67108864 | tf_op jit(solution)/shard_map/pallas_call | solution.py:646
  55.6 0.0 copy-done.8
  55.7 0.0 copy-start.6
  55.7 0.7 copy-done.6
  56.3 0.0 all-to-all-done
  56.3 0.8 shard_map.153
  57.2 8.3 %all-to-all-start.1 = ((bf16[32,16,128]{2,1,0:T(8,128)(2,1)}), bf16[32,16,128]{2,1,0:T(8,128)(2,1)S(1)}, u32[]{:S(2)}, u32[]{:S(2)}) async-start(bf16[32,16,128]{2,1,0:T(8,128)(2,1)} %bitcast.9), calls=%async_computation.1 | async-start | bytes 262144 | tf_op jit(solution)/shard_map/all_to_all | solution.py:609
  65.5 0.0 copy-done.2
  65.5 8.7 %all-to-all-done.1 = bf16[32,16,128]{2,1,0:T(8,128)(2,1)S(1)} async-done(((bf16[32,16,128]{2,1,0:T(8,128)(2,1)}), bf16[32,16,128]{2,1,0:T(8,128)(2,1)S(1)}, u32[]{:S(2)}, u32[]{:S(2)}) %all-to-all-start.1) | async-done | bytes 131104 | tf_op jit(solution)/shard_map/all_to_all | solution.py:609
  74.2 1.6 %copy-done.3 = bf16[8,8,128,128]{3,2,1,0:T(8,128)(2,1)S(1)} copy-done((bf16[8,8,128,128]{3,2,1,0:T(8,128)(2,1)S(1)}, bf16[8,8,128,128]{3,2,1,0:T(8,128)(2,1)}, u32[]{:S(2)}) %copy-start.3) | copy-done | bytes 2097176
  75.8 1.3 %shard_map.154 = (f32[8,1024]{1,0:T(8,128)S(1)}, f32[8,128]{1,0:T(8,128)S(1)}, f32[8,128]{1,0:T(8,128)S(1)}) custom-call(s32[4]{0:T(128)S(1)} %pad_add_fusion.refs_0_.par_ref, bf16[512,128]{1,0:T(8,128)(2,1)S(1)} %bitcast.28, s32[512,128]{1,0:T(8,128)S(1)} %get-tuple-element.40.tcol_ref, bf16[8,1024,128]{2,1,0:T(8,128)(2,1)S(1)} %bitcast.22), custom_call_target="tpu_custom_call" | custom-call | tf_op jit(solution)/shard_map/pallas_call | solution.py:729
  77.1 0.1 collective-permute-start.4
  77.2 2.3 %collective-permute-start.5 = (f32[8,128]{1,0:T(8,128)S(1)}, f32[8,128]{1,0:T(8,128)S(1)}, u32[]{:S(2)}, u32[]{:S(2)}) collective-permute-start(f32[8,128]{1,0:T(8,128)S(1)} %get-tuple-element.46), channel_id=1, source_target_pairs={{0,127},{1,2},{2,1},{3,4},{4,3},{5,6},{6,5},{7,8},{8,7},{9,10},{10... | collective-permute-start | bytes 12296 | tf_op jit(solution)/shard_map/ppermute | solution.py:605
  79.5 0.0 copy-done.5
  79.5 0.0 copy-done.11
  79.5 0.0 copy-done.13
  79.5 0.0 copy-done.7
  79.5 0.0 copy-done.9
  79.5 3.7 %shard_map.155 = (f32[64,1024]{1,0:T(8,128)S(1)}, bf16[2,384,128]{2,1,0:T(8,128)(2,1)S(1)}, f32[8,1024]{1,0:T(8,128)S(1)}, f32[512,128]{1,0:T(8,128)S(1)}, bf16[512,512]{1,0:T(8,128)(2,1)S(1)}) custom-call(s32[4]{0:T(128)S(1)} %pad_add_fusion.refs_0_.par_ref, f32[64,1024]{1,0:T(8,128)S(1)} %bitcast.26, s32[6,1024]{1,0:T(8,128)S(1)} %copy-done.11, ...), custom_call_target="tpu_custom_call" | custom-call | flops 134217728 | bytes 16777216 | tf_op jit(solution)/shard_map/pallas_call | solution.py:735
  83.3 0.0 collective-permute-done.4.ea_ref
  83.3 2.5 %collective-permute-done.5.eb_ref = f32[8,128]{1,0:T(8,128)S(1)} collective-permute-done((f32[8,128]{1,0:T(8,128)S(1)}, f32[8,128]{1,0:T(8,128)S(1)}, u32[]{:S(2)}, u32[]{:S(2)}) %collective-permute-start.5) | collective-permute-done | bytes 4128 | tf_op jit(solution)/shard_map/ppermute | solution.py:605
  85.8 1.9 %shard_map.156 = (f32[64,1024]{1,0:T(8,128)}, bf16[512,128]{1,0:T(8,128)(2,1)S(1)}) custom-call(s32[4]{0:T(128)S(1)} %pad_add_fusion.refs_0_.par_ref, f32[64,1024]{1,0:T(8,128)S(1)} %get-tuple-element.42.n2_ref, bf16[2,384,128]{2,1,0:T(8,128)(2,1)S(1)} %get-tuple-element.43.ends_ref, f32[8,1024]{1,0:T(8,128)S(1)} %get-tuple-element.44.sw_ref, ...), custom_call_target="tpu_custom_call" | custom-call | tf_op jit(solution)/shard_map/pallas_call | solution.py:748
  87.6 11.7 %all_to_all.15 = bf16[32,16,128]{2,1,0:T(8,128)(2,1)S(1)} all-to-all(bf16[32,16,128]{2,1,0:T(8,128)(2,1)S(1)} %bitcast.29), channel_id=1, replica_groups=mesh['tile'=32,'comp'=4] {'tile'}, dimensions={0} | all-to-all | bytes 262144 | tf_op jit(solution)/shard_map/all_to_all | solution.py:609
  99.3 0.9 shard_map.157
  (12 shorter events, 0.1 us)
Async XLA Ops:
  0.6 25.9 %copy-start.18 = (f32[12,4]{0,1:T(4,128)S(1)}, f32[12,4]{0,1:T(4,128)}, u32[]{:S(2)}) copy-start(f32[12,4]{0,1:T(4,128)} %param.16) | copy-start | bytes 580
  0.6 26.1 %copy-start.20 = (f32[2,16]{1,0:T(2,128)S(1)}, f32[2,16]{1,0:T(2,128)}, u32[]{:S(2)}) copy-start(f32[2,16]{1,0:T(2,128)} %param.14) | copy-start | bytes 388
  0.7 26.2 %copy-start.19 = (f32[4,12]{1,0:T(4,128)S(1)}, f32[4,12]{1,0:T(4,128)}, u32[]{:S(2)}) copy-start(f32[4,12]{1,0:T(4,128)} %param.23) | copy-start | bytes 580
  0.8 1.2 %copy-start = (f32[4,16,32,128]{3,2,1,0:T(8,128)S(1)}, f32[4,16,32,128]{3,2,1,0:T(8,128)}, u32[]{:S(2)}) copy-start(f32[4,16,32,128]{3,2,1,0:T(8,128)} %param.13) | copy-start | bytes 3145732
  2.0 0.9 copy-start.4
  2.9 0.8 copy-start.10
  3.7 0.8 copy-start.12
  4.5 0.7 copy-start.14
  5.2 16.9 %copy-start.1 = (f32[4,16,32,128]{3,2,1,0:T(8,128)S(1)}, f32[4,16,32,128]{3,2,1,0:T(8,128)}, u32[]{:S(2)}) copy-start(f32[4,16,32,128]{3,2,1,0:T(8,128)} %param.13) | copy-start | bytes 3145732
  6.0 14.6 %collective-permute-start.1 = (bf16[74,16,128]{2,1,0:T(8,128)(2,1)S(1)}, bf16[74,16,128]{2,1,0:T(8,128)(2,1)S(1)}, u32[]{:S(2)}, u32[]{:S(2)}) collective-permute-start(bf16[74,16,128]{2,1,0:T(8,128)(2,1)S(1)} %get-tuple-element.31.pb_ref), channel_id=1, source_target_pairs={{0,124},{4,8},{8,4},{12,16},{16,12},{20,24},{24,20},{28,32},{32,28... | collective-permute-start | bytes 909320 | tf_op jit(solution)/shard_map/ppermute | solution.py:605
  13.5 8.6 %collective-permute-start = (bf16[74,16,128]{2,1,0:T(8,128)(2,1)S(1)}, bf16[74,16,128]{2,1,0:T(8,128)(2,1)S(1)}, u32[]{:S(2)}, u32[]{:S(2)}) collective-permute-start(bf16[74,16,128]{2,1,0:T(8,128)(2,1)S(1)} %get-tuple-element.28.pa_ref), channel_id=1, source_target_pairs={{0,4},{4,0},{8,12},{12,8},{16,20},{20,16},{24,28},{28,24},{32,36},... | collective-permute-start | bytes 909320 | tf_op jit(solution)/shard_map/ppermute | solution.py:605
  13.5 0.7 copy-start.15
  22.1 11.5 %copy-start.17 = (f32[16,128]{1,0:T(8,128)S(1)}, f32[16,128]{1,0:T(8,128)}, u32[]{:S(2)}) copy-start(f32[16,128]{1,0:T(8,128)} %constant.31.clone.refs_6_) | copy-start | bytes 24580
  23.4 10.1 %collective-permute-start.2 = (bf16[672,128]{1,0:T(8,128)(2,1)S(1)}, bf16[672,128]{1,0:T(8,128)(2,1)S(1)}, u32[]{:S(2)}, u32[]{:S(2)}) collective-permute-start(bf16[672,128]{1,0:T(8,128)(2,1)S(1)} %get-tuple-element.35), channel_id=1, source_target_pairs={{0,1},{1,0},{2,3},{3,2},{4,5},{5,4},{6,7},{7,6},{8,9},{9,8},{10,11... | collective-permute-start | bytes 516104 | tf_op jit(solution)/shard_map/ppermute | solution.py:605
  23.5 10.0 %collective-permute-start.3 = (bf16[672,128]{1,0:T(8,128)(2,1)S(1)}, bf16[672,128]{1,0:T(8,128)(2,1)S(1)}, u32[]{:S(2)}, u32[]{:S(2)}) collective-permute-start(bf16[672,128]{1,0:T(8,128)(2,1)S(1)} %get-tuple-element.36), channel_id=1, source_target_pairs={{0,3},{1,2},{2,1},{3,0},{4,7},{5,6},{6,5},{7,4},{8,11},{9,10},{10,... | collective-permute-start | bytes 516104 | tf_op jit(solution)/shard_map/ppermute | solution.py:605
  27.0 29.4 %all-to-all-start = ((bf16[32,16,128]{2,1,0:T(8,128)(2,1)}), bf16[32,16,128]{2,1,0:T(8,128)(2,1)S(1)}, u32[]{:S(2)}, u32[]{:S(2)}) async-start(bf16[32,16,128]{2,1,0:T(8,128)(2,1)} %bitcast.7), calls=%async_computation | async-start | bytes 262144 | tf_op jit(solution)/shard_map/all_to_all | solution.py:609
  33.6 22.1 %copy-start.8 = (bf16[672,128]{1,0:T(8,128)(2,1)}, bf16[672,128]{1,0:T(8,128)(2,1)S(1)}, u32[]{:S(2)}) copy-start(bf16[672,128]{1,0:T(8,128)(2,1)S(1)} %collective-permute-done.3.refs_5_.yb_ref) | copy-start | bytes 516100
  33.6 1.2 %copy-start.16 = (bf16[2,256,640]{2,1,0:T(8,128)(2,1)S(1)}, bf16[2,256,640]{2,1,0:T(8,128)(2,1)}, u32[]{:S(2)}) copy-start(bf16[2,256,640]{2,1,0:T(8,128)(2,1)} %constant.30.clone.refs_7_) | copy-start | bytes 1966084
  34.7 30.7 %copy-start.2 = (bf16[8,8,128,128]{3,2,1,0:T(8,128)(2,1)S(1)}, bf16[8,8,128,128]{3,2,1,0:T(8,128)(2,1)}, u32[]{:S(2)}) copy-start(bf16[8,8,128,128]{3,2,1,0:T(8,128)(2,1)} %weights_ref.1) | copy-start | bytes 6291460
  55.7 0.7 copy-start.6
  56.3 23.2 %copy-start.5 = (f32[4,16,1024]{2,1,0:T(8,128)S(1)}, f32[4,16,1024]{2,1,0:T(8,128)}, u32[]{:S(2)}) copy-start(f32[4,16,1024]{2,1,0:T(8,128)} %param.20) | copy-start | bytes 786436
  56.3 23.2 %copy-start.11 = (s32[6,1024]{1,0:T(8,128)S(1)}, s32[6,1024]{1,0:T(8,128)}, u32[]{:S(2)}) copy-start(s32[6,1024]{1,0:T(8,128)} %off_ref.1) | copy-start | bytes 73732
  56.3 23.2 %copy-start.13 = (f32[6,1024]{1,0:T(8,128)S(1)}, f32[6,1024]{1,0:T(8,128)}, u32[]{:S(2)}) copy-start(f32[6,1024]{1,0:T(8,128)} %w_ref.1) | copy-start | bytes 73732
  57.2 17.0 %all-to-all-start.1 = ((bf16[32,16,128]{2,1,0:T(8,128)(2,1)}), bf16[32,16,128]{2,1,0:T(8,128)(2,1)S(1)}, u32[]{:S(2)}, u32[]{:S(2)}) async-start(bf16[32,16,128]{2,1,0:T(8,128)(2,1)} %bitcast.9), calls=%async_computation.1 | async-start | bytes 262144 | tf_op jit(solution)/shard_map/all_to_all | solution.py:609
  74.2 1.6 %copy-start.3 = (bf16[8,8,128,128]{3,2,1,0:T(8,128)(2,1)S(1)}, bf16[8,8,128,128]{3,2,1,0:T(8,128)(2,1)}, u32[]{:S(2)}) copy-start(bf16[8,8,128,128]{3,2,1,0:T(8,128)(2,1)} %param.18) | copy-start | bytes 6291460
  75.8 3.7 %copy-start.7 = (bf16[672,128]{1,0:T(8,128)(2,1)S(1)}, bf16[672,128]{1,0:T(8,128)(2,1)}, u32[]{:S(2)}) copy-start(bf16[672,128]{1,0:T(8,128)(2,1)} %copy-done.6) | copy-start | bytes 516100
  75.8 3.7 %copy-start.9 = (bf16[672,128]{1,0:T(8,128)(2,1)S(1)}, bf16[672,128]{1,0:T(8,128)(2,1)}, u32[]{:S(2)}) copy-start(bf16[672,128]{1,0:T(8,128)(2,1)} %copy-done.8) | copy-start | bytes 516100
  77.1 6.2 %collective-permute-start.4 = (f32[8,128]{1,0:T(8,128)S(1)}, f32[8,128]{1,0:T(8,128)S(1)}, u32[]{:S(2)}, u32[]{:S(2)}) collective-permute-start(f32[8,128]{1,0:T(8,128)S(1)} %get-tuple-element.45), channel_id=1, source_target_pairs={{0,1},{1,0},{2,3},{3,2},{4,5},{5,4},{6,7},{7,6},{8,9},{9,8},{10,11... | collective-permute-start | bytes 12296 | tf_op jit(solution)/shard_map/ppermute | solution.py:605
  77.2 8.5 %collective-permute-start.5 = (f32[8,128]{1,0:T(8,128)S(1)}, f32[8,128]{1,0:T(8,128)S(1)}, u32[]{:S(2)}, u32[]{:S(2)}) collective-permute-start(f32[8,128]{1,0:T(8,128)S(1)} %get-tuple-element.46), channel_id=1, source_target_pairs={{0,127},{1,2},{2,1},{3,4},{4,3},{5,6},{6,5},{7,8},{8,7},{9,10},{10... | collective-permute-start | bytes 12296 | tf_op jit(solution)/shard_map/ppermute | solution.py:605

commit v6 on v5

--- a/solution.py
+++ b/solution.py
@@ -726,6 +726,7 @@
     )
     rows = call(pick_kernel, S((512, 128), BF16), [VMEM] * 2)(served, table)
     mean_rows = to_tiles(rows)
+    mean_rows, return_weights = lax.optimization_barrier((mean_rows, return_weights))
     forcing, *edges = call(
         forcing_kernel,
         (S((8, 1024), F32), S((8, 128), F32), S((8, 128), F32)),

time: 101 us -> 99.4 us (0.984)
  blocking collectives: 11.7 us -> 28.7 us
  waiting for transfers between devices: 18.1 us -> 9.35 us
  starting transfers between devices: 26.8 us -> 18.5 us
    all_to_all x1 -> x2, blocking collectives: 11.7 us -> 28.7 us  [to_tiles(): lax.all_to_all(rows.reshape(N_TILE, 16, 128), 'tile', split_axis=0, conca...]
    all_to_all x2 -> x1, waiting for transfers between devices: 8.69 us -> 0.01 us  [to_tiles(): lax.all_to_all(rows.reshape(N_TILE, 16, 128), 'tile', split_axis=0, conca...]
    all_to_all x2 -> x1, starting transfers between devices: 13.9 us -> 5.58 us  [to_tiles(): lax.all_to_all(rows.reshape(N_TILE, 16, 128), 'tile', split_axis=0, conca...]
    unnamed x43 -> x35, local copies, waits for them, and re-layouts: 8.63 us -> 7.9 us
  transfers between devices with their start and end apart: 8 -> 7, of which waited for: 4 -> 3; matrix products, arithmetic and copies ran while one was open for 0% -> 0% of each run, Pallas kernels for 27% -> 27%
where the time goes in v6:
time: 99.4 us; the launch traced here: 98.8 us
  Pallas kernels  33.1 us (33%)
  blocking collectives  28.7 us (29%)
  starting transfers between devices  18.5 us (19%)
  waiting for transfers between devices  9.35 us (9%)
  local copies, waits for them, and re-layouts  8.18 us (8%)
    all_to_all x2, blocking collectives, to_tiles(): lax.all_to_all(rows.reshape(N_TILE, 16, 128), 'tile', split_axis=0, conca...  28.7 us
    pallas_call x2, Pallas kernels, staged(): call(body, out, specs, scratch_shapes, mib, cost)  21.8 us
    ppermute x3, starting transfers between devices, exchange(): lax.ppermute(payloads[1], axis, far)  12.7 us
    unnamed x35, local copies, waits for them, and re-layouts  7.9 us
    ppermute x3, waiting for transfers between devices, exchange(): lax.ppermute(payloads[1], axis, far)  7.88 us
    all_to_all x1, starting transfers between devices, to_tiles(): lax.all_to_all(rows.reshape(N_TILE, 16, 128), 'tile', split_axis=0, conca...  5.58 us
    pallas_call x1, Pallas kernels, per_device(): call(ocean_kernel, (S((64, 1024), F32), S((2, 384, 128), BF16), S((8, 102...  3.74 us
  transfers between devices with their start and end apart: 7, of which 3 were waited for; matrix products, arithmetic and copies ran while one was open for 0% of the time, Pallas kernels for 27%

profile of v6, /device:TPU:0, one launch (start us, length us, event | category | flops | bytes accessed | tf_op | source)
XLA Modules:
  0.0 98.8 jit_solution(18124766133312463787)
XLA Ops:
  0.6 0.0 copy-start.16
  0.6 0.0 copy-start.15
  0.7 0.0 copy-start.14
  0.7 0.1 pad_add_fusion.refs_0_.par_ref
  0.8 0.0 copy-start
  0.8 1.2 %copy-done = f32[4,16,32,128]{3,2,1,0:T(8,128)S(1)} copy-done((f32[4,16,32,128]{3,2,1,0:T(8,128)S(1)}, f32[4,16,32,128]{3,2,1,0:T(8,128)}, u32[]{:S(2)}) %copy-start) | copy-done | bytes 1048600
  2.0 0.0 copy-start.4
  2.0 0.9 copy-done.4
  2.9 0.0 copy-start.6
  2.9 0.8 copy-done.6
  3.7 0.0 copy-start.8
  3.7 0.8 copy-done.8
  4.5 0.0 copy-start.10
  4.5 0.7 copy-done.10
  5.2 0.0 copy-start.1
  5.2 0.9 shard_map.148
  6.0 7.4 %collective-permute-start.1 = (bf16[74,16,128]{2,1,0:T(8,128)(2,1)S(1)}, bf16[74,16,128]{2,1,0:T(8,128)(2,1)S(1)}, u32[]{:S(2)}, u32[]{:S(2)}) collective-permute-start(bf16[74,16,128]{2,1,0:T(8,128)(2,1)S(1)} %get-tuple-element.33.pb_ref), channel_id=1, source_target_pairs={{0,124},{4,8},{8,4},{12,16},{16,12},{20,24},{24,20},{28,32},{32,28... | collective-permute-start | bytes 909320 | tf_op jit(solution)/shard_map/ppermute | solution.py:605
  13.5 0.0 collective-permute-start
  13.5 0.0 copy-start.11
  13.5 0.7 copy-done.11
  14.1 1.0 %shard_map.149 = (bf16[512,128]{1,0:T(8,128)(2,1)}, s32[512,128]{1,0:T(8,128)S(1)}) custom-call(s32[8,8]{1,0:T(8,128)S(1)} %copy-done.11), custom_call_target="tpu_custom_call" | custom-call | tf_op jit(solution)/shard_map/pallas_call | solution.py:697
  15.2 5.5 %collective-permute-done.1.xb_ref = bf16[74,16,128]{2,1,0:T(8,128)(2,1)S(1)} collective-permute-done((bf16[74,16,128]{2,1,0:T(8,128)(2,1)S(1)}, bf16[74,16,128]{2,1,0:T(8,128)(2,1)S(1)}, u32[]{:S(2)}, u32[]{:S(2)}) %collective-permute-start.1) | collective-permute-done | bytes 303136 | tf_op jit(solution)/shard_map/ppermute | solution.py:605
  20.6 1.5 %collective-permute-done.xa_ref = bf16[74,16,128]{2,1,0:T(8,128)(2,1)S(1)} collective-permute-done((bf16[74,16,128]{2,1,0:T(8,128)(2,1)S(1)}, bf16[74,16,128]{2,1,0:T(8,128)(2,1)S(1)}, u32[]{:S(2)}, u32[]{:S(2)}) %collective-permute-start) | collective-permute-done | bytes 303136 | tf_op jit(solution)/shard_map/ppermute | solution.py:605
  22.1 0.0 copy-done.1
  22.1 0.0 copy-start.13
  22.1 1.3 %shard_map.151 = (bf16[672,128]{1,0:T(8,128)(2,1)S(1)}, bf16[672,128]{1,0:T(8,128)(2,1)S(1)}) custom-call(s32[4]{0:T(128)S(1)} %pad_add_fusion.refs_0_.par_ref, f32[64,32,128]{2,1,0:T(8,128)S(1)} %bitcast.20, f32[32,128]{1,0:T(8,128)S(1)} %get-tuple-element.29.flags_ref, bf16[74,16,128]{2,1,0:T(8,128)(2,1)S(1)} %collective-permute-done.xa_ref, ...), custom_call_target="tpu_custom_call" | custom-call | tf_op jit(solution)/shard_map/pallas_call | solution.py:702
  23.4 0.1 collective-permute-start.2
  23.5 3.0 %collective-permute-start.3 = (bf16[672,128]{1,0:T(8,128)(2,1)S(1)}, bf16[672,128]{1,0:T(8,128)(2,1)S(1)}, u32[]{:S(2)}, u32[]{:S(2)}) collective-permute-start(bf16[672,128]{1,0:T(8,128)(2,1)S(1)} %get-tuple-element.38), channel_id=1, source_target_pairs={{0,3},{1,2},{2,1},{3,0},{4,7},{5,6},{6,5},{7,4},{8,11},{9,10},{10,... | collective-permute-start | bytes 516104 | tf_op jit(solution)/shard_map/ppermute | solution.py:605
  26.5 0.0 copy-done.16
  26.5 0.1 reshape.48
  26.6 0.0 copy-done.15
  26.6 0.1 reshape.50
  26.7 0.0 copy-done.14
  26.7 0.1 copy.17
  26.8 0.1 reshape.49
  26.9 0.1 pad_maximum_fusion.refs_1_
  27.0 5.6 %all-to-all-start = ((bf16[32,16,128]{2,1,0:T(8,128)(2,1)}), bf16[32,16,128]{2,1,0:T(8,128)(2,1)S(1)}, u32[]{:S(2)}, u32[]{:S(2)}) async-start(bf16[32,16,128]{2,1,0:T(8,128)(2,1)} %bitcast.7), calls=%async_computation | async-start | bytes 262144 | tf_op jit(solution)/shard_map/all_to_all | solution.py:609
  32.5 1.0 %shard_map.150 = (bf16[16,4,4,16,256]{4,3,2,1,0:T(8,128)(2,1)S(1)}, f32[4,16,128]{2,1,0:T(8,128)S(1)}) custom-call(s32[4]{0:T(128)S(1)} %pad_add_fusion.refs_0_.par_ref, f32[64,32,128]{2,1,0:T(8,128)S(1)} %bitcast.21, f32[32,128]{1,0:T(8,128)S(1)} %get-tuple-element.29.flags_ref, bf16[74,16,128]{2,1,0:T(8,128)(2,1)S(1)} %collective-permute-done.xa_ref, ...), custom_call_target="tpu_custom_call" | custom-call | flops 8388608 | bytes 8388608 | tf_op jit(solution)/shard_map/pallas_call | solution.py:709
  33.5 0.0 collective-permute-done.2.refs_4_.ya_ref
  33.5 0.0 collective-permute-done.3.refs_5_.yb_ref
  33.6 0.0 copy-done.13
  33.6 0.0 copy-start.12
  33.6 1.1 %copy-done.12 = bf16[2,256,640]{2,1,0:T(8,128)(2,1)S(1)} copy-done((bf16[2,256,640]{2,1,0:T(8,128)(2,1)S(1)}, bf16[2,256,640]{2,1,0:T(8,128)(2,1)}, u32[]{:S(2)}) %copy-start.12) | copy-done | bytes 655384
  34.7 0.0 copy-start.5
  34.7 0.0 copy-start.7
  34.7 20.9 %shard_map.152 = (f32[64,32,128]{2,1,0:T(8,128)}, bf16[128,128]{1,0:T(8,128)(2,1)S(1)}) custom-call(s32[4]{0:T(128)S(1)} %pad_add_fusion.refs_0_.par_ref, f32[128]{0:T(128)S(1)} %pad_maximum_fusion.refs_1_, bf16[16,4,4,16,256]{4,3,2,1,0:T(8,128)(2,1)S(1)} %get-tuple-element.35.refs_2_, f32[4,16,128]{2,1,0:T(8,128)S(1)} %get-tuple-element.36.refs_3_, ...), custom_call_target="tpu_custom_call" | custom-call | flops 8589934592 | bytes 67108864 | tf_op jit(solution)/shard_map/pallas_call | solution.py:646
  55.6 0.0 copy-start.2
  55.6 0.0 all-to-all-done
  55.6 0.2 shard_map.153
  55.8 17.0 %all_to_all.15 = bf16[32,16,128]{2,1,0:T(8,128)(2,1)S(1)} all-to-all(bf16[32,16,128]{2,1,0:T(8,128)(2,1)S(1)} %bitcast.28), channel_id=1, replica_groups=mesh['tile'=32,'comp'=4] {'tile'}, dimensions={0} | all-to-all | bytes 262144 | tf_op jit(solution)/shard_map/all_to_all | solution.py:609
  72.8 1.6 %copy-done.3 = bf16[8,8,128,128]{3,2,1,0:T(8,128)(2,1)S(1)} copy-done((bf16[8,8,128,128]{3,2,1,0:T(8,128)(2,1)S(1)}, bf16[8,8,128,128]{3,2,1,0:T(8,128)(2,1)}, u32[]{:S(2)}) %copy-start.3) | copy-done | bytes 2097176
  74.4 1.3 %shard_map.154 = (f32[8,1024]{1,0:T(8,128)S(1)}, f32[8,128]{1,0:T(8,128)S(1)}, f32[8,128]{1,0:T(8,128)S(1)}) custom-call(s32[4]{0:T(128)S(1)} %pad_add_fusion.refs_0_.par_ref, bf16[512,128]{1,0:T(8,128)(2,1)S(1)} %bitcast.29, s32[512,128]{1,0:T(8,128)S(1)} %get-tuple-element.43.tcol_ref, bf16[8,1024,128]{2,1,0:T(8,128)(2,1)S(1)} %bitcast.22), custom_call_target="tpu_custom_call" | custom-call | tf_op jit(solution)/shard_map/pallas_call | solution.py:730
  75.7 0.1 collective-permute-start.4
  75.8 2.3 %collective-permute-start.5 = (f32[8,128]{1,0:T(8,128)S(1)}, f32[8,128]{1,0:T(8,128)S(1)}, u32[]{:S(2)}, u32[]{:S(2)}) collective-permute-start(f32[8,128]{1,0:T(8,128)S(1)} %get-tuple-element.50), channel_id=1, source_target_pairs={{0,127},{1,2},{2,1},{3,4},{4,3},{5,6},{6,5},{7,8},{8,7},{9,10},{10... | collective-permute-start | bytes 12296 | tf_op jit(solution)/shard_map/ppermute | solution.py:605
  78.1 0.0 copy-done.2
  78.1 0.0 copy-done.5
  78.1 0.0 copy-done.7
  78.1 0.0 copy-done.9
  78.1 3.7 %shard_map.155 = (f32[64,1024]{1,0:T(8,128)S(1)}, bf16[2,384,128]{2,1,0:T(8,128)(2,1)S(1)}, f32[8,1024]{1,0:T(8,128)S(1)}, f32[512,128]{1,0:T(8,128)S(1)}, bf16[512,512]{1,0:T(8,128)(2,1)S(1)}) custom-call(s32[4]{0:T(128)S(1)} %pad_add_fusion.refs_0_.par_ref, f32[64,1024]{1,0:T(8,128)S(1)} %bitcast.26, s32[6,1024]{1,0:T(8,128)S(1)} %copy-done.7, ...), custom_call_target="tpu_custom_call" | custom-call | flops 134217728 | bytes 16777216 | tf_op jit(solution)/shard_map/pallas_call | solution.py:736
  81.9 0.0 collective-permute-done.4.ea_ref
  81.9 2.4 %collective-permute-done.5.eb_ref = f32[8,128]{1,0:T(8,128)S(1)} collective-permute-done((f32[8,128]{1,0:T(8,128)S(1)}, f32[8,128]{1,0:T(8,128)S(1)}, u32[]{:S(2)}, u32[]{:S(2)}) %collective-permute-start.5) | collective-permute-done | bytes 4128 | tf_op jit(solution)/shard_map/ppermute | solution.py:605
  84.3 1.9 %shard_map.156 = (f32[64,1024]{1,0:T(8,128)}, bf16[512,128]{1,0:T(8,128)(2,1)S(1)}) custom-call(s32[4]{0:T(128)S(1)} %pad_add_fusion.refs_0_.par_ref, f32[64,1024]{1,0:T(8,128)S(1)} %get-tuple-element.46.n2_ref, bf16[2,384,128]{2,1,0:T(8,128)(2,1)S(1)} %get-tuple-element.47.ends_ref, f32[8,1024]{1,0:T(8,128)S(1)} %get-tuple-element.48.sw_ref, ...), custom_call_target="tpu_custom_call" | custom-call | tf_op jit(solution)/shard_map/pallas_call | solution.py:749
  86.2 11.7 %all_to_all.16 = bf16[32,16,128]{2,1,0:T(8,128)(2,1)S(1)} all-to-all(bf16[32,16,128]{2,1,0:T(8,128)(2,1)S(1)} %bitcast.30), channel_id=1, replica_groups=mesh['tile'=32,'comp'=4] {'tile'}, dimensions={0} | all-to-all | bytes 262144 | tf_op jit(solution)/shard_map/all_to_all | solution.py:609
  97.9 0.9 shard_map.157
  (3 shorter events, 0.0 us)
Async XLA Ops:
  0.6 25.9 %copy-start.16 = (f32[2,16]{1,0:T(2,128)S(1)}, f32[2,16]{1,0:T(2,128)}, u32[]{:S(2)}) copy-start(f32[2,16]{1,0:T(2,128)} %param.14) | copy-start | bytes 388
  0.6 26.0 %copy-start.15 = (f32[4,12]{1,0:T(4,128)S(1)}, f32[4,12]{1,0:T(4,128)}, u32[]{:S(2)}) copy-start(f32[4,12]{1,0:T(4,128)} %param.23) | copy-start | bytes 580
  0.7 26.0 %copy-start.14 = (f32[12,4]{0,1:T(4,128)S(1)}, f32[12,4]{0,1:T(4,128)}, u32[]{:S(2)}) copy-start(f32[12,4]{0,1:T(4,128)} %param.16) | copy-start | bytes 580
  0.8 1.2 %copy-start = (f32[4,16,32,128]{3,2,1,0:T(8,128)S(1)}, f32[4,16,32,128]{3,2,1,0:T(8,128)}, u32[]{:S(2)}) copy-start(f32[4,16,32,128]{3,2,1,0:T(8,128)} %param.13) | copy-start | bytes 3145732
  2.0 0.9 copy-start.4
  2.9 0.8 copy-start.6
  3.7 0.8 copy-start.8
  4.5 0.7 copy-start.10
  5.2 16.9 %copy-start.1 = (f32[4,16,32,128]{3,2,1,0:T(8,128)S(1)}, f32[4,16,32,128]{3,2,1,0:T(8,128)}, u32[]{:S(2)}) copy-start(f32[4,16,32,128]{3,2,1,0:T(8,128)} %param.13) | copy-start | bytes 3145732
  6.0 14.6 %collective-permute-start.1 = (bf16[74,16,128]{2,1,0:T(8,128)(2,1)S(1)}, bf16[74,16,128]{2,1,0:T(8,128)(2,1)S(1)}, u32[]{:S(2)}, u32[]{:S(2)}) collective-permute-start(bf16[74,16,128]{2,1,0:T(8,128)(2,1)S(1)} %get-tuple-element.33.pb_ref), channel_id=1, source_target_pairs={{0,124},{4,8},{8,4},{12,16},{16,12},{20,24},{24,20},{28,32},{32,28... | collective-permute-start | bytes 909320 | tf_op jit(solution)/shard_map/ppermute | solution.py:605
  13.5 8.6 %collective-permute-start = (bf16[74,16,128]{2,1,0:T(8,128)(2,1)S(1)}, bf16[74,16,128]{2,1,0:T(8,128)(2,1)S(1)}, u32[]{:S(2)}, u32[]{:S(2)}) collective-permute-start(bf16[74,16,128]{2,1,0:T(8,128)(2,1)S(1)} %get-tuple-element.30.pa_ref), channel_id=1, source_target_pairs={{0,4},{4,0},{8,12},{12,8},{16,20},{20,16},{24,28},{28,24},{32,36},... | collective-permute-start | bytes 909320 | tf_op jit(solution)/shard_map/ppermute | solution.py:605
  13.5 0.7 copy-start.11
  22.1 11.5 %copy-start.13 = (f32[16,128]{1,0:T(8,128)S(1)}, f32[16,128]{1,0:T(8,128)}, u32[]{:S(2)}) copy-start(f32[16,128]{1,0:T(8,128)} %constant.31.clone.refs_6_) | copy-start | bytes 24580
  23.4 10.1 %collective-permute-start.2 = (bf16[672,128]{1,0:T(8,128)(2,1)S(1)}, bf16[672,128]{1,0:T(8,128)(2,1)S(1)}, u32[]{:S(2)}, u32[]{:S(2)}) collective-permute-start(bf16[672,128]{1,0:T(8,128)(2,1)S(1)} %get-tuple-element.37), channel_id=1, source_target_pairs={{0,1},{1,0},{2,3},{3,2},{4,5},{5,4},{6,7},{7,6},{8,9},{9,8},{10,11... | collective-permute-start | bytes 516104 | tf_op jit(solution)/shard_map/ppermute | solution.py:605
  23.5 10.0 %collective-permute-start.3 = (bf16[672,128]{1,0:T(8,128)(2,1)S(1)}, bf16[672,128]{1,0:T(8,128)(2,1)S(1)}, u32[]{:S(2)}, u32[]{:S(2)}) collective-permute-start(bf16[672,128]{1,0:T(8,128)(2,1)S(1)} %get-tuple-element.38), channel_id=1, source_target_pairs={{0,3},{1,2},{2,1},{3,0},{4,7},{5,6},{6,5},{7,4},{8,11},{9,10},{10,... | collective-permute-start | bytes 516104 | tf_op jit(solution)/shard_map/ppermute | solution.py:605
  27.0 28.6 %all-to-all-start = ((bf16[32,16,128]{2,1,0:T(8,128)(2,1)}), bf16[32,16,128]{2,1,0:T(8,128)(2,1)S(1)}, u32[]{:S(2)}, u32[]{:S(2)}) async-start(bf16[32,16,128]{2,1,0:T(8,128)(2,1)} %bitcast.7), calls=%async_computation | async-start | bytes 262144 | tf_op jit(solution)/shard_map/all_to_all | solution.py:609
  33.6 1.1 %copy-start.12 = (bf16[2,256,640]{2,1,0:T(8,128)(2,1)S(1)}, bf16[2,256,640]{2,1,0:T(8,128)(2,1)}, u32[]{:S(2)}) copy-start(bf16[2,256,640]{2,1,0:T(8,128)(2,1)} %constant.30.clone.refs_7_) | copy-start | bytes 1966084
  34.7 43.5 %copy-start.5 = (f32[4,16,1024]{2,1,0:T(8,128)S(1)}, f32[4,16,1024]{2,1,0:T(8,128)}, u32[]{:S(2)}) copy-start(f32[4,16,1024]{2,1,0:T(8,128)} %param.20) | copy-start | bytes 786436
  34.7 43.5 %copy-start.7 = (s32[6,1024]{1,0:T(8,128)S(1)}, s32[6,1024]{1,0:T(8,128)}, u32[]{:S(2)}) copy-start(s32[6,1024]{1,0:T(8,128)} %off_ref.1) | copy-start | bytes 73732
  34.7 43.5 %copy-start.9 = (f32[6,1024]{1,0:T(8,128)S(1)}, f32[6,1024]{1,0:T(8,128)}, u32[]{:S(2)}) copy-start(f32[6,1024]{1,0:T(8,128)} %w_ref.1) | copy-start | bytes 73732
  55.6 22.5 %copy-start.2 = (bf16[8,8,128,128]{3,2,1,0:T(8,128)(2,1)S(1)}, bf16[8,8,128,128]{3,2,1,0:T(8,128)(2,1)}, u32[]{:S(2)}) copy-start(bf16[8,8,128,128]{3,2,1,0:T(8,128)(2,1)} %weights_ref) | copy-start | bytes 6291460
  72.8 1.6 %copy-start.3 = (bf16[8,8,128,128]{3,2,1,0:T(8,128)(2,1)S(1)}, bf16[8,8,128,128]{3,2,1,0:T(8,128)(2,1)}, u32[]{:S(2)}) copy-start(bf16[8,8,128,128]{3,2,1,0:T(8,128)(2,1)} %param.18) | copy-start | bytes 6291460
  75.7 6.2 %collective-permute-start.4 = (f32[8,128]{1,0:T(8,128)S(1)}, f32[8,128]{1,0:T(8,128)S(1)}, u32[]{:S(2)}, u32[]{:S(2)}) collective-permute-start(f32[8,128]{1,0:T(8,128)S(1)} %get-tuple-element.49), channel_id=1, source_target_pairs={{0,1},{1,0},{2,3},{3,2},{4,5},{5,4},{6,7},{7,6},{8,9},{9,8},{10,11... | collective-permute-start | bytes 12296 | tf_op jit(solution)/shard_map/ppermute | solution.py:605
  75.8 8.5 %collective-permute-start.5 = (f32[8,128]{1,0:T(8,128)S(1)}, f32[8,128]{1,0:T(8,128)S(1)}, u32[]{:S(2)}, u32[]{:S(2)}) collective-permute-start(f32[8,128]{1,0:T(8,128)S(1)} %get-tuple-element.50), channel_id=1, source_target_pairs={{0,127},{1,2},{2,1},{3,4},{4,3},{5,6},{6,5},{7,8},{8,7},{9,10},{10... | collective-permute-start | bytes 12296 | tf_op jit(solution)/shard_map/ppermute | solution.py:605

commit v7 on v6

--- a/solution.py
+++ b/solution.py
@@ -427,7 +427,7 @@
     table_ref[...] = gs_ref[...].reshape(128, 128).astype(BF16)
 
 
-def pick_kernel(served_ref, table_ref, rows_ref):
+def pick_kernel(served_ref, table_ref, weights_ref, rows_ref):
     pick = served_ref[...].astype(F32) == iota((512, 128), 1).astype(F32)
     rows_ref[...] = mm(jnp.where(pick, 1.0, 0.0).astype(BF16), table_ref[...]).astype(BF16)
 
@@ -724,7 +724,9 @@
         mib=32,
         cost=pl.CostEstimate(flops=2**33, bytes_accessed=2**26, transcendentals=0),
     )
-    rows = call(pick_kernel, S((512, 128), BF16), [VMEM] * 2)(served, table)
+    rows = call(pick_kernel, S((512, 128), BF16), [VMEM] * 3)(
+        served, table, regrid_weights.reshape(8, 1024, 128)
+    )
     mean_rows = to_tiles(rows)
     mean_rows, return_weights = lax.optimization_barrier((mean_rows, return_weights))
     forcing, *edges = call(

time: 99.4 us -> 97.8 us (0.984)
  local copies, waits for them, and re-layouts: 8.18 us -> 6.6 us
    unnamed x35, local copies, waits for them, and re-layouts: 7.9 us -> 6.32 us
where the time goes in v7:
time: 97.8 us; the launch traced here: 97.2 us
  Pallas kernels  33.1 us (34%)
  blocking collectives  28.7 us (29%)
  starting transfers between devices  18.5 us (19%)
  waiting for transfers between devices  9.3 us (10%)
  local copies, waits for them, and re-layouts  6.6 us (7%)
    all_to_all x2, blocking collectives, to_tiles(): lax.all_to_all(rows.reshape(N_TILE, 16, 128), 'tile', split_axis=0, conca...  28.7 us
    pallas_call x2, Pallas kernels, staged(): call(body, out, specs, scratch_shapes, mib, cost)  21.8 us
    ppermute x3, starting transfers between devices, exchange(): lax.ppermute(payloads[1], axis, far)  12.8 us
    ppermute x3, waiting for transfers between devices, exchange(): lax.ppermute(payloads[1], axis, far)  7.83 us
    unnamed x35, local copies, waits for them, and re-layouts  6.32 us
    all_to_all x1, starting transfers between devices, to_tiles(): lax.all_to_all(rows.reshape(N_TILE, 16, 128), 'tile', split_axis=0, conca...  5.58 us
    pallas_call x1, Pallas kernels, per_device(): call(ocean_kernel, (S((64, 1024), F32), S((2, 384, 128), BF16), S((8, 102...  3.75 us
  transfers between devices with their start and end apart: 7, of which 3 were waited for; matrix products, arithmetic and copies ran while one was open for 0% of the time, Pallas kernels for 27%

profile of v7, /device:TPU:0, one launch (start us, length us, event | category | flops | bytes accessed | tf_op | source)
XLA Modules:
  0.0 97.2 jit_solution(4086688330574310559)
XLA Ops:
  0.6 0.0 copy-start.16
  0.6 0.0 copy-start.15
  0.7 0.0 copy-start.14
  0.7 0.1 pad_add_fusion.refs_0_.par_ref
  0.8 0.0 copy-start
  0.8 1.2 %copy-done = f32[4,16,32,128]{3,2,1,0:T(8,128)S(1)} copy-done((f32[4,16,32,128]{3,2,1,0:T(8,128)S(1)}, f32[4,16,32,128]{3,2,1,0:T(8,128)}, u32[]{:S(2)}) %copy-start) | copy-done | bytes 1048600
  2.0 0.0 copy-start.4
  2.0 0.9 copy-done.4
  2.9 0.0 copy-start.6
  2.9 0.8 copy-done.6
  3.7 0.0 copy-start.8
  3.7 0.8 copy-done.8
  4.5 0.0 copy-start.10
  4.5 0.7 copy-done.10
  5.2 0.0 copy-start.1
  5.2 0.9 shard_map.148
  6.0 7.4 %collective-permute-start.1 = (bf16[74,16,128]{2,1,0:T(8,128)(2,1)S(1)}, bf16[74,16,128]{2,1,0:T(8,128)(2,1)S(1)}, u32[]{:S(2)}, u32[]{:S(2)}) collective-permute-start(bf16[74,16,128]{2,1,0:T(8,128)(2,1)S(1)} %get-tuple-element.33.pb_ref), channel_id=1, source_target_pairs={{0,124},{4,8},{8,4},{12,16},{16,12},{20,24},{24,20},{28,32},{32,28... | collective-permute-start | bytes 909320 | tf_op jit(solution)/shard_map/ppermute | solution.py:605
  13.5 0.0 collective-permute-start
  13.5 0.0 copy-start.11
  13.5 0.7 copy-done.11
  14.1 1.0 %shard_map.149 = (bf16[512,128]{1,0:T(8,128)(2,1)}, s32[512,128]{1,0:T(8,128)S(1)}) custom-call(s32[8,8]{1,0:T(8,128)S(1)} %copy-done.11), custom_call_target="tpu_custom_call" | custom-call | tf_op jit(solution)/shard_map/pallas_call | solution.py:697
  15.2 5.5 %collective-permute-done.1.xb_ref = bf16[74,16,128]{2,1,0:T(8,128)(2,1)S(1)} collective-permute-done((bf16[74,16,128]{2,1,0:T(8,128)(2,1)S(1)}, bf16[74,16,128]{2,1,0:T(8,128)(2,1)S(1)}, u32[]{:S(2)}, u32[]{:S(2)}) %collective-permute-start.1) | collective-permute-done | bytes 303136 | tf_op jit(solution)/shard_map/ppermute | solution.py:605
  20.6 1.5 %collective-permute-done.xa_ref = bf16[74,16,128]{2,1,0:T(8,128)(2,1)S(1)} collective-permute-done((bf16[74,16,128]{2,1,0:T(8,128)(2,1)S(1)}, bf16[74,16,128]{2,1,0:T(8,128)(2,1)S(1)}, u32[]{:S(2)}, u32[]{:S(2)}) %collective-permute-start) | collective-permute-done | bytes 303136 | tf_op jit(solution)/shard_map/ppermute | solution.py:605
  22.1 0.0 copy-done.1
  22.1 1.3 %shard_map.151 = (bf16[672,128]{1,0:T(8,128)(2,1)S(1)}, bf16[672,128]{1,0:T(8,128)(2,1)S(1)}) custom-call(s32[4]{0:T(128)S(1)} %pad_add_fusion.refs_0_.par_ref, f32[64,32,128]{2,1,0:T(8,128)S(1)} %bitcast.20, f32[32,128]{1,0:T(8,128)S(1)} %get-tuple-element.29.flags_ref, bf16[74,16,128]{2,1,0:T(8,128)(2,1)S(1)} %collective-permute-done.xa_ref, ...), custom_call_target="tpu_custom_call" | custom-call | tf_op jit(solution)/shard_map/pallas_call | solution.py:702
  23.4 0.1 collective-permute-start.2
  23.5 3.0 %collective-permute-start.3 = (bf16[672,128]{1,0:T(8,128)(2,1)S(1)}, bf16[672,128]{1,0:T(8,128)(2,1)S(1)}, u32[]{:S(2)}, u32[]{:S(2)}) collective-permute-start(bf16[672,128]{1,0:T(8,128)(2,1)S(1)} %get-tuple-element.38), channel_id=1, source_target_pairs={{0,3},{1,2},{2,1},{3,0},{4,7},{5,6},{6,5},{7,4},{8,11},{9,10},{10,... | collective-permute-start | bytes 516104 | tf_op jit(solution)/shard_map/ppermute | solution.py:605
  26.5 0.0 copy-done.16
  26.5 0.1 reshape.49
  26.6 0.0 copy-done.15
  26.6 0.1 reshape.51
  26.7 0.0 copy-done.14
  26.7 0.1 copy.17
  26.8 0.1 reshape.50
  26.9 0.1 pad_maximum_fusion.refs_1_
  27.0 5.6 %all-to-all-start = ((bf16[32,16,128]{2,1,0:T(8,128)(2,1)}), bf16[32,16,128]{2,1,0:T(8,128)(2,1)S(1)}, u32[]{:S(2)}, u32[]{:S(2)}) async-start(bf16[32,16,128]{2,1,0:T(8,128)(2,1)} %bitcast.7), calls=%async_computation | async-start | bytes 262144 | tf_op jit(solution)/shard_map/all_to_all | solution.py:609
  32.5 1.0 %shard_map.150 = (bf16[16,4,4,16,256]{4,3,2,1,0:T(8,128)(2,1)S(1)}, f32[4,16,128]{2,1,0:T(8,128)S(1)}) custom-call(s32[4]{0:T(128)S(1)} %pad_add_fusion.refs_0_.par_ref, f32[64,32,128]{2,1,0:T(8,128)S(1)} %bitcast.21, f32[32,128]{1,0:T(8,128)S(1)} %get-tuple-element.29.flags_ref, bf16[74,16,128]{2,1,0:T(8,128)(2,1)S(1)} %collective-permute-done.xa_ref, ...), custom_call_target="tpu_custom_call" | custom-call | flops 8388608 | bytes 8388608 | tf_op jit(solution)/shard_map/pallas_call | solution.py:709
  33.5 0.0 collective-permute-done.2.refs_4_.ya_ref
  33.5 0.0 collective-permute-done.3.refs_5_.yb_ref
  33.6 0.0 copy-done.13
  33.6 0.0 copy-start.12
  33.6 1.1 %copy-done.12 = bf16[2,256,640]{2,1,0:T(8,128)(2,1)S(1)} copy-done((bf16[2,256,640]{2,1,0:T(8,128)(2,1)S(1)}, bf16[2,256,640]{2,1,0:T(8,128)(2,1)}, u32[]{:S(2)}) %copy-start.12) | copy-done | bytes 655384
  34.7 20.9 %shard_map.152 = (f32[64,32,128]{2,1,0:T(8,128)}, bf16[128,128]{1,0:T(8,128)(2,1)S(1)}) custom-call(s32[4]{0:T(128)S(1)} %pad_add_fusion.refs_0_.par_ref, f32[128]{0:T(128)S(1)} %pad_maximum_fusion.refs_1_, bf16[16,4,4,16,256]{4,3,2,1,0:T(8,128)(2,1)S(1)} %get-tuple-element.35.refs_2_, f32[4,16,128]{2,1,0:T(8,128)S(1)} %get-tuple-element.36.refs_3_, ...), custom_call_target="tpu_custom_call" | custom-call | flops 8589934592 | bytes 67108864 | tf_op jit(solution)/shard_map/pallas_call | solution.py:646
  55.6 0.0 all-to-all-done
  55.6 0.0 copy-done.2
  55.6 0.0 copy-start.3
  55.6 0.2 shard_map.153
  55.8 0.0 copy-start.5
  55.8 0.0 copy-start.7
  55.8 0.0 copy-start.9
  55.8 17.0 %all_to_all.15 = bf16[32,16,128]{2,1,0:T(8,128)(2,1)S(1)} all-to-all(bf16[32,16,128]{2,1,0:T(8,128)(2,1)S(1)} %bitcast.28), channel_id=1, replica_groups=mesh['tile'=32,'comp'=4] {'tile'}, dimensions={0} | all-to-all | bytes 262144 | tf_op jit(solution)/shard_map/all_to_all | solution.py:609
  72.8 1.3 %shard_map.154 = (f32[8,1024]{1,0:T(8,128)S(1)}, f32[8,128]{1,0:T(8,128)S(1)}, f32[8,128]{1,0:T(8,128)S(1)}) custom-call(s32[4]{0:T(128)S(1)} %pad_add_fusion.refs_0_.par_ref, bf16[512,128]{1,0:T(8,128)(2,1)S(1)} %bitcast.30, s32[512,128]{1,0:T(8,128)S(1)} %get-tuple-element.43.tcol_ref, bf16[8,1024,128]{2,1,0:T(8,128)(2,1)S(1)} %bitcast.23), custom_call_target="tpu_custom_call" | custom-call | tf_op jit(solution)/shard_map/pallas_call | solution.py:732
  74.1 0.1 collective-permute-start.4
  74.2 2.3 %collective-permute-start.5 = (f32[8,128]{1,0:T(8,128)S(1)}, f32[8,128]{1,0:T(8,128)S(1)}, u32[]{:S(2)}, u32[]{:S(2)}) collective-permute-start(f32[8,128]{1,0:T(8,128)S(1)} %get-tuple-element.50), channel_id=1, source_target_pairs={{0,127},{1,2},{2,1},{3,4},{4,3},{5,6},{6,5},{7,8},{8,7},{9,10},{10... | collective-permute-start | bytes 12296 | tf_op jit(solution)/shard_map/ppermute | solution.py:605
  76.5 0.0 copy-done.3
  76.6 0.0 copy-done.5
  76.6 0.0 copy-done.7
  76.6 0.0 copy-done.9
  76.6 3.8 %shard_map.155 = (f32[64,1024]{1,0:T(8,128)S(1)}, bf16[2,384,128]{2,1,0:T(8,128)(2,1)S(1)}, f32[8,1024]{1,0:T(8,128)S(1)}, f32[512,128]{1,0:T(8,128)S(1)}, bf16[512,512]{1,0:T(8,128)(2,1)S(1)}) custom-call(s32[4]{0:T(128)S(1)} %pad_add_fusion.refs_0_.par_ref, f32[64,1024]{1,0:T(8,128)S(1)} %bitcast.27, s32[6,1024]{1,0:T(8,128)S(1)} %copy-done.7, ...), custom_call_target="tpu_custom_call" | custom-call | flops 134217728 | bytes 16777216 | tf_op jit(solution)/shard_map/pallas_call | solution.py:738
  80.4 0.0 collective-permute-done.4.ea_ref
  80.4 2.4 %collective-permute-done.5.eb_ref = f32[8,128]{1,0:T(8,128)S(1)} collective-permute-done((f32[8,128]{1,0:T(8,128)S(1)}, f32[8,128]{1,0:T(8,128)S(1)}, u32[]{:S(2)}, u32[]{:S(2)}) %collective-permute-start.5) | collective-permute-done | bytes 4128 | tf_op jit(solution)/shard_map/ppermute | solution.py:605
  82.7 1.9 %shard_map.156 = (f32[64,1024]{1,0:T(8,128)}, bf16[512,128]{1,0:T(8,128)(2,1)S(1)}) custom-call(s32[4]{0:T(128)S(1)} %pad_add_fusion.refs_0_.par_ref, f32[64,1024]{1,0:T(8,128)S(1)} %get-tuple-element.46.n2_ref, bf16[2,384,128]{2,1,0:T(8,128)(2,1)S(1)} %get-tuple-element.47.ends_ref, f32[8,1024]{1,0:T(8,128)S(1)} %get-tuple-element.48.sw_ref, ...), custom_call_target="tpu_custom_call" | custom-call | tf_op jit(solution)/shard_map/pallas_call | solution.py:751
  84.6 11.7 %all_to_all.16 = bf16[32,16,128]{2,1,0:T(8,128)(2,1)S(1)} all-to-all(bf16[32,16,128]{2,1,0:T(8,128)(2,1)S(1)} %bitcast.31), channel_id=1, replica_groups=mesh['tile'=32,'comp'=4] {'tile'}, dimensions={0} | all-to-all | bytes 262144 | tf_op jit(solution)/shard_map/all_to_all | solution.py:609
  96.3 0.9 shard_map.157
  (3 shorter events, 0.0 us)
Async XLA Ops:
  0.6 25.9 %copy-start.16 = (f32[2,16]{1,0:T(2,128)S(1)}, f32[2,16]{1,0:T(2,128)}, u32[]{:S(2)}) copy-start(f32[2,16]{1,0:T(2,128)} %param.14) | copy-start | bytes 388
  0.6 26.0 %copy-start.15 = (f32[4,12]{1,0:T(4,128)S(1)}, f32[4,12]{1,0:T(4,128)}, u32[]{:S(2)}) copy-start(f32[4,12]{1,0:T(4,128)} %param.23) | copy-start | bytes 580
  0.7 26.0 %copy-start.14 = (f32[12,4]{0,1:T(4,128)S(1)}, f32[12,4]{0,1:T(4,128)}, u32[]{:S(2)}) copy-start(f32[12,4]{0,1:T(4,128)} %param.16) | copy-start | bytes 580
  0.8 1.2 %copy-start = (f32[4,16,32,128]{3,2,1,0:T(8,128)S(1)}, f32[4,16,32,128]{3,2,1,0:T(8,128)}, u32[]{:S(2)}) copy-start(f32[4,16,32,128]{3,2,1,0:T(8,128)} %param.13) | copy-start | bytes 3145732
  2.0 0.9 copy-start.4
  2.9 0.8 copy-start.6
  3.7 0.8 copy-start.8
  4.5 0.7 copy-start.10
  5.2 16.9 %copy-start.1 = (f32[4,16,32,128]{3,2,1,0:T(8,128)S(1)}, f32[4,16,32,128]{3,2,1,0:T(8,128)}, u32[]{:S(2)}) copy-start(f32[4,16,32,128]{3,2,1,0:T(8,128)} %param.13) | copy-start | bytes 3145732
  6.0 14.6 %collective-permute-start.1 = (bf16[74,16,128]{2,1,0:T(8,128)(2,1)S(1)}, bf16[74,16,128]{2,1,0:T(8,128)(2,1)S(1)}, u32[]{:S(2)}, u32[]{:S(2)}) collective-permute-start(bf16[74,16,128]{2,1,0:T(8,128)(2,1)S(1)} %get-tuple-element.33.pb_ref), channel_id=1, source_target_pairs={{0,124},{4,8},{8,4},{12,16},{16,12},{20,24},{24,20},{28,32},{32,28... | collective-permute-start | bytes 909320 | tf_op jit(solution)/shard_map/ppermute | solution.py:605
  13.5 8.6 %collective-permute-start = (bf16[74,16,128]{2,1,0:T(8,128)(2,1)S(1)}, bf16[74,16,128]{2,1,0:T(8,128)(2,1)S(1)}, u32[]{:S(2)}, u32[]{:S(2)}) collective-permute-start(bf16[74,16,128]{2,1,0:T(8,128)(2,1)S(1)} %get-tuple-element.30.pa_ref), channel_id=1, source_target_pairs={{0,4},{4,0},{8,12},{12,8},{16,20},{20,16},{24,28},{28,24},{32,36},... | collective-permute-start | bytes 909320 | tf_op jit(solution)/shard_map/ppermute | solution.py:605
  13.5 0.7 copy-start.11
  22.1 11.5 %copy-start.13 = (f32[16,128]{1,0:T(8,128)S(1)}, f32[16,128]{1,0:T(8,128)}, u32[]{:S(2)}) copy-start(f32[16,128]{1,0:T(8,128)} %constant.31.clone.refs_6_) | copy-start | bytes 24580
  23.4 10.1 %collective-permute-start.2 = (bf16[672,128]{1,0:T(8,128)(2,1)S(1)}, bf16[672,128]{1,0:T(8,128)(2,1)S(1)}, u32[]{:S(2)}, u32[]{:S(2)}) collective-permute-start(bf16[672,128]{1,0:T(8,128)(2,1)S(1)} %get-tuple-element.37), channel_id=1, source_target_pairs={{0,1},{1,0},{2,3},{3,2},{4,5},{5,4},{6,7},{7,6},{8,9},{9,8},{10,11... | collective-permute-start | bytes 516104 | tf_op jit(solution)/shard_map/ppermute | solution.py:605
  23.5 10.0 %collective-permute-start.3 = (bf16[672,128]{1,0:T(8,128)(2,1)S(1)}, bf16[672,128]{1,0:T(8,128)(2,1)S(1)}, u32[]{:S(2)}, u32[]{:S(2)}) collective-permute-start(bf16[672,128]{1,0:T(8,128)(2,1)S(1)} %get-tuple-element.38), channel_id=1, source_target_pairs={{0,3},{1,2},{2,1},{3,0},{4,7},{5,6},{6,5},{7,4},{8,11},{9,10},{10,... | collective-permute-start | bytes 516104 | tf_op jit(solution)/shard_map/ppermute | solution.py:605
  27.0 28.6 %all-to-all-start = ((bf16[32,16,128]{2,1,0:T(8,128)(2,1)}), bf16[32,16,128]{2,1,0:T(8,128)(2,1)S(1)}, u32[]{:S(2)}, u32[]{:S(2)}) async-start(bf16[32,16,128]{2,1,0:T(8,128)(2,1)} %bitcast.7), calls=%async_computation | async-start | bytes 262144 | tf_op jit(solution)/shard_map/all_to_all | solution.py:609
  33.6 1.1 %copy-start.12 = (bf16[2,256,640]{2,1,0:T(8,128)(2,1)S(1)}, bf16[2,256,640]{2,1,0:T(8,128)(2,1)}, u32[]{:S(2)}) copy-start(bf16[2,256,640]{2,1,0:T(8,128)(2,1)} %constant.30.clone.refs_7_) | copy-start | bytes 1966084
  34.7 20.9 %copy-start.2 = (bf16[8,8,128,128]{3,2,1,0:T(8,128)(2,1)S(1)}, bf16[8,8,128,128]{3,2,1,0:T(8,128)(2,1)}, u32[]{:S(2)}) copy-start(bf16[8,8,128,128]{3,2,1,0:T(8,128)(2,1)} %param.18) | copy-start | bytes 6291460
  55.6 20.9 %copy-start.3 = (bf16[8,8,128,128]{3,2,1,0:T(8,128)(2,1)S(1)}, bf16[8,8,128,128]{3,2,1,0:T(8,128)(2,1)}, u32[]{:S(2)}) copy-start(bf16[8,8,128,128]{3,2,1,0:T(8,128)(2,1)} %weights_ref) | copy-start | bytes 6291460
  55.8 20.8 %copy-start.5 = (f32[4,16,1024]{2,1,0:T(8,128)S(1)}, f32[4,16,1024]{2,1,0:T(8,128)}, u32[]{:S(2)}) copy-start(f32[4,16,1024]{2,1,0:T(8,128)} %param.20) | copy-start | bytes 786436
  55.8 20.8 %copy-start.7 = (s32[6,1024]{1,0:T(8,128)S(1)}, s32[6,1024]{1,0:T(8,128)}, u32[]{:S(2)}) copy-start(s32[6,1024]{1,0:T(8,128)} %off_ref.1) | copy-start | bytes 73732
  55.8 20.8 %copy-start.9 = (f32[6,1024]{1,0:T(8,128)S(1)}, f32[6,1024]{1,0:T(8,128)}, u32[]{:S(2)}) copy-start(f32[6,1024]{1,0:T(8,128)} %w_ref.1) | copy-start | bytes 73732
  74.1 6.3 %collective-permute-start.4 = (f32[8,128]{1,0:T(8,128)S(1)}, f32[8,128]{1,0:T(8,128)S(1)}, u32[]{:S(2)}, u32[]{:S(2)}) collective-permute-start(f32[8,128]{1,0:T(8,128)S(1)} %get-tuple-element.49), channel_id=1, source_target_pairs={{0,1},{1,0},{2,3},{3,2},{4,5},{5,4},{6,7},{7,6},{8,9},{9,8},{10,11... | collective-permute-start | bytes 12296 | tf_op jit(solution)/shard_map/ppermute | solution.py:605
  74.2 8.5 %collective-permute-start.5 = (f32[8,128]{1,0:T(8,128)S(1)}, f32[8,128]{1,0:T(8,128)S(1)}, u32[]{:S(2)}, u32[]{:S(2)}) collective-permute-start(f32[8,128]{1,0:T(8,128)S(1)} %get-tuple-element.50), channel_id=1, source_target_pairs={{0,127},{1,2},{2,1},{3,4},{4,3},{5,6},{6,5},{7,8},{8,7},{9,10},{10... | collective-permute-start | bytes 12296 | tf_op jit(solution)/shard_map/ppermute | solution.py:605
